TPU v7x, 32 devices: a whole 2x2x4 slice. The times are simulated.
32 devices in a mesh: dp: 16 (over z, y, core), tensor: 2 (over x).
Axes of the slice: x: 2, y: 2, z: 4, core: 2. Of those that a mesh axis runs over, the one named last changes fastest.
Arguments:
- token_codes: int32 [96, 196], P('dp'), may hold values from 0 to 8191
- mask_slots: int32 [96, 78], P('dp'), may hold values from 0 to 195, as said below
- mask_counts: int32 [96], P('dp'), may hold values from 1 to 78, as said below
- embedding: float32 [8192, 768], P('tensor', 'dp'), may hold values from -6 to 6
- emb_first: float32 [8192, 768], P('tensor', 'dp'), may hold values from -0.001953125 to 0.001953125
- emb_second: float32 [8192, 768], P('tensor', 'dp'), may hold values from 1.6302126e-08 to 6.52085e-08
- readout: float32 [8192, 768], P('tensor', 'dp')
- read_first: float32 [8192, 768], P('tensor', 'dp'), may hold values from -0.001953125 to 0.001953125
- read_second: float32 [8192, 768], P('tensor', 'dp'), may hold values from 1.6302126e-08 to 6.52085e-08
- in_proj: float32 [2, 768, 3, 768], P(None, 'dp', None, 'tensor'), may hold values from -0.21875 to 0.21875
- in_first: float32 [2, 768, 3, 768], P(None, 'dp', None, 'tensor'), may hold values from -0.005859375 to 0.005859375
- in_second: float32 [2, 768, 3, 768], P(None, 'dp', None, 'tensor'), may hold values from 1.7388933e-07 to 6.9555733e-07
- out_proj: float32 [2, 768, 768], P(None, 'dp', 'tensor'), may hold values from -0.875 to 0.875
- out_first: float32 [2, 768, 768], P(None, 'dp', 'tensor'), may hold values from -0.005859375 to 0.005859375
- out_second: float32 [2, 768, 768], P(None, 'dp', 'tensor'), may hold values from 1.7388933e-07 to 6.9555733e-07
- up_proj: float32 [2, 768, 3072], P(None, 'dp', 'tensor'), may hold values from -0.21875 to 0.21875
- up_first: float32 [2, 768, 3072], P(None, 'dp', 'tensor'), may hold values from -0.005859375 to 0.005859375
- up_second: float32 [2, 768, 3072], P(None, 'dp', 'tensor'), may hold values from 1.7388933e-07 to 6.9555733e-07
- down_proj: float32 [2, 768, 3072], P(None, 'dp', 'tensor'), may hold values from -0.109375 to 0.109375
- down_first: float32 [2, 768, 3072], P(None, 'dp', 'tensor'), may hold values from -0.005859375 to 0.005859375
- down_second: float32 [2, 768, 3072], P(None, 'dp', 'tensor'), may hold values from 1.7388933e-07 to 6.9555733e-07
- vectors: float32 [32, 768], replicated
- vec_first: float32 [32, 768], replicated, may hold values from -0.01953125 to 0.01953125
- vec_second: float32 [32, 768], replicated, may hold values from 1.565004e-06 to 6.260016e-06
- position: float32 [2, 12, 732], replicated, may hold values from -3 to 3
- pos_first: float32 [2, 12, 732], replicated, may hold values from -0.01953125 to 0.01953125
- pos_second: float32 [2, 12, 732], replicated, may hold values from 1.565004e-06 to 6.260016e-06
Outputs:
- loss_sum: float32 [], replicated
- mask_total: float32 [], replicated
- emb_master: float32 [8192, 768], P('tensor', 'dp')
- emb_mean: float32 [8192, 768], P('tensor', 'dp')
- emb_square: float32 [8192, 768], P('tensor', 'dp')
- read_master: float32 [8192, 768], P('tensor', 'dp')
- read_mean: float32 [8192, 768], P('tensor', 'dp')
- read_square: float32 [8192, 768], P('tensor', 'dp')
- in_master: float32 [2, 768, 3, 768], P(None, 'dp', None, 'tensor')
- in_mean: float32 [2, 768, 3, 768], P(None, 'dp', None, 'tensor')
- in_square: float32 [2, 768, 3, 768], P(None, 'dp', None, 'tensor')
- out_master: float32 [2, 768, 768], P(None, 'dp', 'tensor')
- out_mean: float32 [2, 768, 768], P(None, 'dp', 'tensor')
- out_square: float32 [2, 768, 768], P(None, 'dp', 'tensor')
- up_master: float32 [2, 768, 3072], P(None, 'dp', 'tensor')
- up_mean: float32 [2, 768, 3072], P(None, 'dp', 'tensor')
- up_square: float32 [2, 768, 3072], P(None, 'dp', 'tensor')
- down_master: float32 [2, 768, 3072], P(None, 'dp', 'tensor')
- down_mean: float32 [2, 768, 3072], P(None, 'dp', 'tensor')
- down_square: float32 [2, 768, 3072], P(None, 'dp', 'tensor')
- vec_master: float32 [32, 768], replicated
- vec_mean: float32 [32, 768], replicated
- vec_square: float32 [32, 768], replicated
- pos_master: float32 [2, 12, 732], replicated
- pos_mean: float32 [2, 12, 732], replicated
- pos_square: float32 [2, 12, 732], replicated
- in_copy: bfloat16 [2, 768, 3, 768], P(None, 'dp', None, 'tensor')
- out_copy: bfloat16 [2, 768, 768], P(None, 'dp', 'tensor')
- up_copy: bfloat16 [2, 768, 3072], P(None, 'dp', 'tensor')
- down_copy: bfloat16 [2, 768, 3072], P(None, 'dp', 'tensor')
Inputs may be any that keep to these rules, and one draw needn't show every extreme that they name: `mask_slots`: each row names 78 different patch indices; the first mask_counts entries of a row are that sequence's masked patches, the others are unused. `mask_counts`: some sequence uses all 78 slots.
All inputs are finite; a program needn't handle non-finite values.
Results may differ from a plain program's by a relative error of at most 0.007.
The roundings to bfloat16 on the way count: a program that leaves them out, or rounds other values in their place, can miss the bound.
Values may be sent and summed in bfloat16 or wider, within the bound.
A program may use at most 256 MiB of HBM per device.

v0:
```python
import math

import jax
import jax.numpy as jnp
import numpy as np
from jax import lax
from jax.sharding import PartitionSpec as P

HEADS = 12
HD = 64
STEP = 5
L = 197


beta_one = 0.5
beta_two = 0.5
adam_eps = 1e-08
rate_matrix = 0.05
rate_vector = 0.3
rate_table = 0.5
decay_matrix = 0.05
norm_eps = 1e-06


def merged(value, axis, join):
    pieces = jax.tree.map(lambda part: lax.all_gather(part, axis), value)
    head = jax.tree.map(lambda part: part[0], pieces)
    tail = jax.tree.map(lambda part: part[1:], pieces)
    so_far, _ = lax.scan(lambda so_far, share: (join(so_far, share), None), head, tail)
    return so_far


def layer_norm(values, gain_row, shift_row):
    center = values - jnp.mean(values, axis=-1, keepdims=True)
    spread_sq = jnp.mean(center * center, axis=-1, keepdims=True)
    return center * lax.rsqrt(spread_sq + norm_eps) * gain_row + shift_row


def gelu_exact(values):
    return jax.nn.gelu(values, approximate=False)


def relative_table(grid_side):
    coords = np.stack(
        np.meshgrid(np.arange(grid_side), np.arange(grid_side), indexing="ij")
    ).reshape(2, -1)
    offsets = coords[:, :, None] - coords[:, None, :] + grid_side - 1
    inner_idx = offsets[0] * (2 * grid_side - 1) + offsets[1]
    cell_count = (2 * grid_side - 1) ** 2
    result = np.zeros((grid_side * grid_side + 1, grid_side * grid_side + 1), np.int32)
    result[1:, 1:] = inner_idx
    result[0, 1:] = cell_count
    result[1:, 0] = cell_count + 1
    result[0, 0] = cell_count + 2
    return result


def spread_rows(value):
    return lax.all_gather(value, "tensor", axis=0, tiled=True)


def collect_rows(value):
    return lax.psum_scatter(
        value.astype(jnp.bfloat16), "tensor", scatter_dimension=0, tiled=True
    ).astype(jnp.float32)


def fetch_layer(in_proj, out_proj, up_proj, down_proj, layer_at):
    return (
        lax.all_gather(in_proj[layer_at].astype(jnp.bfloat16), "dp", axis=0, tiled=True),
        lax.all_gather(out_proj[layer_at].astype(jnp.bfloat16), "dp", axis=0, tiled=True),
        lax.all_gather(up_proj[layer_at].astype(jnp.bfloat16), "dp", axis=0, tiled=True),
        lax.all_gather(down_proj[layer_at].astype(jnp.bfloat16), "dp", axis=0, tiled=True),
    )


def merge_stats(former, latter):
    joined_peak = jnp.maximum(former[0], latter[0])
    joined_sum = former[1] * jnp.exp(former[0] - joined_peak) + latter[1] * jnp.exp(
        latter[0] - joined_peak
    )
    return (joined_peak, joined_sum, former[2] + latter[2])


def local_bias(position, layer_at, lookup, tensor_at, head_count):
    table_rows = lax.dynamic_slice_in_dim(position[layer_at], tensor_at * head_count, head_count, 0)
    return jnp.take(table_rows, lookup, axis=1)


def attention_scores(triple, rel_bias):
    scores = jnp.einsum(
        "bqhe,bkhe->bhqk", triple[:, :, 0], triple[:, :, 1], preferred_element_type=jnp.float32
    )
    return scores * HD ** (-0.5) + rel_bias


def forward_layer(stream, matrices, vectors, position, layer_at, lookup, tensor_at):
    w_in, w_out, w_up, w_down = matrices
    first_row = layer_at * 14
    model_width = w_in.shape[0]
    head_cols = w_in.shape[2]
    head_count = head_cols // HD
    ff_cols = w_up.shape[1]
    normed_in = spread_rows(
        layer_norm(stream, vectors[first_row], vectors[first_row + 1]).astype(jnp.bfloat16)
    )
    row_count = normed_in.shape[0]
    seq_count = row_count // L
    mixed_in = jnp.dot(
        normed_in, w_in.reshape(model_width, 3 * head_cols), preferred_element_type=jnp.float32
    ).reshape(row_count, 3, head_cols)
    q_bias = lax.dynamic_slice_in_dim(vectors[first_row + 2], tensor_at * head_cols, head_cols)
    v_bias = lax.dynamic_slice_in_dim(vectors[first_row + 3], tensor_at * head_cols, head_cols)
    offset = jnp.stack([q_bias, jnp.zeros_like(q_bias), v_bias])
    triple = (mixed_in + offset).astype(jnp.bfloat16).reshape(seq_count, L, 3, head_count, HD)
    scores = attention_scores(triple, local_bias(position, layer_at, lookup, tensor_at, head_count))
    peak_here = jnp.max(scores, axis=-1, keepdims=True)
    log_sum = peak_here + jnp.log(jnp.sum(jnp.exp(scores - peak_here), axis=-1, keepdims=True))
    weights = jnp.exp(scores - log_sum).astype(jnp.bfloat16)
    attended = jnp.einsum(
        "bhqk,bkhe->bqhe", weights, triple[:, :, 2], preferred_element_type=jnp.float32
    )
    attended = attended.astype(jnp.bfloat16).reshape(row_count, head_cols)
    branch_one = collect_rows(
        jnp.einsum("rk,dk->rd", attended, w_out, preferred_element_type=jnp.float32)
    )
    middle = stream + vectors[first_row + 5] * (branch_one + vectors[first_row + 4])
    normed_mid = spread_rows(
        layer_norm(middle, vectors[first_row + 6], vectors[first_row + 7]).astype(jnp.bfloat16)
    )
    up_bias = lax.dynamic_slice_in_dim(
        vectors[first_row + 10 : first_row + 14].reshape(-1), tensor_at * ff_cols, ff_cols
    )
    hidden_pre = jnp.dot(normed_mid, w_up, preferred_element_type=jnp.float32) + up_bias
    hidden = gelu_exact(hidden_pre).astype(jnp.bfloat16)
    branch_two = collect_rows(
        jnp.einsum("rf,df->rd", hidden, w_down, preferred_element_type=jnp.float32)
    )
    result = middle + vectors[first_row + 9] * (branch_two + vectors[first_row + 8])
    saved = (
        stream,
        normed_in,
        triple,
        log_sum,
        attended,
        branch_one,
        middle,
        normed_mid,
        hidden_pre,
        hidden,
        branch_two,
    )
    return (result, saved)


def backward_layer(grad_out, saved, matrices, vectors, position, layer_at, lookup, tensor_at):
    w_in, w_out, w_up, w_down = matrices
    (
        stream,
        normed_in,
        triple,
        log_sum,
        attended,
        branch_one,
        middle,
        normed_mid,
        hidden_pre,
        hidden,
        branch_two,
    ) = saved
    first_row = layer_at * 14
    model_width = w_in.shape[0]
    head_cols = w_in.shape[2]
    head_count = head_cols // HD
    ff_cols = w_up.shape[1]
    row_count = normed_in.shape[0]
    seq_count = row_count // L
    grad_gamma_two = jnp.sum(grad_out * (branch_two + vectors[first_row + 8]), axis=0)
    grad_down_bias = jnp.sum(grad_out * vectors[first_row + 9], axis=0)
    grad_branch = spread_rows((grad_out * vectors[first_row + 9]).astype(jnp.bfloat16))
    grad_down = jnp.einsum("rd,rf->df", grad_branch, hidden, preferred_element_type=jnp.float32)
    grad_hidden = jnp.dot(grad_branch, w_down, preferred_element_type=jnp.float32)
    _unused, gelu_pull = jax.vjp(gelu_exact, hidden_pre)
    grad_pre = gelu_pull(grad_hidden)[0].astype(jnp.bfloat16)
    grad_up_bias = jnp.sum(grad_pre.astype(jnp.float32), axis=0)
    grad_up = jnp.einsum("rd,rf->df", normed_mid, grad_pre, preferred_element_type=jnp.float32)
    grad_normed = collect_rows(
        jnp.einsum("rf,df->rd", grad_pre, w_up, preferred_element_type=jnp.float32)
    )
    _unused, norm_pull = jax.vjp(layer_norm, middle, vectors[first_row + 6], vectors[first_row + 7])
    grad_mid, grad_gain_two, grad_shift_two = norm_pull(grad_normed)
    grad_mid = grad_mid + grad_out
    grad_gamma_one = jnp.sum(grad_mid * (branch_one + vectors[first_row + 4]), axis=0)
    grad_out_bias = jnp.sum(grad_mid * vectors[first_row + 5], axis=0)
    grad_attn = spread_rows((grad_mid * vectors[first_row + 5]).astype(jnp.bfloat16))
    grad_outw = jnp.einsum("rd,rk->dk", grad_attn, attended, preferred_element_type=jnp.float32)
    grad_attended = jnp.dot(grad_attn, w_out, preferred_element_type=jnp.float32).astype(
        jnp.bfloat16
    )
    grad_attended = grad_attended.reshape(seq_count, L, head_count, HD)
    scores = attention_scores(triple, local_bias(position, layer_at, lookup, tensor_at, head_count))
    prob_full = jnp.exp(scores - log_sum)
    grad_probs = jnp.einsum(
        "bqhe,bkhe->bhqk", grad_attended, triple[:, :, 2], preferred_element_type=jnp.float32
    )
    grad_scores = prob_full * (grad_probs - jnp.sum(prob_full * grad_probs, axis=-1, keepdims=True))
    grad_scores = grad_scores.astype(jnp.bfloat16)
    score_scale = HD ** (-0.5)
    grad_query = (
        jnp.einsum(
            "bhqk,bkhe->bqhe", grad_scores, triple[:, :, 1], preferred_element_type=jnp.float32
        )
        * score_scale
    )
    grad_key = (
        jnp.einsum(
            "bhqk,bqhe->bkhe", grad_scores, triple[:, :, 0], preferred_element_type=jnp.float32
        )
        * score_scale
    )
    grad_value = jnp.einsum(
        "bhqk,bqhe->bkhe",
        prob_full.astype(jnp.bfloat16),
        grad_attended,
        preferred_element_type=jnp.float32,
    )
    grad_triple = (
        jnp.stack([grad_query, grad_key, grad_value], axis=2)
        .astype(jnp.bfloat16)
        .reshape(row_count, 3 * head_cols)
    )
    per_head = jnp.sum(grad_scores.astype(jnp.float32), axis=0).reshape(head_count, L * L)
    grad_rel = jax.ops.segment_sum(per_head.T, lookup.reshape(-1), num_segments=position.shape[2]).T
    grad_bias_sums = jnp.sum(grad_triple.astype(jnp.float32), axis=0).reshape(3, head_cols)
    grad_inw = jnp.einsum(
        "rd,rk->dk", normed_in, grad_triple, preferred_element_type=jnp.float32
    ).reshape(model_width, 3, head_cols)
    grad_normed = collect_rows(
        jnp.einsum(
            "rk,dk->rd",
            grad_triple,
            w_in.reshape(model_width, 3 * head_cols),
            preferred_element_type=jnp.float32,
        )
    )
    _unused, norm_pull = jax.vjp(layer_norm, stream, vectors[first_row], vectors[first_row + 1])
    grad_stream, grad_gain_one, grad_shift_one = norm_pull(grad_normed)
    grad_stream = grad_stream + grad_mid
    zero_row = jnp.zeros((model_width,), jnp.float32)
    q_grad = lax.dynamic_update_slice_in_dim(zero_row, grad_bias_sums[0], tensor_at * head_cols, 0)
    v_grad = lax.dynamic_update_slice_in_dim(zero_row, grad_bias_sums[2], tensor_at * head_cols, 0)
    up_full = lax.dynamic_update_slice_in_dim(
        jnp.zeros((4 * model_width,), jnp.float32), grad_up_bias, tensor_at * ff_cols, 0
    )
    vec_grads = jnp.concatenate(
        [
            jnp.stack(
                [
                    grad_gain_one,
                    grad_shift_one,
                    q_grad,
                    v_grad,
                    grad_out_bias,
                    grad_gamma_one,
                    grad_gain_two,
                    grad_shift_two,
                    grad_down_bias,
                    grad_gamma_two,
                ]
            ),
            up_full.reshape(4, model_width),
        ],
        axis=0,
    )
    rel_full = lax.dynamic_update_slice_in_dim(
        jnp.zeros((HEADS, position.shape[2]), jnp.float32), grad_rel, tensor_at * head_count, 0
    )
    return (grad_stream, (grad_inw, grad_outw, grad_up, grad_down), vec_grads, rel_full)


def adamw_update(master, gradient, first_mom, second_mom, step_rate, decay_rate):
    first_mom = beta_one * first_mom + (1.0 - beta_one) * gradient
    second_mom = beta_two * second_mom + (1.0 - beta_two) * gradient * gradient
    step_dir = (
        first_mom
        / (1.0 - beta_one**STEP)
        / (jnp.sqrt(second_mom / (1.0 - beta_two**STEP)) + adam_eps)
    )
    return (master - step_rate * (step_dir + decay_rate * master), first_mom, second_mom)


def local(
    token_codes,
    mask_slots,
    mask_counts,
    embedding,
    emb_first,
    emb_second,
    readout,
    read_first,
    read_second,
    in_proj,
    in_first,
    in_second,
    out_proj,
    out_first,
    out_second,
    up_proj,
    up_first,
    up_second,
    down_proj,
    down_first,
    down_second,
    vectors,
    vec_first,
    vec_second,
    position,
    pos_first,
    pos_second,
):
    tensor_at = lax.axis_index("tensor")
    tensor_size = lax.axis_size("tensor")
    seq_count = token_codes.shape[0]
    patch_count = token_codes.shape[1]
    seq_len = patch_count + 1
    slot_most = mask_slots.shape[1]
    my_seqs = seq_count // tensor_size
    lookup = jnp.asarray(relative_table(math.isqrt(patch_count))).astype(jnp.int32)
    live_slot = jnp.arange(slot_most)[None, :] < mask_counts[:, None]
    masked = jnp.any(
        (mask_slots[:, :, None] == jnp.arange(patch_count)[None, None, :]) & live_slot[:, :, None],
        axis=1,
    )
    count_here = jnp.sum(mask_counts.astype(jnp.float32))
    emb_table, read_table = (
        lax.all_gather(embedding.astype(jnp.bfloat16), "dp", axis=1, tiled=True),
        lax.all_gather(readout.astype(jnp.bfloat16), "dp", axis=1, tiled=True),
    )
    vocab_here = emb_table.shape[0]
    model_width = emb_table.shape[1]
    vocab_start = tensor_at * vocab_here
    shifted = token_codes - vocab_start
    usable = (shifted >= 0) & (shifted < vocab_here) & jnp.logical_not(masked)
    looked = jnp.take(emb_table, jnp.clip(shifted, 0, vocab_here - 1), axis=0)
    looked = jnp.where(usable[:, :, None], looked, jnp.zeros_like(looked))
    padded = jnp.concatenate(
        [jnp.zeros((seq_count, 1, model_width), jnp.bfloat16), looked], axis=1
    ).reshape(seq_count * seq_len, model_width)
    summed_rows = lax.psum_scatter(padded, "tensor", scatter_dimension=0, tiled=True).astype(
        jnp.float32
    )
    my_masked = lax.dynamic_slice_in_dim(masked, tensor_at * my_seqs, my_seqs, 0).astype(
        jnp.float32
    )
    lead_flag = jnp.concatenate(
        [jnp.ones((my_seqs, 1), jnp.float32), jnp.zeros((my_seqs, patch_count), jnp.float32)],
        axis=1,
    ).reshape(-1, 1)
    mask_flag = jnp.concatenate([jnp.zeros((my_seqs, 1), jnp.float32), my_masked], axis=1).reshape(
        -1, 1
    )
    tail_row = vectors.shape[0] - 4
    stream = summed_rows + lead_flag * vectors[tail_row] + mask_flag * vectors[tail_row + 1]
    layer_count = in_proj.shape[0]
    saved_all = []
    fetched_all = []
    for layer_at in range(layer_count):
        matrices = fetch_layer(in_proj, out_proj, up_proj, down_proj, layer_at)
        fetched_all.append(matrices)
        stream, saved = forward_layer(
            stream, matrices, vectors, position, layer_at, lookup, tensor_at
        )
        saved_all.append(saved)
    my_slots = lax.dynamic_slice_in_dim(mask_slots, tensor_at * my_seqs, my_seqs, 0)
    pick_rows = (jnp.arange(my_seqs)[:, None] * seq_len + 1 + my_slots).reshape(-1)
    final_in = stream[pick_rows]
    final_rows = spread_rows(
        layer_norm(final_in, vectors[tail_row + 2], vectors[tail_row + 3]).astype(jnp.bfloat16)
    )
    logits = jnp.einsum("md,vd->mv", final_rows, read_table, preferred_element_type=jnp.float32)
    target = jnp.take_along_axis(token_codes, mask_slots, axis=1).reshape(-1) - vocab_start
    is_target = jnp.arange(vocab_here)[None, :] == target[:, None]
    peak_here = jnp.max(logits, axis=1)
    exp_sum = jnp.sum(jnp.exp(logits - peak_here[:, None]), axis=1)
    chosen = jnp.sum(jnp.where(is_target, logits, 0.0), axis=1)
    peak_all, exp_all, chosen_all = merged((peak_here, exp_sum, chosen), "tensor", merge_stats)
    log_total = peak_all + jnp.log(exp_all)
    weight_row = live_slot.reshape(-1).astype(jnp.float32)
    loss_here = jnp.sum((log_total - chosen_all) * weight_row)
    loss_sum, mask_total = lax.psum((loss_here, count_here), "dp")
    prob_rows = jnp.exp(logits - log_total[:, None])
    grad_logits = (
        (prob_rows - is_target.astype(jnp.float32)) * (weight_row / mask_total)[:, None]
    ).astype(jnp.bfloat16)
    grad_final = collect_rows(jnp.dot(grad_logits, read_table, preferred_element_type=jnp.float32))
    grad_read = jnp.einsum("mv,md->vd", grad_logits, final_rows, preferred_element_type=jnp.float32)
    grad_read = lax.psum_scatter(grad_read, "dp", scatter_dimension=1, tiled=True)
    _unused, norm_pull = jax.vjp(layer_norm, final_in, vectors[tail_row + 2], vectors[tail_row + 3])
    grad_in, grad_gain_final, grad_shift_final = norm_pull(grad_final)
    grad_stream = jnp.zeros_like(stream).at[pick_rows].add(grad_in)
    matrix_grads = [None] * layer_count
    vec_by_layer = [None] * layer_count
    rel_by_layer = [None] * layer_count
    for layer_at in reversed(range(layer_count)):
        matrices = fetch_layer(in_proj, out_proj, up_proj, down_proj, layer_at)
        grad_stream, mats_grad, vec_grad, rel_grad = backward_layer(
            grad_stream,
            saved_all[layer_at],
            matrices,
            vectors,
            position,
            layer_at,
            lookup,
            tensor_at,
        )
        matrix_grads[layer_at] = (
            lax.psum_scatter(mats_grad[0], "dp", scatter_dimension=0, tiled=True),
            lax.psum_scatter(mats_grad[1], "dp", scatter_dimension=0, tiled=True),
            lax.psum_scatter(mats_grad[2], "dp", scatter_dimension=0, tiled=True),
            lax.psum_scatter(mats_grad[3], "dp", scatter_dimension=0, tiled=True),
        )
        vec_by_layer[layer_at] = vec_grad
        rel_by_layer[layer_at] = rel_grad
    grad_embed_rows = grad_stream.astype(jnp.bfloat16)
    grad_lead = jnp.sum(grad_embed_rows.astype(jnp.float32) * lead_flag, axis=0)
    grad_mask_token = jnp.sum(grad_embed_rows.astype(jnp.float32) * mask_flag, axis=0)
    grad_all_rows = spread_rows(grad_embed_rows).reshape(seq_count, seq_len, model_width)[:, 1:]
    segment_ids = jnp.where(usable, shifted, vocab_here).reshape(-1)
    grad_embed = jax.ops.segment_sum(
        grad_all_rows.reshape(-1, model_width).astype(jnp.float32),
        segment_ids,
        num_segments=vocab_here + 1,
    )[:vocab_here]
    grad_embed = lax.psum_scatter(grad_embed, "dp", scatter_dimension=1, tiled=True)
    vec_local = jnp.concatenate(
        vec_by_layer + [jnp.stack([grad_lead, grad_mask_token, grad_gain_final, grad_shift_final])],
        axis=0,
    )
    rel_local = jnp.stack(rel_by_layer)
    vec_grad_all, rel_grad_all = lax.psum((vec_local, rel_local), ("dp", "tensor"))
    in_grad = jnp.stack([entry_list[0] for entry_list in matrix_grads])
    out_grad = jnp.stack([entry_list[1] for entry_list in matrix_grads])
    up_grad = jnp.stack([entry_list[2] for entry_list in matrix_grads])
    down_grad = jnp.stack([entry_list[3] for entry_list in matrix_grads])
    emb_new = adamw_update(embedding, grad_embed, emb_first, emb_second, rate_table, decay_matrix)
    read_new = adamw_update(readout, grad_read, read_first, read_second, rate_matrix, decay_matrix)
    in_new = adamw_update(in_proj, in_grad, in_first, in_second, rate_matrix, decay_matrix)
    out_new = adamw_update(out_proj, out_grad, out_first, out_second, rate_matrix, decay_matrix)
    up_new = adamw_update(up_proj, up_grad, up_first, up_second, rate_matrix, decay_matrix)
    down_new = adamw_update(
        down_proj, down_grad, down_first, down_second, rate_matrix, decay_matrix
    )
    vec_new = adamw_update(vectors, vec_grad_all, vec_first, vec_second, rate_vector, 0.0)
    pos_new = adamw_update(position, rel_grad_all, pos_first, pos_second, rate_vector, 0.0)
    return (
        loss_sum,
        mask_total,
        emb_new[0],
        emb_new[1],
        emb_new[2],
        read_new[0],
        read_new[1],
        read_new[2],
        in_new[0],
        in_new[1],
        in_new[2],
        out_new[0],
        out_new[1],
        out_new[2],
        up_new[0],
        up_new[1],
        up_new[2],
        down_new[0],
        down_new[1],
        down_new[2],
        vec_new[0],
        vec_new[1],
        vec_new[2],
        pos_new[0],
        pos_new[1],
        pos_new[2],
        in_new[0].astype(jnp.bfloat16),
        out_new[0].astype(jnp.bfloat16),
        up_new[0].astype(jnp.bfloat16),
        down_new[0].astype(jnp.bfloat16),
    )


def solution(mesh):
    return jax.shard_map(
        local,
        mesh=mesh,
        in_specs=(
            P("dp", None),
            P("dp", None),
            P("dp"),
            P("tensor", "dp"),
            P("tensor", "dp"),
            P("tensor", "dp"),
            P("tensor", "dp"),
            P("tensor", "dp"),
            P("tensor", "dp"),
            P(None, "dp", None, "tensor"),
            P(None, "dp", None, "tensor"),
            P(None, "dp", None, "tensor"),
            P(None, "dp", "tensor"),
            P(None, "dp", "tensor"),
            P(None, "dp", "tensor"),
            P(None, "dp", "tensor"),
            P(None, "dp", "tensor"),
            P(None, "dp", "tensor"),
            P(None, "dp", "tensor"),
            P(None, "dp", "tensor"),
            P(None, "dp", "tensor"),
            P(),
            P(),
            P(),
            P(),
            P(),
            P(),
        ),
        out_specs=(
            P(),
            P(),
            P("tensor", "dp"),
            P("tensor", "dp"),
            P("tensor", "dp"),
            P("tensor", "dp"),
            P("tensor", "dp"),
            P("tensor", "dp"),
            P(None, "dp", None, "tensor"),
            P(None, "dp", None, "tensor"),
            P(None, "dp", None, "tensor"),
            P(None, "dp", "tensor"),
            P(None, "dp", "tensor"),
            P(None, "dp", "tensor"),
            P(None, "dp", "tensor"),
            P(None, "dp", "tensor"),
            P(None, "dp", "tensor"),
            P(None, "dp", "tensor"),
            P(None, "dp", "tensor"),
            P(None, "dp", "tensor"),
            P(),
            P(),
            P(),
            P(),
            P(),
            P(),
            P(None, "dp", None, "tensor"),
            P(None, "dp", "tensor"),
            P(None, "dp", "tensor"),
            P(None, "dp", "tensor"),
        ),
        check_vma=False,
    )
```

profile of v0, /device:TPU:9, one launch (start us, length us, event | category | flops | bytes accessed | tf_op | source)
XLA Modules:
  0.0 2961.5 jit_solution(6284256318169620097)
XLA Ops:
  13.5 61.0 %all-gather.39.cloned.1.call-done = bf16[4096,768]{0,1:T(8,128)(2,1)} async-done(((bf16[4096,48]{0,1:T(8,128)(2,1)}), bf16[4096,768]{0,1:T(8,128)(2,1)}) %all-gather.39.cloned.1.call-update) | async-done | bytes 6291472 | tf_op jit(solution)/shard_map/all_gather | solution.py:336
  98.1 25.5 fusion
  135.0 128.5 %gather_fusion.3 = f32[38809,6]{1,0:T(8,128)} fusion(f32[6,732]{0,1:T(8,128)S(1)} %bitcast.268, s32[38912]{0:T(1024)S(1)} %pad_clamp_fusion), kind=kCustom, calls=%fused_computation.clone | custom fusion | bytes 2018068 | tf_op jit(solution)/shard_map/jit(_take)/gather | solution.py:87
  357.5 25.9 fusion.1
  399.1 29.4 all-gather.57.cloned.1.call-done
  431.6 41.7 %all-gather.45.cloned.1.call-done = bf16[1,768,1536]{2,1,0:T(8,128)(2,1)} async-done(((bf16[1,48,1536]{2,1,0:T(8,128)(2,1)}), bf16[1,768,1536]{2,1,0:T(8,128)(2,1)}) %all-gather.45.cloned.1.call-update) | async-done | bytes 2359312 | tf_op jit(solution)/shard_map/all_gather | solution.py:72
  524.1 25.5 fusion.2
  560.9 128.5 %gather_fusion.4 = f32[38809,6]{1,0:T(8,128)} fusion(f32[6,732]{0,1:T(8,128)S(1)} %bitcast.269, s32[38912]{0:T(1024)S(1)} %pad_clamp_fusion), kind=kCustom, calls=%fused_computation.1.clone | custom fusion | bytes 2018068 | tf_op jit(solution)/shard_map/jit(_take)/gather | solution.py:87
  779.7 26.4 fusion.3
  851.1 43.0 %all-gather.51.cloned.1.call-done = bf16[1,768,1536]{2,1,0:T(8,128)(2,1)} async-done(((bf16[1,48,1536]{2,1,0:T(8,128)(2,1)}), bf16[1,768,1536]{2,1,0:T(8,128)(2,1)}) %all-gather.51.cloned.1.call-update) | async-done | bytes 2359312 | tf_op jit(solution)/shard_map/all_gather | solution.py:72
  945.0 25.5 fusion.4
  1027.7 25.2 all-reduce.26
  1105.4 37.7 %all-gather.63.cloned.1.call-done = bf16[2,591,768]{2,1,0:T(8,128)(2,1)} async-done(((bf16[1,591,768]{2,1,0:T(8,128)(2,1)}), bf16[2,591,768]{2,1,0:T(8,128)(2,1)}) %all-gather.63.cloned.1.call-update) | async-done | bytes 1815568 | tf_op jit(solution)/shard_map/all_gather | solution.py:59
  1162.3 24.0 fusion.6
  1201.0 33.9 %all-gather.65.cloned.1.call-done = bf16[2,591,768]{2,1,0:T(8,128)(2,1)} async-done(((bf16[1,591,768]{2,1,0:T(8,128)(2,1)}), bf16[2,591,768]{2,1,0:T(8,128)(2,1)}) %all-gather.65.cloned.1.call-update) | async-done | bytes 1815568 | tf_op jit(solution)/shard_map/all_gather | solution.py:59
  1280.0 24.1 fusion.7
  1319.0 33.8 %all-gather.67.cloned.1.call-done = bf16[2,591,768]{2,1,0:T(8,128)(2,1)} async-done(((bf16[1,591,768]{2,1,0:T(8,128)(2,1)}), bf16[2,591,768]{2,1,0:T(8,128)(2,1)}) %all-gather.67.cloned.1.call-update) | async-done | bytes 1815568 | tf_op jit(solution)/shard_map/all_gather | solution.py:59
  1370.4 24.1 fusion.8
  1409.3 33.8 %all-gather.69.cloned.1.call-done = bf16[2,591,768]{2,1,0:T(8,128)(2,1)} async-done(((bf16[1,591,768]{2,1,0:T(8,128)(2,1)}), bf16[2,591,768]{2,1,0:T(8,128)(2,1)}) %all-gather.69.cloned.1.call-update) | async-done | bytes 1815568 | tf_op jit(solution)/shard_map/all_gather | solution.py:59
  1488.7 24.1 fusion.9
  1536.1 207.7 %scatter_custom_fusion.3 = f32[732,6]{1,0:T(8,128)S(1)} fusion(s32[38809]{0:T(1024)} %constant.294, f32[38809,6]{1,0:T(8,128)} %copy.211, f32[]{:T(128)} %constant.86.clone.1), kind=kCustom, calls=%fused_computation.252 | custom fusion | flops 232854 | bytes 18080 | tf_op jit(solution)/shard_map/scatter-add | solution.py:233
  1758.0 207.7 %scatter_custom_fusion.2 = f32[732,6]{1,0:T(8,128)S(1)} fusion(s32[38809]{0:T(1024)} %constant.294, f32[38809,6]{1,0:T(8,128)} %copy.208, f32[]{:T(128)} %constant.86.clone.1), kind=kCustom, calls=%fused_computation.254 | custom fusion | flops 232854 | bytes 18080 | tf_op jit(solution)/shard_map/scatter-add | solution.py:233
  2098.7 58.7 %reduce-scatter.41.cloned.1.call-done = f32[48,384]{1,0:T(8,128)} async-done(((f32[768,384]{1,0:T(8,128)}), f32[48,384]{1,0:T(8,128)}) %reduce-scatter.41.cloned.1.call-update) | async-done | bytes 73744 | tf_op jit(solution)/shard_map/reduce_scatter | solution.py:418
  2157.4 60.5 %reduce-scatter.39.cloned.1.call-done = f32[48,384]{1,0:T(8,128)} async-done(((f32[768,384]{1,0:T(8,128)}), f32[48,384]{1,0:T(8,128)}) %reduce-scatter.39.cloned.1.call-update) | async-done | bytes 73744 | tf_op jit(solution)/shard_map/reduce_scatter | solution.py:418
  2219.6 76.8 %reduce-scatter.49.cloned.1.call-done = f32[48,1536]{1,0:T(8,128)} async-done(((f32[768,1536]{1,0:T(8,128)}), f32[48,1536]{1,0:T(8,128)}) %reduce-scatter.49.cloned.1.call-update) | async-done | bytes 294928 | tf_op jit(solution)/shard_map/reduce_scatter | solution.py:420
  2296.4 79.0 %reduce-scatter.47.cloned.1.call-done = f32[48,1536]{1,0:T(8,128)} async-done(((f32[768,1536]{1,0:T(8,128)}), f32[48,1536]{1,0:T(8,128)}) %reduce-scatter.47.cloned.1.call-update) | async-done | bytes 294928 | tf_op jit(solution)/shard_map/reduce_scatter | solution.py:420
  2378.3 75.6 %reduce-scatter.45.cloned.1.call-done = f32[48,1536]{1,0:T(8,128)} async-done(((f32[768,1536]{1,0:T(8,128)}), f32[48,1536]{1,0:T(8,128)}) %reduce-scatter.45.cloned.1.call-update) | async-done | bytes 294928 | tf_op jit(solution)/shard_map/reduce_scatter | solution.py:419
  2453.9 78.9 %reduce-scatter.43.cloned.1.call-done = f32[48,1536]{1,0:T(8,128)} async-done(((f32[768,1536]{1,0:T(8,128)}), f32[48,1536]{1,0:T(8,128)}) %reduce-scatter.43.cloned.1.call-update) | async-done | bytes 294928 | tf_op jit(solution)/shard_map/reduce_scatter | solution.py:419
  2535.5 68.3 %reduce-scatter.37.cloned.1.call-done = f32[48,3,384]{2,0,1:T(8,128)} async-done(((f32[768,3,384]{2,0,1:T(8,128)}), f32[48,3,384]{2,0,1:T(8,128)}) %reduce-scatter.37.cloned.1.call-update) | async-done | bytes 221200 | tf_op jit(solution)/shard_map/reduce_scatter | solution.py:417
  2603.8 70.7 %reduce-scatter.35.cloned.1.call-done = f32[48,3,384]{2,0,1:T(8,128)} async-done(((f32[768,3,384]{2,0,1:T(8,128)}), f32[48,3,384]{2,0,1:T(8,128)}) %reduce-scatter.35.cloned.1.call-update) | async-done | bytes 221200 | tf_op jit(solution)/shard_map/reduce_scatter | solution.py:417
  2677.2 135.8 %reduce-scatter.33.cloned.1.call-done = f32[4096,48]{0,1:T(8,128)} async-done(((f32[4096,768]{0,1:T(8,128)}), f32[4096,48]{0,1:T(8,128)}) %reduce-scatter.33.cloned.1.call-update) | async-done | bytes 786448 | tf_op jit(solution)/shard_map/reduce_scatter | solution.py:397
  2815.9 135.1 %reduce-scatter.31.cloned.1.call-done = f32[4096,48]{0,1:T(8,128)} async-done(((f32[4096,768]{0,1:T(8,128)}), f32[4096,48]{0,1:T(8,128)}) %reduce-scatter.31.cloned.1.call-update) | async-done | bytes 786448 | tf_op jit(solution)/shard_map/reduce_scatter | solution.py:434
  (730 shorter events, 865.1 us)
Async XLA Ops:
  7.3 67.1 %all-gather.39.cloned.1.call-start = ((), (), s32[]{:S(2)}) async-start(), calls=%async_computation.10 | async-start | bytes 6684672 | tf_op jit(solution)/shard_map/all_gather | solution.py:336
  9.3 291.5 %all-gather.43.cloned.1.call-start = ((), (), s32[]{:S(2)}) async-start(), calls=%async_computation.22 | async-start | bytes 1880064 | tf_op jit(solution)/shard_map/all_gather | solution.py:70
  11.1 293.5 %all-gather.55.cloned.1.call-start = ((), (), s32[]{:S(2)}) async-start(), calls=%async_computation.28 | async-start | bytes 2727936 | tf_op jit(solution)/shard_map/all_gather | solution.py:59
  134.7 293.8 %all-gather.57.cloned.1.call-start = ((), (), s32[]{:S(2)}) async-start(), calls=%async_computation.29 | async-start | bytes 2727936 | tf_op jit(solution)/shard_map/all_gather | solution.py:59
  396.4 76.9 %all-gather.45.cloned.1.call-start = ((), (), s32[]{:S(2)}) async-start(), calls=%async_computation.23 | async-start | bytes 2506752 | tf_op jit(solution)/shard_map/all_gather | solution.py:72
  397.3 119.8 %all-gather.47.cloned.1.call-start = ((), (), s32[]{:S(2)}) async-start(), calls=%async_computation.24 | async-start | bytes 2506752 | tf_op jit(solution)/shard_map/all_gather | solution.py:73
  398.2 326.1 %all-gather.49.cloned.1.call-start = ((), (), s32[]{:S(2)}) async-start(), calls=%async_computation.25 | async-start | bytes 1880064 | tf_op jit(solution)/shard_map/all_gather | solution.py:70
  399.0 329.4 %all-gather.59.cloned.1.call-start = ((), (), s32[]{:S(2)}) async-start(), calls=%async_computation.30 | async-start | bytes 2727936 | tf_op jit(solution)/shard_map/all_gather | solution.py:59
  560.7 288.6 %all-gather.61.cloned.1.call-start = ((), (), s32[]{:S(2)}) async-start(), calls=%async_computation.31 | async-start | bytes 2727936 | tf_op jit(solution)/shard_map/all_gather | solution.py:59
  817.2 76.9 %all-gather.51.cloned.1.call-start = ((), (), s32[]{:S(2)}) async-start(), calls=%async_computation.26 | async-start | bytes 2506752 | tf_op jit(solution)/shard_map/all_gather | solution.py:72
  817.8 120.2 %all-gather.53.cloned.1.call-start = ((), (), s32[]{:S(2)}) async-start(), calls=%async_computation.27 | async-start | bytes 2506752 | tf_op jit(solution)/shard_map/all_gather | solution.py:73
  818.5 183.4 %all-gather.41.cloned.1.call-start = ((), (), s32[]{:S(2)}) async-start(), calls=%async_computation.11 | async-start | bytes 6684672 | tf_op jit(solution)/shard_map/all_gather | solution.py:337
  819.4 323.8 %all-gather.63.cloned.1.call-start = ((), (), s32[]{:S(2)}) async-start(), calls=%async_computation.32 | async-start | bytes 2727936 | tf_op jit(solution)/shard_map/all_gather | solution.py:59
  970.5 5.4 collective-permute-start.4
  1105.4 129.5 %all-gather.65.cloned.1.call-start = ((), (), s32[]{:S(2)}) async-start(), calls=%async_computation.33 | async-start | bytes 2727936 | tf_op jit(solution)/shard_map/all_gather | solution.py:59
  1200.9 151.9 %all-gather.67.cloned.1.call-start = ((), (), s32[]{:S(2)}) async-start(), calls=%async_computation.34 | async-start | bytes 2727936 | tf_op jit(solution)/shard_map/all_gather | solution.py:59
  1304.2 4.0 collective-permute-start.7
  1319.0 124.1 %all-gather.69.cloned.1.call-start = ((), (), s32[]{:S(2)}) async-start(), calls=%async_computation.35 | async-start | bytes 2727936 | tf_op jit(solution)/shard_map/all_gather | solution.py:59
  1394.5 4.0 collective-permute-start.8
  1409.2 626.4 %all-gather.71.cloned.1.call-start = ((), (), s32[]{:S(2)}) async-start(), calls=%async_computation.36 | async-start | bytes 2727936 | tf_op jit(solution)/shard_map/all_gather | solution.py:59
  1512.8 3.8 collective-permute-start.9
  1523.8 571.5 %all-reduce.30.cloned.1.call-start = ((), (), s32[]{:S(2)}) async-start(), calls=%async_computation.37 | async-start | bytes 344064 | tf_op jit(solution)/shard_map/psum | solution.py:440
  1969.4 187.9 %reduce-scatter.41.cloned.1.call-start = ((), (), s32[]{:S(2)}) async-start(), calls=%async_computation.17 | async-start | bytes 1253376 | tf_op jit(solution)/shard_map/reduce_scatter | solution.py:418
  1973.0 244.8 %reduce-scatter.39.cloned.1.call-start = ((), (), s32[]{:S(2)}) async-start(), calls=%async_computation.16 | async-start | bytes 1253376 | tf_op jit(solution)/shard_map/reduce_scatter | solution.py:418
  1977.2 319.2 %reduce-scatter.49.cloned.1.call-start = ((), (), s32[]{:S(2)}) async-start(), calls=%async_computation.21 | async-start | bytes 5013504 | tf_op jit(solution)/shard_map/reduce_scatter | solution.py:420
  1984.3 391.2 %reduce-scatter.47.cloned.1.call-start = ((), (), s32[]{:S(2)}) async-start(), calls=%async_computation.20 | async-start | bytes 5013504 | tf_op jit(solution)/shard_map/reduce_scatter | solution.py:420
  1992.8 461.1 %reduce-scatter.45.cloned.1.call-start = ((), (), s32[]{:S(2)}) async-start(), calls=%async_computation.19 | async-start | bytes 5013504 | tf_op jit(solution)/shard_map/reduce_scatter | solution.py:419
  2001.1 531.6 %reduce-scatter.43.cloned.1.call-start = ((), (), s32[]{:S(2)}) async-start(), calls=%async_computation.18 | async-start | bytes 5013504 | tf_op jit(solution)/shard_map/reduce_scatter | solution.py:419
  2009.5 594.3 %reduce-scatter.37.cloned.1.call-start = ((), (), s32[]{:S(2)}) async-start(), calls=%async_computation.15 | async-start | bytes 3760128 | tf_op jit(solution)/shard_map/reduce_scatter | solution.py:417
  2017.4 657.0 %reduce-scatter.35.cloned.1.call-start = ((), (), s32[]{:S(2)}) async-start(), calls=%async_computation.14 | async-start | bytes 3760128 | tf_op jit(solution)/shard_map/reduce_scatter | solution.py:417
  2025.3 787.7 %reduce-scatter.33.cloned.1.call-start = ((), (), s32[]{:S(2)}) async-start(), calls=%async_computation.13 | async-start | bytes 13369344 | tf_op jit(solution)/shard_map/reduce_scatter | solution.py:397
  2034.9 916.1 %reduce-scatter.31.cloned.1.call-start = ((), (), s32[]{:S(2)}) async-start(), calls=%async_computation.12 | async-start | bytes 13369344 | tf_op jit(solution)/shard_map/reduce_scatter | solution.py:434
  (175 other events, 9220.7 us)
Sparse Core Ops, SparseCore 0:
  11.0 63.4 all-gather.38
  77.3 37.9 all-gather.42
  134.8 30.3 all-gather.54
  396.5 31.9 all-gather.56
  431.2 42.0 all-gather.44
  476.0 40.9 all-gather.46
  520.0 38.6 all-gather.48
  560.8 31.5 all-gather.58
  817.3 31.9 all-gather.60
  852.0 42.0 all-gather.50
  896.9 40.9 all-gather.52
  940.7 61.1 all-gather.40
  1105.5 37.6 all-gather.62
  1201.0 33.7 all-gather.64
  1319.1 33.7 all-gather.66
  1409.3 33.7 all-gather.68
  1523.9 33.7 all-gather.70
  1969.5 125.6 all-reduce.29
  2098.8 58.4 reduce-scatter.40
  2160.8 56.9 reduce-scatter.38
  2221.7 74.6 reduce-scatter.48
  2300.8 74.6 reduce-scatter.46
  2379.3 74.5 reduce-scatter.44
  2458.1 74.6 reduce-scatter.42
  2536.6 67.1 reduce-scatter.36
  2607.5 66.9 reduce-scatter.34
  2678.4 134.5 reduce-scatter.32
  2817.0 133.9 reduce-scatter.30
where the time goes:
time: 2980 us; the launch traced here: 2960 us
  waiting for transfers between devices  1240 us (42%)
  local copies, waits for them, and re-layouts  589 us (20%)
  other arithmetic  537 us (18%)
  blocking collectives  324 us (11%)
  matrix products  225 us (8%)
    scatter-add x2, other arithmetic, backward_layer(): jax.ops.segment_sum(per_head.T, lookup.reshape(-1), num_segments=position...  415 us
    gather x8, local copies, waits for them, and re-layouts, local_bias(): return jnp.take(table_rows, lookup, axis=1)  285 us
    unnamed x11, blocking collectives  246 us
    all_gather x9, waiting for transfers between devices, spread_rows(): return lax.all_gather(value, 'tensor', axis=0, tiled=True)  192 us
    reduce_scatter x2, waiting for transfers between devices, local(): lax.psum_scatter(mats_grad[3], 'dp', scatter_dimension=0, tiled=True)  156 us
    reduce_scatter x2, waiting for transfers between devices, local(): lax.psum_scatter(mats_grad[2], 'dp', scatter_dimension=0, tiled=True)  154 us
    unnamed x381, local copies, waits for them, and re-layouts  140 us
    reduce_scatter x2, waiting for transfers between devices, local(): lax.psum_scatter(mats_grad[0], 'dp', scatter_dimension=0, tiled=True)  139 us
  transfers between devices with their start and end apart: 38, of which 30 were waited for; matrix products, arithmetic and copies ran while one was open for 36% of the time, Pallas kernels for 0%

commit v1 on v0

v1 whole, which is shorter than its diff:
```python
import functools
import math

import jax
import jax.numpy as jnp
import numpy as np
from jax import lax
from jax.experimental import pallas as pl
from jax.experimental.pallas import tpu as pltpu
from jax.sharding import PartitionSpec as P

HEADS = 12
HD = 64
STEP = 5

beta_one = 0.5
beta_two = 0.5
adam_eps = 1e-08
rate_matrix = 0.05
rate_vector = 0.3
rate_table = 0.5
decay_matrix = 0.05
norm_eps = 1e-06
F32 = jnp.float32
BF16 = jnp.bfloat16
BIG = -1e30
ROOT_HALF = 0.5**0.5


def dot_nn(a, b):
    return lax.dot_general(a, b, (((1,), (0,)), ((), ())), preferred_element_type=F32)


def dot_nt(a, b):
    return lax.dot_general(a, b, (((1,), (1,)), ((), ())), preferred_element_type=F32)


def dot_tn(a, b):
    return lax.dot_general(a, b, (((0,), (0,)), ((), ())), preferred_element_type=F32)


def norm_parts(values):
    center = values - jnp.mean(values, axis=-1, keepdims=True)
    spread_sq = jnp.mean(center * center, axis=-1, keepdims=True)
    scale = lax.rsqrt(spread_sq + norm_eps)
    return center * scale, scale


def norm_back(grad, values, gain):
    unit, scale = norm_parts(values)
    inner = grad * gain
    back = scale * (
        inner
        - jnp.mean(inner, axis=-1, keepdims=True)
        - unit * jnp.mean(inner * unit, axis=-1, keepdims=True)
    )
    return back, jnp.sum(grad * unit, axis=0), jnp.sum(grad, axis=0)


def norm_back(grad, values, gain):
    unit, scale = norm_parts(values)
    inner = grad * gain
    back = scale * (
        inner
        - jnp.mean(inner, axis=-1, keepdims=True)
        - unit * jnp.mean(inner * unit, axis=-1, keepdims=True)
    )
    return back, jnp.sum(grad * unit, axis=0), jnp.sum(grad, axis=0)


ROWS = 48


def row_loop(rows, body):
    def step(i, _):
        body(pl.ds(pl.multiple_of(i * ROWS, ROWS), ROWS))
        return 0

    lax.fori_loop(0, rows // ROWS, step, 0)


def lane_low():
    return lax.broadcasted_iota(jnp.int32, (1, 2 * HD), 1) < HD


def halves(pair):
    low = lane_low()
    zero = jnp.zeros_like(pair)
    return jnp.where(low, pair, zero), jnp.where(low, zero, pair)


def softmax_rows(scores):
    e = jnp.exp(scores - jnp.max(scores, axis=-1, keepdims=True))
    return e * (1.0 / jnp.sum(e, axis=-1, keepdims=True))


def attention_loop(seqs, lp, half, body):
    pairs = half // (2 * HD)
    for t in range(2):

        def step(s, _):
            rows = pl.ds(pl.multiple_of(s * lp, 16), lp)
            for hp in range(pairs):
                body(t, s, rows, hp * 2 * HD, t * 2 * pairs + 2 * hp)
            return 0

        lax.fori_loop(0, seqs, step, 0)


def forward_kernel(
    seqs, x, w_attn, w_up, w_down, vec, bias, out, y1, qkv, att, r, middle, y2, pre, hid, z
):
    rows, d = x.shape
    half = d // 2
    lp = rows // seqs
    ff = w_up.shape[-1]
    tile = ff // 3

    def first_norm(at):
        unit, _ = norm_parts(x[at, :])
        y1[at, :] = (unit * vec[0:1, :] + vec[1:2, :]).astype(BF16)

    row_loop(rows, first_norm)
    for t in range(2):
        for w in range(3):
            mixed = dot_nn(y1[...], w_attn[t, :, w * half : (w + 1) * half])
            if w != 1:
                row = 2 if w == 0 else 3
                mixed = mixed + vec[row : row + 1, t * half : (t + 1) * half]
            qkv[t, :, w * half : (w + 1) * half] = mixed.astype(BF16)

    def attend(t, s, at, col, head):
        q = qkv[t, at, pl.ds(col, 2 * HD)]
        k = qkv[t, at, pl.ds(half + col, 2 * HD)]
        v = qkv[t, at, pl.ds(2 * half + col, 2 * HD)]
        found = []
        for i, part in enumerate(halves(q)):
            scores = dot_nt(part, k) * HD**-0.5 + bias[head + i]
            found.append(dot_nn(softmax_rows(scores).astype(BF16), v))
        att[t, at, pl.ds(col, 2 * HD)] = jnp.where(lane_low(), found[0], found[1]).astype(BF16)

    attention_loop(seqs, lp, half, attend)
    r[...] = dot_nt(att[0], w_attn[0, :, 3 * half :])
    r[...] += dot_nt(att[1], w_attn[1, :, 3 * half :])

    def second_norm(at):
        here = x[at, :] + vec[5:6, :] * (r[at, :] + vec[4:5, :])
        middle[at, :] = here
        unit, _ = norm_parts(here)
        y2[at, :] = (unit * vec[6:7, :] + vec[7:8, :]).astype(BF16)

    row_loop(rows, second_norm)
    per = 2 * ff // d
    for t in range(2):
        for j in range(3):
            cols = slice(j * tile, (j + 1) * tile)
            a = dot_nn(y2[...], w_up[t, :, cols])
            off = t * ff + j * tile
            shift = jnp.concatenate(
                [
                    vec[10 + o // d : 11 + o // d, o % d : o % d + half // 3]
                    for o in range(off, off + tile, half // 3)
                ],
                axis=1,
            )
            a = a + shift
            pre[t, :, cols] = a
            h = (0.5 * a * (1.0 + lax.erf(a * ROOT_HALF))).astype(BF16)
            hid[t, :, cols] = h
            part = dot_nt(h, w_down[t, :, cols])
            if t == 0 and j == 0:
                z[...] = part
            else:
                z[...] += part

    def finish(at):
        out[at, :] = middle[at, :] + vec[9:10, :] * (z[at, :] + vec[8:9, :])

    row_loop(rows, finish)


def whole():
    return pl.BlockSpec(memory_space=pltpu.VMEM)


def third(shape, k):
    return pl.BlockSpec((shape[0], shape[1], shape[2] // 3), lambda *_: (0, 0, k))


def big_call(kernel, ins, specs, outs, scratch, name, flops):
    return pl.pallas_call(
        kernel,
        out_shape=outs,
        grid=(1,),
        in_specs=specs,
        out_specs=[
            pl.BlockSpec(o.shape, functools.partial(lambda n, *_: (0,) * n, len(o.shape)))
            for o in outs
        ],
        scratch_shapes=scratch,
        compiler_params=pltpu.CompilerParams(vmem_limit_bytes=60 * 2**20),
        cost_estimate=pl.CostEstimate(flops=flops, bytes_accessed=4 * 10**7, transcendentals=0),
        name=name,
    )(*ins)


def full(a):
    return pl.BlockSpec(a.shape, functools.partial(lambda n, *_: (0,) * n, len(a.shape)))


def forward_layer(x, weights, vec, bias, seqs):
    rows, d = x.shape
    half, ff = d // 2, weights.shape[2] // 3
    s = jax.ShapeDtypeStruct
    outs = [
        s((rows, d), F32),
        s((rows, d), BF16),
        s((2, rows, 3 * half), BF16),
        s((2, rows, half), BF16),
        s((rows, d), F32),
        s((rows, d), F32),
        s((rows, d), BF16),
        s((2, rows, ff), F32),
        s((2, rows, ff), BF16),
        s((rows, d), F32),
    ]
    specs = [full(x)] + [third(weights.shape, k) for k in range(3)] + [full(vec), full(bias)]
    ins = [x, weights, weights, weights, vec, bias]
    found = big_call(
        functools.partial(forward_kernel, seqs), ins, specs, outs, [], "forward", 10**10
    )
    return found[0], (x,) + tuple(found[1:])


def norm_back_rows(grad, values, gain):
    unit, scale = norm_parts(values)
    inner = grad * gain
    back = scale * (
        inner
        - jnp.mean(inner, axis=-1, keepdims=True)
        - unit * jnp.mean(inner * unit, axis=-1, keepdims=True)
    )
    return back, unit


def col_sum(v):
    return jnp.sum(v, axis=0, keepdims=True)


def feed_back_kernel(
    g, z, hid, pre, middle, y2, vec, w_up, w_down, gm, g_up, g_down, sums, upb, dz, dy2
):
    rows, d = g.shape
    ff = w_up.shape[-1]
    tile = ff // 3
    sums[...] = jnp.zeros_like(sums)

    def first(at):
        here = g[at, :]
        scaled = here * vec[9:10, :]
        dz[at, :] = scaled.astype(BF16)
        sums[0:1, :] += col_sum(scaled)
        sums[1:2, :] += col_sum(here * (z[at, :] + vec[8:9, :]))

    row_loop(rows, first)
    for t in range(2):
        for j in range(3):
            cols = slice(j * tile, (j + 1) * tile)
            dh = dot_nn(dz[...], w_down[t, :, cols])
            a = pre[t, :, cols]
            slope = 0.5 * (1.0 + lax.erf(a * ROOT_HALF))
            slope = slope + a * (jnp.exp(-0.5 * a * a) * (2 * math.pi) ** -0.5)
            da = (dh * slope).astype(BF16)
            upb[t : t + 1, cols] = col_sum(da.astype(F32))
            g_down[t, :, cols] = dot_tn(dz[...], hid[t, :, cols]).astype(BF16)
            g_up[t, :, cols] = dot_tn(y2[...], da).astype(BF16)
            part = dot_nt(da, w_up[t, :, cols])
            if t == 0 and j == 0:
                dy2[...] = part
            else:
                dy2[...] += part

    def last(at):
        grad = dy2[at, :]
        back, unit = norm_back_rows(grad, middle[at, :], vec[6:7, :])
        gm[at, :] = g[at, :] + back
        sums[2:3, :] += col_sum(grad * unit)
        sums[3:4, :] += col_sum(grad)

    row_loop(rows, last)


def attn_back_kernel(
    seqs, gm, r, x, y1, qkv, att, bias, vec, w_attn, g, g_attn, sums, rel, dr, do, dqkv, dy1
):
    rows, d = gm.shape
    half = d // 2
    lp = rows // seqs
    sums[...] = jnp.zeros_like(sums)

    def first(at):
        here = gm[at, :]
        scaled = here * vec[5:6, :]
        dr[at, :] = scaled.astype(BF16)
        sums[0:1, :] += col_sum(scaled)
        sums[1:2, :] += col_sum(here * (r[at, :] + vec[4:5, :]))

    row_loop(rows, first)
    for t in range(2):
        g_attn[t, :, 3 * half :] = dot_tn(dr[...], att[t]).astype(BF16)
        do[t] = dot_nn(dr[...], w_attn[t, :, 3 * half :]).astype(BF16)

    def attend(t, s, at, col, head):
        q = qkv[t, at, pl.ds(col, 2 * HD)]
        k = qkv[t, at, pl.ds(half + col, 2 * HD)]
        v = qkv[t, at, pl.ds(2 * half + col, 2 * HD)]
        o = do[t, at, pl.ds(col, 2 * HD)]
        dq, dk, dv = [], [], []
        for i, (q_part, o_part) in enumerate(zip(halves(q), halves(o))):
            p = softmax_rows(dot_nt(q_part, k) * HD**-0.5 + bias[head + i])
            dp = dot_nt(o_part, v)
            ds = (p * (dp - jnp.sum(p * dp, axis=-1, keepdims=True))).astype(BF16)
            wide = ds.astype(F32)
            rel[head + i] = jnp.where(s == 0, wide, rel[head + i] + wide)
            dq.append(dot_nn(ds, k))
            dk.append(dot_tn(ds, q))
            dv.append(dot_tn(p.astype(BF16), o))
        low = lane_low()
        for w, pair in enumerate((dq, dk, dv)):
            value = jnp.where(low, pair[0], pair[1])
            if w < 2:
                value = value * HD**-0.5
            dqkv[t, at, pl.ds(w * half + col, 2 * HD)] = value.astype(BF16)

    attention_loop(seqs, lp, half, attend)
    for t in range(2):
        for w in range(3):
            cols = slice(w * half, (w + 1) * half)
            part = dqkv[t, :, cols]
            if w != 1:
                row = 2 if w == 0 else 3
                sums[row : row + 1, t * half : (t + 1) * half] = col_sum(part.astype(F32))
            g_attn[t, :, cols] = dot_tn(y1[...], part).astype(BF16)
            more = dot_nt(part, w_attn[t, :, cols])
            if t == 0 and w == 0:
                dy1[...] = more
            else:
                dy1[...] += more

    def last(at):
        grad = dy1[at, :]
        back, unit = norm_back_rows(grad, x[at, :], vec[0:1, :])
        g[at, :] = gm[at, :] + back
        sums[4:5, :] += col_sum(grad * unit)
        sums[5:6, :] += col_sum(grad)

    row_loop(rows, last)


def backward_layer(g, saved, weights, vec, bias, seqs):
    x, y1, qkv, att, r, middle, y2, pre, hid, z = saved
    rows, d = x.shape
    half, ff = d // 2, weights.shape[2] // 3
    s = jax.ShapeDtypeStruct
    part = s((2, d, ff), BF16)
    ins = [g, z, hid, pre, middle, y2, vec, weights, weights]
    gm, g_up, g_down, low_sums, upb = big_call(
        feed_back_kernel,
        ins,
        [full(a) for a in ins[:7]] + [third(weights.shape, 1), third(weights.shape, 2)],
        [s((rows, d), F32), part, part, s((8, d), F32), s((8, ff), F32)],
        [pltpu.VMEM((rows, d), BF16), pltpu.VMEM((rows, d), F32)],
        "feed_back",
        12 * 10**9,
    )
    ins = [gm, r, x, y1, qkv, att, bias, vec, weights]
    g, g_attn, top_sums, rel = big_call(
        functools.partial(attn_back_kernel, seqs),
        ins,
        [full(a) for a in ins[:8]] + [third(weights.shape, 0)],
        [s((rows, d), F32), part, s((8, d), F32), s(bias.shape, F32)],
        [
            pltpu.VMEM((rows, d), BF16),
            pltpu.VMEM((2, rows, half), BF16),
            pltpu.VMEM((2, rows, 3 * half), BF16),
            pltpu.VMEM((rows, d), F32),
        ],
        "attn_back",
        6 * 10**9,
    )
    vec_grad = jnp.concatenate(
        [
            top_sums[4:6],
            top_sums[2:4],
            top_sums[0:2],
            low_sums[2:4],
            low_sums[0:2],
            upb[:2].reshape(4, d),
        ],
        axis=0,
    )
    return g, (g_attn, g_up, g_down), vec_grad, rel


def strip_constant(side):
    width = 2 * side - 1
    wide = -(-(width * side) // 128) * 128
    out = np.zeros((width * width, 16, wide), np.float32)
    for c in range(side):
        for k in range(width):
            for e in range(side):
                out[width * k + side - 1 - c + e, c, k * side + e] = 1.0
    return out.reshape(width * width, 16 * wide), wide


def split_three(v):
    high = lax.reduce_precision(v, 8, 7)
    rest = v - high
    mid = lax.reduce_precision(rest, 8, 7)
    return jnp.concatenate([high, mid, rest - mid], axis=0).astype(BF16)


def add_three(v):
    n = v.shape[0] // 3
    return v[:n] + v[n : 2 * n] + v[2 * n :]


def expand_kernel(side, strips, ends, out):
    lp = out.shape[1]
    wide = strips.shape[2]
    tokens = side * side + 1
    a = strips[0]
    lane = lax.broadcasted_iota(jnp.int32, (1, lp), 1)
    row_end, col_end, corner = ends[0, 0:1, 0:1], ends[0, 0:1, 1:2], ends[0, 0:1, 2:3]
    top = jnp.where(lane == 0, corner, row_end)
    out[0, 0:1, :] = jnp.where(lane < tokens, top, BIG)
    for r in range(side):
        shift = (side - 1 - r) * side - 1
        moved = pltpu.roll(a, (wide - shift) % wide, 1)[:side, :lp]
        moved = jnp.where(lane == 0, col_end, moved)
        out[0, 1 + r * side : 1 + (r + 1) * side, :] = jnp.where(lane < tokens, moved, BIG)
    tail = jnp.where(lane < tokens, 0.0, BIG)
    out[0, tokens:, :] = jnp.broadcast_to(tail, (lp - tokens, lp))


def expand_bias(position, side, lp):
    layers, heads, entries = position.shape
    flat = position.reshape(layers * heads, entries)
    hot, wide = strip_constant(side)
    cells = hot.shape[0]
    strips = add_three(dot_nn(split_three(flat[:, :cells][:, ::-1]), jnp.asarray(hot, BF16)))
    strips = strips.reshape(layers * heads, 16, wide)
    ends = jnp.pad(flat[:, cells:], ((0, 0), (0, 125)))[:, None, :]
    out = pl.pallas_call(
        functools.partial(expand_kernel, side),
        out_shape=jax.ShapeDtypeStruct((layers * heads, lp, lp), F32),
        grid=(layers * heads,),
        in_specs=[
            pl.BlockSpec((1, 16, wide), lambda i: (i, 0, 0)),
            pl.BlockSpec((1, 1, 128), lambda i: (i, 0, 0)),
        ],
        out_specs=pl.BlockSpec((1, lp, lp), lambda i: (i, 0, 0)),
        name="expand",
    )(strips, ends)
    return out.reshape(layers, heads, lp, lp)


def fold_kernel(side, grads, strips, ends):
    lp = grads.shape[1]
    wide = strips.shape[2]
    tokens = side * side + 1
    lane = lax.broadcasted_iota(jnp.int32, (1, lp), 1)
    total = jnp.zeros((16, wide), F32)
    for r in range(side):
        shift = (side - 1 - r) * side - 1
        part = jnp.where(lane == 0, 0.0, grads[0, 1 + r * side : 1 + (r + 1) * side, :])
        part = jnp.concatenate([part, jnp.zeros((16 - side, lp), F32)], axis=0)
        part = jnp.concatenate([part, jnp.zeros((16, wide - lp), F32)], axis=1)
        total = total + pltpu.roll(part, shift % wide, 1)
    strips[0] = total
    corner = grads[0, 0:1, 0:1]
    row_end = jnp.sum(grads[0, 0:1, :], axis=1, keepdims=True) - corner
    col_end = jnp.sum(grads[0, 1:tokens, 0:1], axis=0, keepdims=True)
    out_lane = lax.broadcasted_iota(jnp.int32, (1, 128), 1)
    ends[0] = jnp.where(
        out_lane == 0, row_end, jnp.where(out_lane == 1, col_end, jnp.where(out_lane == 2, corner, 0.0))
    )


def fold_bias(grads, side):
    layers, heads, lp, _ = grads.shape
    hot, wide = strip_constant(side)
    n = layers * heads
    strips, ends = pl.pallas_call(
        functools.partial(fold_kernel, side),
        out_shape=[
            jax.ShapeDtypeStruct((n, 16, wide), F32),
            jax.ShapeDtypeStruct((n, 1, 128), F32),
        ],
        grid=(n,),
        in_specs=[pl.BlockSpec((1, lp, lp), lambda i: (i, 0, 0))],
        out_specs=[
            pl.BlockSpec((1, 16, wide), lambda i: (i, 0, 0)),
            pl.BlockSpec((1, 1, 128), lambda i: (i, 0, 0)),
        ],
        name="fold",
    )(grads.reshape(n, lp, lp))
    cells = add_three(dot_nt(split_three(strips.reshape(n, 16 * wide)), jnp.asarray(hot, BF16)))
    flat = jnp.concatenate([cells[:, ::-1], ends[:, 0, :3]], axis=1)
    return flat.reshape(layers, heads, -1)


def adamw_update(master, gradient, first_mom, second_mom, step_rate, decay_rate):
    first_mom = beta_one * first_mom + (1.0 - beta_one) * gradient
    second_mom = beta_two * second_mom + (1.0 - beta_two) * gradient * gradient
    step_dir = (
        first_mom
        / (1.0 - beta_one**STEP)
        / (jnp.sqrt(second_mom / (1.0 - beta_two**STEP)) + adam_eps)
    )
    return (master - step_rate * (step_dir + decay_rate * master), first_mom, second_mom)


def pack_layer(in_proj, out_proj, up_proj, down_proj):
    return jnp.concatenate(
        [in_proj[:, 0], in_proj[:, 1], in_proj[:, 2], out_proj, up_proj, down_proj], axis=1
    )


MESH = pl.DeviceIdType.MESH


def place():
    dp = lax.axis_index("dp")
    return lax.axis_index("tensor"), dp // 4, lax.rem(dp // 2, 2), lax.rem(dp, 2)


def at(x, z, y, c):
    return ((z * 2 + y) * 2 + c, x)


def near(v, step, size):
    return lax.rem(v + step, size)


def greet(peers):
    barrier = pltpu.get_barrier_semaphore()
    for peer in peers:
        pl.semaphore_signal(barrier, inc=1, device_id=peer, device_id_type=MESH)
    pl.semaphore_wait(barrier, len(peers))


def gather_kernel(wide, *refs):
    n = len(wide)
    srcs, dsts = refs[:n], refs[n : 2 * n]
    own_sem, send_sem, recv_sem = refs[2 * n :]
    x, z, y, c = place()
    peer_x, peer_y, peer_c = at(1 - x, z, y, c), at(x, z, 1 - y, c), at(x, z, y, 1 - c)
    up, down = at(x, jnp.minimum(z + 1, 3), y, c), at(x, jnp.maximum(z - 1, 0), y, c)
    barrier = pltpu.get_barrier_semaphore()
    for peer in (peer_x, peer_y, peer_c):
        pl.semaphore_signal(barrier, inc=1, device_id=peer, device_id_type=MESH)

    @pl.when(z < 3)
    def _():
        pl.semaphore_signal(barrier, inc=1, device_id=up, device_id_type=MESH)

    @pl.when(z > 0)
    def _():
        pl.semaphore_signal(barrier, inc=1, device_id=down, device_id_type=MESH)

    pl.semaphore_wait(barrier, 3 + jnp.where(z < 3, 1, 0) + jnp.where(z > 0, 1, 0))

    def slot(i, ox, oz, oy, oc):
        ref = dsts[i]
        dp = (oz * 2 + oy) * 2 + oc
        return ref.at[ox, dp] if wide[i] else ref.at[dp]

    Z, Y, X, C, Z2 = 0, 4, 8, 16, 32

    def make(i, src, origin, way, peer, two=False):
        ox, oz, oy, oc = origin
        if way == Z:
            k = Z + oz
        elif way == Y:
            k = Y + oz
        elif way == X:
            k = X + oy * 4 + oz
        else:
            k = C + (ox * 2 + oy) * 4 + oz
        return pltpu.make_async_remote_copy(
            src_ref=src,
            dst_ref=slot(i, *origin),
            send_sem=send_sem.at[i, Z2 if two else k],
            recv_sem=recv_sem.at[i, k],
            device_id=peer,
            device_id_type=MESH,
        )

    own = (x, z, y, c)
    locals_ = []
    for i in range(n):
        copy = pltpu.make_async_copy(srcs[i], slot(i, *own), own_sem.at[i])
        copy.start()
        locals_.append(copy)

    def spread(i, src, origin, ways):
        for way, peer in ((Y, peer_y), (X, peer_x), (C, peer_c)):
            if way in ways and (wide[i] or way != X):
                make(i, src, origin, way, peer).start()

    def begin(i):
        src = srcs[i]

        @pl.when(z < 3)
        def _():
            make(i, src, own, Z, up).start()

        @pl.when(z > 0)
        def _():
            make(i, src, own, Z, down, True).start()

        spread(i, src, own, (Y, X, C))

    def each_z(fn):
        for k in (1, 2, 3):
            pl.when(z - k >= 0)(functools.partial(fn, z - k, True))
            pl.when(z + k <= 3)(functools.partial(fn, z + k, False))

    def landed(i, origin, way, peer):
        ref = slot(i, *origin)
        make(i, ref, origin, way, peer).wait_recv()
        return ref

    def after_z(i):
        def one(oz, rising):
            origin = (x, oz, y, c)
            ref = landed(i, origin, Z, up)
            if rising:

                @pl.when(z < 3)
                def _():
                    make(i, ref, origin, Z, up).start()
            else:

                @pl.when(z > 0)
                def _():
                    make(i, ref, origin, Z, down).start()

            spread(i, ref, origin, (Y, X, C))

        each_z(one)

    def after_y(i):
        def one(oz, rising):
            origin = (x, oz, 1 - y, c)
            spread(i, landed(i, origin, Y, peer_y), origin, (X, C))

        one(z, True)
        each_z(one)

    def after_x(i):
        for oy in (y, 1 - y):

            def one(oz, rising):
                origin = (1 - x, oz, oy, c)
                spread(i, landed(i, origin, X, peer_x), origin, (C,))

            one(z, True)
            each_z(one)

    AHEAD = 1
    for i in range(min(AHEAD, n)):
        begin(i)
    for i in range(n + 2):
        if i + AHEAD < n:
            begin(i + AHEAD)
        if i < n:
            after_z(i)
        if 0 <= i - 1 < n:
            after_y(i - 1)
        if 0 <= i - 2 < n and wide[i - 2]:
            after_x(i - 2)
    for i in range(n):
        for ox in (0, 1) if wide[i] else (x,):
            for oy in (0, 1):
                for oz in range(4):
                    landed(i, (ox, oz, oy, 1 - c), C, peer_c)
                    make(i, slot(i, ox, oz, oy, c), (ox, oz, oy, c), C, peer_c).wait_send()
        for oz in range(4):
            make(i, slot(i, x, oz, y, c), (x, oz, y, c), Y, peer_y).wait_send()
        if wide[i]:
            for oy in (0, 1):
                for oz in range(4):
                    make(i, slot(i, x, oz, oy, c), (x, oz, oy, c), X, peer_x).wait_send()

        def sent(oz, rising):
            origin = (x, oz, y, c)
            pl.when(z < 3 if rising else z > 0)(
                lambda: make(i, slot(i, *origin), origin, Z, up).wait_send()
            )

        each_z(sent)
        pl.when(z < 3)(lambda: make(i, srcs[i], own, Z, up).wait_send())
        pl.when(z > 0)(lambda: make(i, srcs[i], own, Z, down, True).wait_send())
        locals_[i].wait()


def gather_all(shards, wide, cid):
    n = len(shards)
    outs = [
        jax.ShapeDtypeStruct(((2, 16) if w else (16,)) + s.shape, s.dtype)
        for s, w in zip(shards, wide)
    ]
    any_ = pl.BlockSpec(memory_space=pl.ANY)
    return pl.pallas_call(
        functools.partial(gather_kernel, wide),
        out_shape=outs,
        in_specs=[any_] * n,
        out_specs=[any_] * n,
        scratch_shapes=[
            pltpu.SemaphoreType.DMA((n,)),
            pltpu.SemaphoreType.DMA((n, 33)),
            pltpu.SemaphoreType.DMA((n, 33)),
        ],
        compiler_params=pltpu.CompilerParams(collective_id=cid, has_side_effects=True),
        name="gather",
    )(*shards)


RING = 3


def reduce_kernel(nw, nt, *refs):
    srcs, small = refs[: nw + nt], refs[nw + nt]
    outs, small_out = refs[nw + nt + 1 : 2 * (nw + nt) + 1], refs[2 * (nw + nt) + 1]
    accw, rcw, rxw, ryw, rzw, acct, rct, ryt, rzt, tot, rsm = refs[2 * (nw + nt) + 2 : -3]
    send_sem, recv_sem, free_sem = refs[-3:]
    x, z, y, c = place()
    zs = [near(z, k, 4) for k in (1, 2, 3)]
    peer_x, peer_y, peer_c = at(1 - x, z, y, c), at(x, z, 1 - y, c), at(x, z, y, 1 - c)
    greet([at(x, k, y, c) for k in zs] + [peer_x, peer_y, peer_c])
    counts = [0]

    def remote(src, dst, peer):
        k = counts[0]
        counts[0] += 1
        copy = pltpu.make_async_remote_copy(
            src_ref=src,
            dst_ref=dst,
            send_sem=send_sem.at[k],
            recv_sem=recv_sem.at[k],
            device_id=peer,
            device_id_type=MESH,
        )
        copy.start()
        return copy

    def local(src, dst):
        k = counts[0]
        counts[0] += 1
        copy = pltpu.make_async_copy(src, dst, send_sem.at[k])
        copy.start()
        return copy

    rw, rt = accw.shape[-2], acct.shape[-2]
    wide = [(i, j) for i in range(nw) for j in range(0, srcs[0].shape[-2], rw)]
    slim = [(nw + i, j) for i in range(nt) for j in range(0, srcs[nw].shape[-2], rt)]

    def group(kind, chunk, gx, gy, gc):
        i, j = chunk
        rows = pl.ds(j, rw if kind == "w" else rt)
        if kind == "w":
            return srcs[i].at[gx, :, gy, gc, rows, :]
        return srcs[i].at[:, gy, gc, rows, :]

    def groups(kind):
        if kind == "w":
            return [(1 - x, 1 - y), (1 - x, y), (x, 1 - y), (x, y)]
        return [(0, 1 - y), (0, y)]

    bufs = {"w": (accw, rcw, rxw, ryw, rzw), "t": (acct, rct, None, ryt, rzt)}
    chunks = {"w": wide, "t": slim}
    state = {}
    pending = []

    def add_into(dst, other):
        def body(k, _):
            dst[k] = dst[k] + other[k]
            return 0

        lax.fori_loop(0, dst.shape[0], body, 0)

    def fetch(kind, k):
        acc, rc = bufs[kind][:2]
        items = []
        if k >= RING:
            pl.semaphore_wait(free_sem.at[0 if kind == "w" else 1], 1)
        for g, (gx, gy) in enumerate(groups(kind)):
            mine = local(group(kind, chunks[kind][k], gx, gy, c), acc.at[k, g])
            other = remote(group(kind, chunks[kind][k], gx, gy, 1 - c), rc.at[k % RING, g], peer_c)
            items.append((mine, other))
        state[kind, k] = items

    def core_sum(kind, k):
        acc, rc, rx, ry, _ = bufs[kind]
        sent = []
        for g, (mine, other) in enumerate(state[kind, k]):
            mine.wait()
            other.wait_recv()
            pending.append(other)
            add_into(acc.at[k, g], rc.at[k % RING, g])
            if kind == "w" and g < 2:
                sent.append(remote(acc.at[k, g], rx.at[k, g], peer_x))
            if kind == "t" and g == 0:
                sent.append(remote(acc.at[k, g], ry.at[k], peer_y))
        if k + RING < len(chunks[kind]):
            pl.semaphore_signal(
                free_sem.at[0 if kind == "w" else 1], inc=1, device_id=peer_c, device_id_type=MESH
            )
        state[kind, k] = sent

    def after_x(k):
        sent = state["w", k]
        for g in range(2):
            sent[g].wait_recv()
            pending.append(sent[g])
            add_into(accw.at[k, 2 + g], rxw.at[k, g])
            if g == 0:
                state["w", k] = [remote(accw.at[k, 2], ryw.at[k], peer_y)]

    def after_y(kind, k):
        acc, _, _, ry, rz = bufs[kind]
        last = 3 if kind == "w" else 1
        copy = state[kind, k][0]
        copy.wait_recv()
        pending.append(copy)
        add_into(acc.at[k, last], ry.at[k])
        state[kind, k] = [
            remote(acc.at[k, last, zs[s]], rz.at[k, 2 - s], at(x, zs[s], y, c)) for s in range(3)
        ]

    def after_z(kind, k):
        acc, _, _, _, rz = bufs[kind]
        last = 3 if kind == "w" else 1
        total = acc[k, last, z].astype(F32)
        for s in range(3):
            state[kind, k][s].wait_recv()
            pending.append(state[kind, k][s])
        for s in range(3):
            total = total + rz[k, s].astype(F32)
        i, j = chunks[kind][k]
        outs[i][j : j + total.shape[0], :] = total

    tot[0] = small[...]
    flips = [peer_c, peer_x, peer_y]
    flips += [at(x, z + 1 - 2 * lax.rem(z, 2), y, c), at(x, lax.rem(z + 2, 4), y, c)]
    small_state = []

    def small_step(s):
        if s > 0:
            copy = small_state[-1]
            copy.wait_recv()
            pending.append(copy)
            tot[s] = tot[s - 1] + rsm[s - 1]
        if s < len(flips):
            small_state.append(remote(tot.at[s], rsm.at[s], flips[s]))

    n, m = len(wide), len(slim)
    fetch("w", 0)
    fetch("t", 0)
    for k in range(max(n, m) + 4):
        if k + 1 < n:
            fetch("w", k + 1)
        if k < n:
            core_sum("w", k)
        if k + 1 < m:
            fetch("t", k + 1)
        if k < m:
            core_sum("t", k)
        if k <= len(flips):
            small_step(k)
        if 0 <= k - 1 < n:
            after_x(k - 1)
        if 0 <= k - 1 < m:
            after_y("t", k - 1)
        if 0 <= k - 2 < n:
            after_y("w", k - 2)
        if 0 <= k - 2 < m:
            after_z("t", k - 2)
        if 0 <= k - 3 < n:
            after_z("w", k - 3)
    small_out[...] = tot[len(flips)]
    for copy in pending:
        copy.wait_send()


def reduce_all(wide, slim, small, cid):
    nw, nt = len(wide), len(slim)
    rows, cw = wide[0].shape[-2:]
    ct = slim[0].shape[-1]
    kw, kt = nw, nt * rows // 16
    outs = [jax.ShapeDtypeStruct((rows, a.shape[-1]), F32) for a in wide + slim]
    outs.append(jax.ShapeDtypeStruct(small.shape, F32))
    copies = kw * (8 + 2 + 1 + 3) + kt * (4 + 1 + 3) + 5
    any_ = pl.BlockSpec(memory_space=pl.ANY)
    vm = pl.BlockSpec(memory_space=pltpu.VMEM)
    return pl.pallas_call(
        functools.partial(reduce_kernel, nw, nt),
        out_shape=outs,
        in_specs=[any_] * (nw + nt) + [vm],
        out_specs=[vm] * (nw + nt + 1),
        scratch_shapes=[
            pltpu.VMEM((kw, 4, 4, rows, cw), BF16),
            pltpu.VMEM((RING, 4, 4, rows, cw), BF16),
            pltpu.VMEM((kw, 2, 4, rows, cw), BF16),
            pltpu.VMEM((kw, 4, rows, cw), BF16),
            pltpu.VMEM((kw, 3, rows, cw), BF16),
            pltpu.VMEM((kt, 2, 4, 16, ct), BF16),
            pltpu.VMEM((RING, 2, 4, 16, ct), BF16),
            pltpu.VMEM((kt, 4, 16, ct), BF16),
            pltpu.VMEM((kt, 3, 16, ct), BF16),
            pltpu.VMEM((6,) + small.shape, F32),
            pltpu.VMEM((5,) + small.shape, F32),
            pltpu.SemaphoreType.DMA((copies,)),
            pltpu.SemaphoreType.DMA((copies,)),
            pltpu.SemaphoreType.REGULAR((2,)),
        ],
        compiler_params=pltpu.CompilerParams(
            collective_id=cid, has_side_effects=True, vmem_limit_bytes=62 * 2**20
        ),
        name="reduce",
    )(*wide, *slim, small)


def gather_plain(shards, wide):
    full = [lax.all_gather(s, "dp") for s in shards]
    return [lax.all_gather(f, "tensor") if w else f for f, w in zip(full, wide)]


def reduce_plain(wide, slim, small):
    outs = []
    for grads in wide:
        part = lax.psum_scatter(grads, "tensor", scatter_dimension=0, tiled=False)
        outs.append(lax.psum_scatter(part, "dp", scatter_dimension=0, tiled=False).astype(F32))
    for grads in slim:
        outs.append(lax.psum_scatter(grads, "dp", scatter_dimension=0, tiled=False).astype(F32))
    outs.append(lax.psum(small, ("dp", "tensor")))
    return outs


def local(
    token_codes,
    mask_slots,
    mask_counts,
    embedding,
    emb_first,
    emb_second,
    readout,
    read_first,
    read_second,
    in_proj,
    in_first,
    in_second,
    out_proj,
    out_first,
    out_second,
    up_proj,
    up_first,
    up_second,
    down_proj,
    down_first,
    down_second,
    vectors,
    vec_first,
    vec_second,
    position,
    pos_first,
    pos_second,
):
    tensor_at = lax.axis_index("tensor")
    tensor_size = lax.axis_size("tensor")
    seqs, patches = token_codes.shape
    side = math.isqrt(patches)
    tokens = patches + 1
    lp = -(-tokens // 16) * 16
    slots = mask_slots.shape[1]
    mine = seqs // tensor_size
    layers = in_proj.shape[0]
    tail = vectors.shape[0] - 4
    half_vocab = embedding.shape[0]
    vocab_start = tensor_at * half_vocab
    d = vectors.shape[1]

    live_slot = jnp.arange(slots)[None, :] < mask_counts[:, None]
    hits = (mask_slots[:, :, None] == jnp.arange(patches)[None, None, :])
    masked = jnp.any(hits & live_slot[:, :, None], axis=1)
    targets = jnp.sum(jnp.where(hits, token_codes[:, None, :], 0), axis=2)
    count_here = jnp.sum(mask_counts.astype(F32))
    dp_size = lax.axis_size("dp")
    custom = dp_size == 16 and tensor_size == 2

    shards = [
        pack_layer(in_proj[l], out_proj[l], up_proj[l], down_proj[l]).astype(BF16)
        for l in range(layers)
    ]
    sources = [
        shards[0],
        jnp.full((8, 128), count_here),
        shards[1],
        embedding.T.astype(BF16),
        readout.T.astype(BF16),
    ]
    wide = (True, False, True, False, False)
    found = gather_all(sources, wide, 1) if custom else gather_plain(sources, wide)
    mask_total = jnp.sum(found[1][:, 0, 0])
    weights = [found[0].reshape(2, d, -1), found[2].reshape(2, d, -1)]
    emb_table = found[3].reshape(d, half_vocab)
    read_table = found[4].reshape(d, half_vocab)

    code_rows = jnp.where(masked, -1, token_codes - vocab_start)
    code_rows = jnp.pad(code_rows, ((0, 0), (1, lp - tokens)), constant_values=-1).reshape(-1)
    code_hot = (code_rows[:, None] == jnp.arange(half_vocab)[None, :]).astype(BF16)
    part = dot_nt(code_hot, emb_table).astype(BF16)
    summed = lax.psum_scatter(part, "tensor", scatter_dimension=0, tiled=True).astype(F32)
    my_masked = lax.dynamic_slice_in_dim(masked, tensor_at * mine, mine, 0)
    mask_flag = jnp.pad(my_masked.astype(F32), ((0, 0), (1, lp - tokens))).reshape(-1, 1)
    lead_flag = jnp.zeros((mine, lp), F32).at[:, 0].set(1.0).reshape(-1, 1)
    x = summed + lead_flag * vectors[tail] + mask_flag * vectors[tail + 1]

    biases = expand_bias(position, side, lp)
    kept = []
    for l in range(layers):
        x, saved = forward_layer(x, weights[l], vectors[14 * l : 14 * l + 14], biases[l], mine)
        kept.append(saved)

    my_slots = lax.dynamic_slice_in_dim(mask_slots, tensor_at * mine, mine, 0)
    pick = (jnp.arange(mine)[:, None] * lp + 1 + my_slots).reshape(-1)
    final_in = x[pick]
    unit, _ = norm_parts(final_in)
    u = (unit * vectors[tail + 2] + vectors[tail + 3]).astype(BF16)
    u_all = lax.all_gather(u, "tensor", axis=0, tiled=True)
    logits = dot_nn(u_all, read_table)
    is_target = jnp.arange(half_vocab)[None, :] == (targets.reshape(-1) - vocab_start)[:, None]
    peak = jnp.max(logits, axis=1)
    total = jnp.sum(jnp.exp(logits - peak[:, None]), axis=1)
    chosen = jnp.sum(jnp.where(is_target, logits, 0.0), axis=1)
    stats = lax.all_gather(jnp.stack([peak, total, chosen]), "tensor")
    top = jnp.maximum(stats[0, 0], stats[1, 0])
    log_total = top + jnp.log(
        stats[0, 1] * jnp.exp(stats[0, 0] - top) + stats[1, 1] * jnp.exp(stats[1, 0] - top)
    )
    weight_row = live_slot.reshape(-1).astype(F32)
    loss_here = jnp.sum((log_total - stats[0, 2] - stats[1, 2]) * weight_row)
    g_logits = (jnp.exp(logits - log_total[:, None]) - is_target.astype(F32)) * (
        weight_row / mask_total
    )[:, None]
    g_logits = g_logits.astype(BF16)
    grad_final = lax.psum_scatter(
        dot_nt(g_logits, read_table).astype(BF16), "tensor", scatter_dimension=0, tiled=True
    ).astype(F32)
    grad_read = dot_tn(u_all, g_logits)
    back, g_gain, g_shift = norm_back(grad_final, final_in, vectors[tail + 2])
    g = jnp.zeros_like(x).at[pick].add(back)

    mat_grads = [None] * layers
    vec_grads = [None] * layers
    rel_grads = [None] * layers
    for l in reversed(range(layers)):
        g, full, vec_grads[l], rel = backward_layer(
            g, kept[l], weights[l], vectors[14 * l : 14 * l + 14], biases[l], mine
        )
        mat_grads[l] = full
        rel_grads[l] = rel

    g0 = g.astype(BF16)
    grad_lead = jnp.sum(g0.astype(F32) * lead_flag, axis=0)
    grad_mask = jnp.sum(g0.astype(F32) * mask_flag, axis=0)
    g0_all = lax.all_gather(g0, "tensor", axis=0, tiled=True)
    grad_emb = dot_tn(g0_all, code_hot)
    vec_local = jnp.concatenate(
        vec_grads + [jnp.stack([grad_lead, grad_mask, g_gain, g_shift])], axis=0
    )
    small_parts = [vec_local, fold_bias(jnp.stack(rel_grads), side), loss_here / tensor_size]
    flat = jnp.concatenate([p.reshape(-1) for p in small_parts])
    flat = jnp.pad(flat, (0, -flat.size % 1024)).reshape(-1, 128)
    if custom:
        lead = (4, 2, 2, d // 16)
        reduced = reduce_all(
            [m.reshape((2,) + lead + m.shape[-1:]) for layer in mat_grads for m in layer],
            [m.astype(BF16).reshape(lead + m.shape[-1:]) for m in (grad_read, grad_emb)],
            flat,
            2,
        )
    else:
        lead = (dp_size, d // dp_size)
        reduced = reduce_plain(
            [m.reshape((2,) + lead + m.shape[-1:]) for layer in mat_grads for m in layer],
            [m.astype(BF16).reshape(lead + m.shape[-1:]) for m in (grad_read, grad_emb)],
            flat,
        )
    grad_read, grad_emb, flat = reduced[3 * layers :]
    flat = flat.reshape(-1)
    vec_all = flat[: vectors.size].reshape(vectors.shape)
    rel_all = flat[vectors.size : vectors.size + position.size].reshape(position.shape)
    loss_sum = flat[vectors.size + position.size]

    half = d // 2
    in_g, out_g, up_g, down_g = [], [], [], []
    for l in range(layers):
        attn, up, down = reduced[3 * l : 3 * l + 3]
        in_g.append(attn[:, : 3 * half].reshape(-1, 3, half))
        out_g.append(attn[:, 3 * half :])
        up_g.append(up)
        down_g.append(down)
    emb_new = adamw_update(
        embedding, grad_emb.astype(F32).T, emb_first, emb_second, rate_table, decay_matrix
    )
    read_new = adamw_update(
        readout, grad_read.astype(F32).T, read_first, read_second, rate_matrix, decay_matrix
    )
    in_new = adamw_update(in_proj, jnp.stack(in_g), in_first, in_second, rate_matrix, decay_matrix)
    out_new = adamw_update(
        out_proj, jnp.stack(out_g), out_first, out_second, rate_matrix, decay_matrix
    )
    up_new = adamw_update(up_proj, jnp.stack(up_g), up_first, up_second, rate_matrix, decay_matrix)
    down_new = adamw_update(
        down_proj, jnp.stack(down_g), down_first, down_second, rate_matrix, decay_matrix
    )
    vec_new = adamw_update(vectors, vec_all, vec_first, vec_second, rate_vector, 0.0)
    pos_new = adamw_update(position, rel_all, pos_first, pos_second, rate_vector, 0.0)
    return (
        (loss_sum, mask_total)
        + emb_new
        + read_new
        + in_new
        + out_new
        + up_new
        + down_new
        + vec_new
        + pos_new
        + tuple(n[0].astype(BF16) for n in (in_new, out_new, up_new, down_new))
    )


def solution(mesh):
    table = P("tensor", "dp")
    in_spec = P(None, "dp", None, "tensor")
    mat = P(None, "dp", "tensor")
    return jax.shard_map(
        local,
        mesh=mesh,
        in_specs=(P("dp", None), P("dp", None), P("dp"))
        + (table,) * 6
        + (in_spec,) * 3
        + (mat,) * 9
        + (P(),) * 6,
        out_specs=(P(), P())
        + (table,) * 6
        + (in_spec,) * 3
        + (mat,) * 9
        + (P(),) * 6
        + (in_spec, mat, mat, mat),
        check_vma=False,
    )
```

time: 2980 us -> 846 us (0.28)
  waiting for transfers between devices: 1240 us -> 24.4 us
  Pallas kernels: 0 us -> 632 us
  local copies, waits for them, and re-layouts: 589 us -> 37 us
  other arithmetic: 537 us -> 44.2 us
  blocking collectives: 324 us -> 23.9 us
  matrix products: 225 us -> 53.8 us
    reduce_scatter x10 -> x1, waiting for transfers between devices: 839 us -> 0.01 us  [local(): lax.psum_scatter(part, 'tensor', scatter_dimension=0, tiled=True)]
    pallas_call x0 -> x10, Pallas kernels: none -> 632 us  [the longest x6 231 us: big_call(): pl.pallas_call(kernel, out_shape=outs, grid=(1,), in_specs=specs, out_spe...]
    scatter-add x4 -> x1, other arithmetic: 436 us -> 3.85 us  [local(): g = jnp.zeros_like(x).at[pick].add(back)]
    all_gather x17 -> x1, waiting for transfers between devices: 380 us -> 24.4 us  [local(): g0_all = lax.all_gather(g0, 'tensor', axis=0, tiled=True)]
    gather x14 -> x1, local copies, waits for them, and re-layouts: 305 us -> 2.86 us  [local(): final_in = x[pick]]
    unnamed x11 -> x1, blocking collectives: 246 us -> 9.81 us
    dot_general x39 -> x7, matrix products: 225 us -> 53.8 us  [the longest x3 23.1 us: dot_nt(): lax.dot_general(a, b, (((1,), (1,)), ((), ())), preferred_element_type=F32)]
    unnamed x381 -> x111, local copies, waits for them, and re-layouts: 140 us -> 9.63 us
  transfers between devices with their start and end apart: 38 -> 3, of which waited for: 30 -> 1; matrix products, arithmetic and copies ran while one was open for 36% -> 4% of each run, Pallas kernels for 0% -> 2%
where the time goes in v1:
time: 846 us; the launch traced here: 837 us
  Pallas kernels  632 us (75%)
  matrix products  53.8 us (6%)
  other arithmetic  44.2 us (5%)
  local copies, waits for them, and re-layouts  37 us (4%)
  waiting for transfers between devices  24.4 us (3%)
  blocking collectives  23.9 us (3%)
  between operations  17.9 us (2%)
    pallas_call x6, Pallas kernels, big_call(): pl.pallas_call(kernel, out_shape=outs, grid=(1,), in_specs=specs, out_spe...  231 us
    pallas_call x1, Pallas kernels, reduce_all(): pl.pallas_call(functools.partial(reduce_kernel, nw, nt), out_shape=outs,...  209 us
    pallas_call x1, Pallas kernels, gather_all(): pl.pallas_call(functools.partial(gather_kernel, wide), out_shape=outs, in...  164 us
    all_gather x1, waiting for transfers between devices, local(): g0_all = lax.all_gather(g0, 'tensor', axis=0, tiled=True)  24.4 us
    dot_general x3, matrix products, dot_nt(): lax.dot_general(a, b, (((1,), (1,)), ((), ())), preferred_element_type=F32)  23.1 us
    dot_general x2, matrix products, dot_tn(): lax.dot_general(a, b, (((0,), (0,)), ((), ())), preferred_element_type=F32)  20 us
  transfers between devices with their start and end apart: 3, of which 1 were waited for; matrix products, arithmetic and copies ran while one was open for 4% of the time, Pallas kernels for 2%

profile of v1, /device:TPU:9, one launch (start us, length us, event | category | flops | bytes accessed | tf_op | source)
XLA Modules:
  0.0 836.9 jit_solution(16884866850082730724)
XLA Ops:
  15.3 2.3 convert_bitcast_fusion
  19.0 163.7 %gather.7 = (bf16[2,16,48,4608]{3,2,1,0:T(8,128)(2,1)}, f32[16,8,128]{2,1,0:T(8,128)}, bf16[2,16,48,4608]{3,2,1,0:T(8,128)(2,1)}, bf16[16,48,4096]{2,1,0:T(8,128)(2,1)}, bf16[16,48,4096]{2,1,0:T(8,128)(2,1)}) custom-call(bf16[48,4608]{1,0:T(8,128)(2,1)} %copy-done.19, f32[8,128]{1,0:T(8,128)} %broadcast_in_dim.27.refs_1_, bf16[48,4608]{1,0:T(8,128)(2,1)} %copy-done.20, ...), custom_call_target="tpu_custom_call" | custom-call | tf_op jit(solution)/shard_map/gather/pallas_call | solution.py:716
  182.7 13.4 %fusion.6 = bf16[1248,768]{1,0:T(8,128)(2,1)} fusion(bf16[768,4096]{1,0:T(8,128)(2,1)} %bitcast.180, s32[1248]{0:T(1024)S(1)} %eq.44), kind=kOutput, calls=%fused_computation.14 | convolution fusion | flops 7857807360 | bytes 8213376 | tf_op jit(solution)/shard_map/dot_general | solution.py:35
  198.9 5.3 fusion.43
  209.9 13.7 %expand.1 = f32[24,208,208]{2,1,0:T(8,128)} custom-call(f32[24,16,384]{2,1,0:T(8,128)} %bitcast.153, f32[24,1,128]{2,1,0:T(1,128)} %bitcast.165), custom_call_target="tpu_custom_call" | custom-call | tf_op jit(solution)/shard_map/expand/pallas_call | solution.py:454
  224.3 5.2 fusion.75
  229.5 2.9 multiply_add_fusion.x
  232.4 39.8 %forward.2 = (f32[624,768]{1,0:T(8,128)}, bf16[624,768]{1,0:T(8,128)(2,1)}, bf16[2,624,1152]{2,1,0:T(8,128)(2,1)}, bf16[2,624,384]{2,1,0:T(8,128)(2,1)}, f32[624...) custom-call(f32[624,768]{1,0:T(8,128)} %multiply_add_fusion.x, ...), custom_call_target="tpu_custom_call" | custom-call | flops 10000000000 | bytes 40000000 | tf_op jit(solution)/shard_map/forward/pallas_call | solution.py:191
  272.1 39.3 %forward.3 = (f32[624,768]{1,0:T(8,128)}, bf16[624,768]{1,0:T(8,128)(2,1)}, bf16[2,624,1152]{2,1,0:T(8,128)(2,1)}, bf16[2,624,384]{2,1,0:T(8,128)(2,1)}, f32[624...) custom-call(f32[624,768]{1,0:T(8,128)} %get-tuple-element.98.x, ...), custom_call_target="tpu_custom_call" | custom-call | flops 10000000000 | bytes 40000000 | tf_op jit(solution)/shard_map/forward/pallas_call | solution.py:191
  311.4 2.9 gather_fusion
  314.8 10.8 %all-gather.1 = bf16[2,234,768]{2,1,0:T(8,128)(2,1)S(1)} all-gather(bf16[1,234,768]{2,1,0:T(8,128)(2,1)S(1)} %fusion.29), channel_id=1, replica_groups=mesh['dp'=16,'tensor'=2] {'tensor'}, dimensions={0}, use_global_device_ids=true | all-gather | bytes 1078272 | tf_op jit(solution)/shard_map/all_gather | solution.py:1042
  325.8 5.5 fusion.81
  331.3 2.7 exponential_reduce_fusion
  334.1 3.2 all-gather.2
  337.9 3.1 multiply_convert_fusion
  341.0 1.9 copy-done
  342.9 3.3 convolution_convert_fusion.1
  346.2 9.8 %fusion = bf16[240,768]{1,0:T(8,128)(2,1)S(1)} fusion(bf16[468,768]{1,0:T(8,128)(2,1)S(1)} %convolution_convert_fusion.1), kind=kCustom, calls=%all-reduce-scatter | all-reduce-scatter fusion | flops 368641 | bytes 1088000
  356.0 3.1 collective-permute-start
  359.2 7.5 convolution_convert_fusion
  369.3 3.8 scatter_custom_fusion.g
  373.1 32.4 %feed_back.2 = (f32[624,768]{1,0:T(8,128)}, bf16[2,768,1536]{2,1,0:T(8,128)(2,1)}, bf16[2,768,1536]{2,1,0:T(8,128)(2,1)}, f32[8,768]{1,0:T(8,128)}, f32[8,1536]{1,0:T(8,128)}) custom-call(f32[624,768]{1,0:T(8,128)} %scatter_custom_fusion.g, f32[624,768]{1,0:T(8,128)} %get-tuple-element.103.z, bf16[2,624,1536]{2,1,0:T(8,128)(2,1)} %get-tuple-element.104.hid, ...), custom_call_target="tpu_custom_call" | custom-call | flops 12000000000 | bytes 40000000 | tf_op jit(solution)/shard_map/feed_back/pallas_call | solution.py:191
  405.5 43.3 %attn_back.2 = (f32[624,768]{1,0:T(8,128)}, bf16[2,768,1536]{2,1,0:T(8,128)(2,1)}, f32[8,768]{1,0:T(8,128)}, f32[12,208,208]{2,1,0:T(8,128)}) custom-call(f32[624,768]{1,0:T(8,128)} %get-tuple-element.108.gm, f32[624,768]{1,0:T(8,128)} %get-tuple-element.109.r, f32[624,768]{1,0:T(8,128)} %get-tuple-element.98.x, bf16[624,768]{1,0:T(8,128)(2,1)} %get-tuple-element.110.y1, ...), custom_call_target="tpu_custom_call" | custom-call | flops 6000000000 | bytes 40000000 | tf_op jit(solution)/shard_map/attn_back/pallas_call | solution.py:191
  448.8 32.8 %feed_back.3 = (f32[624,768]{1,0:T(8,128)}, bf16[2,768,1536]{2,1,0:T(8,128)(2,1)}, bf16[2,768,1536]{2,1,0:T(8,128)(2,1)}, f32[8,768]{1,0:T(8,128)}, f32[8,1536]{1,0:T(8,128)}) custom-call(f32[624,768]{1,0:T(8,128)} %get-tuple-element.113.g, f32[624,768]{1,0:T(8,128)} %get-tuple-element.114.z, bf16[2,624,1536]{2,1,0:T(8,128)(2,1)} %get-tuple-element.115.hid, ...), custom_call_target="tpu_custom_call" | custom-call | flops 12000000000 | bytes 40000000 | tf_op jit(solution)/shard_map/feed_back/pallas_call | solution.py:191
  481.6 43.5 %attn_back.3 = (f32[624,768]{1,0:T(8,128)}, bf16[2,768,1536]{2,1,0:T(8,128)(2,1)}, f32[8,768]{1,0:T(8,128)}, f32[12,208,208]{2,1,0:T(8,128)}) custom-call(f32[624,768]{1,0:T(8,128)} %get-tuple-element.119.gm, f32[624,768]{1,0:T(8,128)} %get-tuple-element.120.r, f32[624,768]{1,0:T(8,128)} %multiply_add_fusion.x, bf16[624,768]{1,0:T(8,128)(2,1)} %get-tuple-element.121.y1, ...), custom_call_target="tpu_custom_call" | custom-call | flops 6000000000 | bytes 40000000 | tf_op jit(solution)/shard_map/attn_back/pallas_call | solution.py:191
  525.1 4.4 pad_maximum_fusion
  529.5 15.2 %fold.1 = (f32[24,16,384]{2,1,0:T(8,128)}, f32[24,1,128]{2,1,0:T(1,128)}) custom-call(f32[24,208,208]{2,1,0:T(8,128)} %bitcast.142), custom_call_target="tpu_custom_call" | custom-call | tf_op jit(solution)/shard_map/fold/pallas_call | solution.py:494
  547.5 6.3 fusion.14
  557.3 24.4 %all-gather.5.cloned.1.call-done = bf16[1248,768]{1,0:T(8,128)(2,1)} async-done(((bf16[624,768]{1,0:T(8,128)(2,1)}), bf16[1248,768]{1,0:T(8,128)(2,1)}) %all-gather.5.cloned.1.call-update) | async-done | bytes 1916944 | tf_op jit(solution)/shard_map/all_gather | solution.py:1079
  581.7 12.6 %fusion.5 = bf16[768,4096]{1,0:T(8,128)(2,1)} fusion(bf16[1248,768]{1,0:T(8,128)(2,1)} %all-gather.5.cloned.1.call-done, s32[1248]{0:T(1024)S(1)} %eq.44), kind=kOutput, calls=%fused_computation.12 | convolution fusion | flops 7859994624 | bytes 8213376 | tf_op jit(solution)/shard_map/dot_general | solution.py:39
  594.3 208.7 %reduce.21 = (f32[48,1536]{1,0:T(8,128)}, f32[48,1536]{1,0:T(8,128)}, f32[48,1536]{1,0:T(8,128)}, f32[48,1536]{1,0:T(8,128)}, f32[48,1536]{1,0:T(8,128)}, /*inde...) custom-call(bf16[2,4,2,2,48,1536]{5,4,3,2,1,0:T(8,128)(2,1)} %bitcast.150, ...), custom_call_target="tpu_custom_call" | custom-call | tf_op jit(solution)/shard_map/reduce/pallas_call | solution.py:908
  818.5 2.5 fusion.69
  (207 shorter events, 49.9 us)
Async XLA Ops:
  7.2 222.3 %reduce-scatter.4.cloned.1.call-start = ((), (), s32[]{:S(2)}) async-start(), calls=%async_computation.1 | async-start | bytes 2875392 | tf_op jit(solution)/shard_map/reduce_scatter | solution.py:1025
  182.7 15.5 %copy-start.29 = (f32[2,12,732]{2,0,1:T(2,128)S(1)}, f32[2,12,732]{2,0,1:T(2,128)}, u32[]{:S(2)}) copy-start(f32[2,12,732]{2,0,1:T(2,128)} %param.55) | copy-start | bytes 210820
  196.2 385.6 %all-gather.5.cloned.1.call-start = ((), (), s32[]{:S(2)}) async-start(), calls=%async_computation.2 | async-start | bytes 2875392 | tf_op jit(solution)/shard_map/all_gather | solution.py:1079
  198.8 6.9 copy-start.35
  198.8 7.1 copy-start.34
  198.9 9.6 %copy-start.41 = (s32[6]{0:T(128)S(1)}, s32[6]{0:T(128)}, u32[]{:S(2)}) copy-start(s32[6]{0:T(128)} %param.33) | copy-start | bytes 76
  198.9 9.8 %copy-start.42 = (u32[32]{0:T(128)S(1)}, u32[32]{0:T(128)}, u32[]{:S(2)}) copy-start(u32[32]{0:T(128)} %constant.139) | copy-start | bytes 388
  204.2 19.3 %copy-start.21 = (f32[32,768]{1,0:T(8,128)S(1)}, f32[32,768]{1,0:T(8,128)}, u32[]{:S(2)}) copy-start(f32[32,768]{1,0:T(8,128)} %param.52) | copy-start | bytes 294916
  331.3 11.6 %slice-start = ((s8[6291456]{0:T(1024)(128)(4,1)}), s8[4194304]{0:T(1024)(128)(4,1)S(1)}, s32[]{:S(2)}) async-start(s8[6291456]{0:T(1024)(128)(4,1)} %bitcast.177), calls=%async_computation.3 | async-start | bytes 8388608
  337.9 5.0 slice-start.1
  356.0 11.2 %collective-permute-start = (bf16[6,768]{1,0:T(8,128)(2,1)S(1)}, bf16[6,768]{1,0:T(8,128)(2,1)S(1)}, u32[]{:S(2)}, u32[]{:S(2)}) collective-permute-start(bf16[6,768]{1,0:T(8,128)(2,1)S(1)} %slice.296), channel_id=1, source_target_pairs={{0,1},{2,3},{4,5},{6,7},{8,9},{10,11},{12,13},{14,15},{16,17},{18,... | collective-permute-start | bytes 27656
  481.6 43.5 %copy-start.3 = (f32[12,208,208]{2,1,0:T(8,128)S(1)}, f32[12,208,208]{2,1,0:T(8,128)}, u32[]{:S(2)}) copy-start(f32[12,208,208]{2,1,0:T(8,128)} %get-tuple-element.138) | copy-start | bytes 6230020
  529.5 16.6 %copy-start.6 = (f32[624,768]{1,0:T(8,128)S(1)}, f32[624,768]{1,0:T(8,128)}, u32[]{:S(2)}) copy-start(f32[624,768]{1,0:T(8,128)} %get-tuple-element.130) | copy-start | bytes 5750788
  547.4 7.0 copy-start.38
  547.5 8.9 %copy-start.40 = (f32[8,768]{1,0:T(8,128)S(1)}, f32[8,768]{1,0:T(8,128)}, u32[]{:S(2)}) copy-start(f32[8,768]{1,0:T(8,128)} %get-tuple-element.132) | copy-start | bytes 73732
  547.5 8.9 %copy-start.39 = (f32[8,768]{1,0:T(8,128)S(1)}, f32[8,768]{1,0:T(8,128)}, u32[]{:S(2)}) copy-start(f32[8,768]{1,0:T(8,128)} %get-tuple-element.135) | copy-start | bytes 73732
  547.5 8.9 %copy-start.37 = (f32[8,768]{1,0:T(8,128)S(1)}, f32[8,768]{1,0:T(8,128)}, u32[]{:S(2)}) copy-start(f32[8,768]{1,0:T(8,128)} %get-tuple-element.131) | copy-start | bytes 73732
  547.5 8.9 %copy-start.36 = (f32[8,768]{1,0:T(8,128)S(1)}, f32[8,768]{1,0:T(8,128)}, u32[]{:S(2)}) copy-start(f32[8,768]{1,0:T(8,128)} %get-tuple-element.134) | copy-start | bytes 73732
  803.0 15.5 %copy-start.7 = (f32[2,48,3,384]{3,1,2,0:T(8,128)S(1)}, f32[2,48,3,384]{3,1,2,0:T(8,128)}, u32[]{:S(2)}) copy-start(f32[2,48,3,384]{3,1,2,0:T(8,128)} %param.40) | copy-start | bytes 1327108
  803.0 15.5 %copy-start.22 = (f32[2,48,3,384]{3,1,2,0:T(8,128)S(1)}, f32[2,48,3,384]{3,1,2,0:T(8,128)}, u32[]{:S(2)}) copy-start(f32[2,48,3,384]{3,1,2,0:T(8,128)} %param.41) | copy-start | bytes 1327108
  807.1 14.0 %copy-start.1 = (f32[4096,48]{0,1:T(8,128)S(1)}, f32[4096,48]{0,1:T(8,128)}, u32[]{:S(2)}) copy-start(f32[4096,48]{0,1:T(8,128)} %param.37) | copy-start | bytes 2359300
  807.1 14.0 %copy-start.8 = (f32[4096,48]{0,1:T(8,128)S(1)}, f32[4096,48]{0,1:T(8,128)}, u32[]{:S(2)}) copy-start(f32[4096,48]{0,1:T(8,128)} %param.38) | copy-start | bytes 2359300
  818.5 4.5 copy-start.2
  818.5 4.5 copy-start.10
  818.5 4.5 copy-start.11
  818.5 4.5 copy-start.12
  822.9 2.7 copy-start.14
  825.6 3.4 copy-start.18
  825.6 3.4 copy-start.27
  825.6 3.3 copy-start.28
  825.7 3.3 copy-start.30
  825.7 3.3 copy-start.31
  (16 other events, 36.9 us)
Sparse Core Ops, SparseCore 0:
  196.3 29.5 reduce-scatter.3
  547.6 34.1 all-gather.4

commit v2 on v1

--- a/solution.py
+++ b/solution.py
@@ -96,52 +96,51 @@
 
 def attention_loop(seqs, lp, half, body):
     pairs = half // (2 * HD)
-    for t in range(2):
-
-        def step(s, _):
-            rows = pl.ds(pl.multiple_of(s * lp, 16), lp)
-            for hp in range(pairs):
-                body(t, s, rows, hp * 2 * HD, t * 2 * pairs + 2 * hp)
-            return 0
-
-        lax.fori_loop(0, seqs, step, 0)
-
-
-def forward_kernel(
-    seqs, x, w_attn, w_up, w_down, vec, bias, out, y1, qkv, att, r, middle, y2, pre, hid, z
-):
+
+    def step(s, _):
+        rows = pl.ds(pl.multiple_of(s * lp, 16), lp)
+        for hp in range(pairs):
+            body(s, rows, hp * 2 * HD, 2 * hp)
+        return 0
+
+    lax.fori_loop(0, seqs, step, 0)
+
+
+def attn_kernel(seqs, x, w, vec, bias, y1, qkv, att, r, middle, y2):
     rows, d = x.shape
     half = d // 2
     lp = rows // seqs
-    ff = w_up.shape[-1]
-    tile = ff // 3
+    t = pl.program_id(0)
+    mine = pl.ds(pl.multiple_of(t * half, 128), half)
 
     def first_norm(at):
         unit, _ = norm_parts(x[at, :])
         y1[at, :] = (unit * vec[0:1, :] + vec[1:2, :]).astype(BF16)
 
-    row_loop(rows, first_norm)
-    for t in range(2):
-        for w in range(3):
-            mixed = dot_nn(y1[...], w_attn[t, :, w * half : (w + 1) * half])
-            if w != 1:
-                row = 2 if w == 0 else 3
-                mixed = mixed + vec[row : row + 1, t * half : (t + 1) * half]
-            qkv[t, :, w * half : (w + 1) * half] = mixed.astype(BF16)
-
-    def attend(t, s, at, col, head):
-        q = qkv[t, at, pl.ds(col, 2 * HD)]
-        k = qkv[t, at, pl.ds(half + col, 2 * HD)]
-        v = qkv[t, at, pl.ds(2 * half + col, 2 * HD)]
+    pl.when(t == 0)(lambda: row_loop(rows, first_norm))
+    for k in range(3):
+        mixed = dot_nn(y1[...], w[0, :, k * half : (k + 1) * half])
+        if k != 1:
+            row = 2 if k == 0 else 3
+            mixed = mixed + vec[row : row + 1, mine]
+        qkv[0, :, k * half : (k + 1) * half] = mixed.astype(BF16)
+
+    def attend(s, at, col, head):
+        q = qkv[0, at, pl.ds(col, 2 * HD)]
+        k = qkv[0, at, pl.ds(half + col, 2 * HD)]
+        v = qkv[0, at, pl.ds(2 * half + col, 2 * HD)]
         found = []
         for i, part in enumerate(halves(q)):
             scores = dot_nt(part, k) * HD**-0.5 + bias[head + i]
             found.append(dot_nn(softmax_rows(scores).astype(BF16), v))
-        att[t, at, pl.ds(col, 2 * HD)] = jnp.where(lane_low(), found[0], found[1]).astype(BF16)
+        att[0, at, pl.ds(col, 2 * HD)] = jnp.where(lane_low(), found[0], found[1]).astype(BF16)
 
     attention_loop(seqs, lp, half, attend)
-    r[...] = dot_nt(att[0], w_attn[0, :, 3 * half :])
-    r[...] += dot_nt(att[1], w_attn[1, :, 3 * half :])
+    part = dot_nt(att[0], w[0, :, 3 * half :])
+
+    @pl.when(t == 0)
+    def _():
+        r[...] = part
 
     def second_norm(at):
         here = x[at, :] + vec[5:6, :] * (r[at, :] + vec[4:5, :])
@@ -149,87 +148,107 @@
         unit, _ = norm_parts(here)
         y2[at, :] = (unit * vec[6:7, :] + vec[7:8, :]).astype(BF16)
 
-    row_loop(rows, second_norm)
-    per = 2 * ff // d
-    for t in range(2):
-        for j in range(3):
-            cols = slice(j * tile, (j + 1) * tile)
-            a = dot_nn(y2[...], w_up[t, :, cols])
-            off = t * ff + j * tile
-            shift = jnp.concatenate(
-                [
-                    vec[10 + o // d : 11 + o // d, o % d : o % d + half // 3]
-                    for o in range(off, off + tile, half // 3)
-                ],
-                axis=1,
-            )
-            a = a + shift
-            pre[t, :, cols] = a
-            h = (0.5 * a * (1.0 + lax.erf(a * ROOT_HALF))).astype(BF16)
-            hid[t, :, cols] = h
-            part = dot_nt(h, w_down[t, :, cols])
-            if t == 0 and j == 0:
-                z[...] = part
-            else:
-                z[...] += part
+    @pl.when(t == 1)
+    def _():
+        r[...] += part
+        row_loop(rows, second_norm)
+
+
+def feed_kernel(middle, y2, w_up, w_down, shift, vec, pre, hid, z, out):
+    rows = middle.shape[0]
+    i = pl.program_id(0)
+    a = dot_nn(y2[...], w_up[0]) + shift[0]
+    pre[0] = a
+    h = (0.5 * a * (1.0 + lax.erf(a * ROOT_HALF))).astype(BF16)
+    hid[0] = h
+    part = dot_nt(h, w_down[0])
+
+    @pl.when(i == 0)
+    def _():
+        z[...] = part
+
+    @pl.when(i > 0)
+    def _():
+        z[...] += part
 
     def finish(at):
         out[at, :] = middle[at, :] + vec[9:10, :] * (z[at, :] + vec[8:9, :])
 
-    row_loop(rows, finish)
-
-
-def whole():
-    return pl.BlockSpec(memory_space=pltpu.VMEM)
-
-
-def third(shape, k):
-    return pl.BlockSpec((shape[0], shape[1], shape[2] // 3), lambda *_: (0, 0, k))
-
-
-def big_call(kernel, ins, specs, outs, scratch, name, flops):
+    pl.when(i == pl.num_programs(0) - 1)(lambda: row_loop(rows, finish))
+
+
+def full(shape):
+    return pl.BlockSpec(shape, functools.partial(lambda n, *_: (0,) * n, len(shape)))
+
+
+def lead(shape):
+    return pl.BlockSpec((1,) + tuple(shape[1:]), lambda i: (i,) + (0,) * (len(shape) - 1))
+
+
+def heads_of(shape):
+    return pl.BlockSpec((shape[0] // 2,) + tuple(shape[1:]), lambda i: (i, 0, 0))
+
+
+def tiles(rows, cols, first=0):
+    return pl.BlockSpec((1, rows, cols), lambda i: (i // 3, 0, first + i % 3))
+
+
+def call(kernel, steps, ins, in_specs, outs, out_specs, scratch, name, flops):
     return pl.pallas_call(
         kernel,
         out_shape=outs,
-        grid=(1,),
-        in_specs=specs,
-        out_specs=[
-            pl.BlockSpec(o.shape, functools.partial(lambda n, *_: (0,) * n, len(o.shape)))
-            for o in outs
-        ],
+        grid=(steps,),
+        in_specs=in_specs,
+        out_specs=out_specs,
         scratch_shapes=scratch,
         compiler_params=pltpu.CompilerParams(vmem_limit_bytes=60 * 2**20),
-        cost_estimate=pl.CostEstimate(flops=flops, bytes_accessed=4 * 10**7, transcendentals=0),
+        cost_estimate=pl.CostEstimate(flops=flops, bytes_accessed=3 * 10**7, transcendentals=0),
         name=name,
     )(*ins)
 
 
-def full(a):
-    return pl.BlockSpec(a.shape, functools.partial(lambda n, *_: (0,) * n, len(a.shape)))
+def attn_spec(weights):
+    return pl.BlockSpec((1, weights.shape[1], weights.shape[2] // 3), lambda i: (i, 0, 0))
 
 
 def forward_layer(x, weights, vec, bias, seqs):
     rows, d = x.shape
     half, ff = d // 2, weights.shape[2] // 3
+    tile = ff // 3
     s = jax.ShapeDtypeStruct
-    outs = [
-        s((rows, d), F32),
-        s((rows, d), BF16),
-        s((2, rows, 3 * half), BF16),
-        s((2, rows, half), BF16),
-        s((rows, d), F32),
-        s((rows, d), F32),
-        s((rows, d), BF16),
-        s((2, rows, ff), F32),
-        s((2, rows, ff), BF16),
-        s((rows, d), F32),
-    ]
-    specs = [full(x)] + [third(weights.shape, k) for k in range(3)] + [full(vec), full(bias)]
-    ins = [x, weights, weights, weights, vec, bias]
-    found = big_call(
-        functools.partial(forward_kernel, seqs), ins, specs, outs, [], "forward", 10**10
-    )
-    return found[0], (x,) + tuple(found[1:])
+    wide, slim = s((rows, d), F32), s((rows, d), BF16)
+    qkv, att = s((2, rows, 3 * half), BF16), s((2, rows, half), BF16)
+    y1, qkv, att, r, middle, y2 = call(
+        functools.partial(attn_kernel, seqs),
+        2,
+        [x, weights, vec, bias],
+        [full(x.shape), attn_spec(weights), full(vec.shape), heads_of(bias.shape)],
+        [slim, qkv, att, wide, wide, slim],
+        [full(slim.shape), lead(qkv.shape), lead(att.shape)] + [full(wide.shape)] * 3,
+        [],
+        "attn",
+        4 * 10**9,
+    )
+    shift = vec[10:14].reshape(6, 1, tile)
+    pre, hid, z, out = call(
+        feed_kernel,
+        6,
+        [middle, y2, weights, weights, shift, vec],
+        [
+            full(wide.shape),
+            full(wide.shape),
+            tiles(d, tile, 3),
+            tiles(d, tile, 6),
+            lead(shift.shape),
+            full(vec.shape),
+        ],
+        [s((2, rows, ff), F32), s((2, rows, ff), BF16), wide, wide],
+        [tiles(rows, tile), tiles(rows, tile), full(wide.shape), full(wide.shape)],
+        [],
+        "feed",
+        6 * 10**9,
+    )
+    return out, (x, y1, qkv, att, r, middle, y2, pre, hid, z)
 
 
 def norm_back_rows(grad, values, gain):
@@ -250,10 +269,8 @@
 def feed_back_kernel(
     g, z, hid, pre, middle, y2, vec, w_up, w_down, gm, g_up, g_down, sums, upb, dz, dy2
 ):
-    rows, d = g.shape
-    ff = w_up.shape[-1]
-    tile = ff // 3
-    sums[...] = jnp.zeros_like(sums)
+    rows = g.shape[0]
+    i = pl.program_id(0)
 
     def first(at):
         here = g[at, :]
@@ -262,23 +279,28 @@
         sums[0:1, :] += col_sum(scaled)
         sums[1:2, :] += col_sum(here * (z[at, :] + vec[8:9, :]))
 
-    row_loop(rows, first)
-    for t in range(2):
-        for j in range(3):
-            cols = slice(j * tile, (j + 1) * tile)
-            dh = dot_nn(dz[...], w_down[t, :, cols])
-            a = pre[t, :, cols]
-            slope = 0.5 * (1.0 + lax.erf(a * ROOT_HALF))
-            slope = slope + a * (jnp.exp(-0.5 * a * a) * (2 * math.pi) ** -0.5)
-            da = (dh * slope).astype(BF16)
-            upb[t : t + 1, cols] = col_sum(da.astype(F32))
-            g_down[t, :, cols] = dot_tn(dz[...], hid[t, :, cols]).astype(BF16)
-            g_up[t, :, cols] = dot_tn(y2[...], da).astype(BF16)
-            part = dot_nt(da, w_up[t, :, cols])
-            if t == 0 and j == 0:
-                dy2[...] = part
-            else:
-                dy2[...] += part
+    @pl.when(i == 0)
+    def _():
+        sums[...] = jnp.zeros_like(sums)
+        row_loop(rows, first)
+
+    dh = dot_nn(dz[...], w_down[0])
+    a = pre[0]
+    slope = 0.5 * (1.0 + lax.erf(a * ROOT_HALF))
+    slope = slope + a * (jnp.exp(-0.5 * a * a) * (2 * math.pi) ** -0.5)
+    da = (dh * slope).astype(BF16)
+    upb[0] = col_sum(da.astype(F32))
+    g_down[0] = dot_tn(dz[...], hid[0]).astype(BF16)
+    g_up[0] = dot_tn(y2[...], da).astype(BF16)
+    part = dot_nt(da, w_up[0])
+
+    @pl.when(i == 0)
+    def _():
+        dy2[...] = part
+
+    @pl.when(i > 0)
+    def _():
+        dy2[...] += part
 
     def last(at):
         grad = dy2[at, :]
@@ -287,16 +309,17 @@
         sums[2:3, :] += col_sum(grad * unit)
         sums[3:4, :] += col_sum(grad)
 
-    row_loop(rows, last)
+    pl.when(i == pl.num_programs(0) - 1)(lambda: row_loop(rows, last))
 
 
 def attn_back_kernel(
-    seqs, gm, r, x, y1, qkv, att, bias, vec, w_attn, g, g_attn, sums, rel, dr, do, dqkv, dy1
+    seqs, gm, r, x, y1, qkv, att, bias, vec, w, g, g_attn, sums, rel, dr, do, dqkv, dy1
 ):
     rows, d = gm.shape
     half = d // 2
     lp = rows // seqs
-    sums[...] = jnp.zeros_like(sums)
+    t = pl.program_id(0)
+    mine = pl.ds(pl.multiple_of(t * half, 128), half)
 
     def first(at):
         here = gm[at, :]
@@ -305,47 +328,50 @@
         sums[0:1, :] += col_sum(scaled)
         sums[1:2, :] += col_sum(here * (r[at, :] + vec[4:5, :]))
 
-    row_loop(rows, first)
-    for t in range(2):
-        g_attn[t, :, 3 * half :] = dot_tn(dr[...], att[t]).astype(BF16)
-        do[t] = dot_nn(dr[...], w_attn[t, :, 3 * half :]).astype(BF16)
-
-    def attend(t, s, at, col, head):
-        q = qkv[t, at, pl.ds(col, 2 * HD)]
-        k = qkv[t, at, pl.ds(half + col, 2 * HD)]
-        v = qkv[t, at, pl.ds(2 * half + col, 2 * HD)]
-        o = do[t, at, pl.ds(col, 2 * HD)]
+    @pl.when(t == 0)
+    def _():
+        sums[...] = jnp.zeros_like(sums)
+        row_loop(rows, first)
+
+    g_attn[0, :, 3 * half :] = dot_tn(dr[...], att[0]).astype(BF16)
+    do[...] = dot_nn(dr[...], w[0, :, 3 * half :]).astype(BF16)
+
+    def attend(s, at, col, head):
+        q = qkv[0, at, pl.ds(col, 2 * HD)]
+        k = qkv[0, at, pl.ds(half + col, 2 * HD)]
+        v = qkv[0, at, pl.ds(2 * half + col, 2 * HD)]
+        o = do[at, pl.ds(col, 2 * HD)]
         dq, dk, dv = [], [], []
         for i, (q_part, o_part) in enumerate(zip(halves(q), halves(o))):
             p = softmax_rows(dot_nt(q_part, k) * HD**-0.5 + bias[head + i])
             dp = dot_nt(o_part, v)
             ds = (p * (dp - jnp.sum(p * dp, axis=-1, keepdims=True))).astype(BF16)
-            wide = ds.astype(F32)
-            rel[head + i] = jnp.where(s == 0, wide, rel[head + i] + wide)
+            more = ds.astype(F32)
+            rel[head + i] = jnp.where(s == 0, more, rel[head + i] + more)
             dq.append(dot_nn(ds, k))
             dk.append(dot_tn(ds, q))
             dv.append(dot_tn(p.astype(BF16), o))
         low = lane_low()
-        for w, pair in enumerate((dq, dk, dv)):
+        for k, pair in enumerate((dq, dk, dv)):
             value = jnp.where(low, pair[0], pair[1])
-            if w < 2:
+            if k < 2:
                 value = value * HD**-0.5
-            dqkv[t, at, pl.ds(w * half + col, 2 * HD)] = value.astype(BF16)
+            dqkv[at, pl.ds(k * half + col, 2 * HD)] = value.astype(BF16)
 
     attention_loop(seqs, lp, half, attend)
-    for t in range(2):
-        for w in range(3):
-            cols = slice(w * half, (w + 1) * half)
-            part = dqkv[t, :, cols]
-            if w != 1:
-                row = 2 if w == 0 else 3
-                sums[row : row + 1, t * half : (t + 1) * half] = col_sum(part.astype(F32))
-            g_attn[t, :, cols] = dot_tn(y1[...], part).astype(BF16)
-            more = dot_nt(part, w_attn[t, :, cols])
-            if t == 0 and w == 0:
-                dy1[...] = more
-            else:
-                dy1[...] += more
+    total = 0.0
+    for k in range(3):
+        cols = slice(k * half, (k + 1) * half)
+        part = dqkv[:, cols]
+        if k != 1:
+            row = 2 if k == 0 else 3
+            sums[row : row + 1, mine] = col_sum(part.astype(F32))
+        g_attn[0, :, cols] = dot_tn(y1[...], part).astype(BF16)
+        total = total + dot_nt(part, w[0, :, cols])
+
+    @pl.when(t == 0)
+    def _():
+        dy1[...] = total
 
     def last(at):
         grad = dy1[at, :]
@@ -354,35 +380,44 @@
         sums[4:5, :] += col_sum(grad * unit)
         sums[5:6, :] += col_sum(grad)
 
-    row_loop(rows, last)
+    @pl.when(t == 1)
+    def _():
+        dy1[...] += total
+        row_loop(rows, last)
 
 
 def backward_layer(g, saved, weights, vec, bias, seqs):
     x, y1, qkv, att, r, middle, y2, pre, hid, z = saved
     rows, d = x.shape
     half, ff = d // 2, weights.shape[2] // 3
+    tile = ff // 3
     s = jax.ShapeDtypeStruct
     part = s((2, d, ff), BF16)
-    ins = [g, z, hid, pre, middle, y2, vec, weights, weights]
-    gm, g_up, g_down, low_sums, upb = big_call(
+    wide = full((rows, d))
+    gm, g_up, g_down, low_sums, upb = call(
         feed_back_kernel,
-        ins,
-        [full(a) for a in ins[:7]] + [third(weights.shape, 1), third(weights.shape, 2)],
-        [s((rows, d), F32), part, part, s((8, d), F32), s((8, ff), F32)],
+        6,
+        [g, z, hid, pre, middle, y2, vec, weights, weights],
+        [wide, wide, tiles(rows, tile), tiles(rows, tile), wide, wide, full(vec.shape)]
+        + [tiles(d, tile, 3), tiles(d, tile, 6)],
+        [s((rows, d), F32), part, part, s((8, d), F32), s((6, 1, tile), F32)],
+        [wide, tiles(d, tile), tiles(d, tile), full((8, d)), lead((6, 1, tile))],
         [pltpu.VMEM((rows, d), BF16), pltpu.VMEM((rows, d), F32)],
         "feed_back",
         12 * 10**9,
     )
-    ins = [gm, r, x, y1, qkv, att, bias, vec, weights]
-    g, g_attn, top_sums, rel = big_call(
+    g, g_attn, top_sums, rel = call(
         functools.partial(attn_back_kernel, seqs),
-        ins,
-        [full(a) for a in ins[:8]] + [third(weights.shape, 0)],
+        2,
+        [gm, r, x, y1, qkv, att, bias, vec, weights],
+        [wide, wide, wide, wide, lead(qkv.shape), lead(att.shape)]
+        + [heads_of(bias.shape), full(vec.shape), attn_spec(weights)],
         [s((rows, d), F32), part, s((8, d), F32), s(bias.shape, F32)],
+        [wide, lead(part.shape), full((8, d)), heads_of(bias.shape)],
         [
             pltpu.VMEM((rows, d), BF16),
-            pltpu.VMEM((2, rows, half), BF16),
-            pltpu.VMEM((2, rows, 3 * half), BF16),
+            pltpu.VMEM((rows, half), BF16),
+            pltpu.VMEM((rows, 3 * half), BF16),
             pltpu.VMEM((rows, d), F32),
         ],
         "attn_back",
@@ -395,7 +430,7 @@
             top_sums[0:2],
             low_sums[2:4],
             low_sums[0:2],
-            upb[:2].reshape(4, d),
+            upb.reshape(4, d),
         ],
         axis=0,
     )
@@ -426,21 +461,29 @@
 
 
 def expand_kernel(side, strips, ends, out):
+    def head(h, _):
+        expand_head(side, strips, ends, out, h)
+        return 0
+
+    lax.fori_loop(0, out.shape[0], head, 0)
+
+
+def expand_head(side, strips, ends, out, h):
     lp = out.shape[1]
     wide = strips.shape[2]
     tokens = side * side + 1
-    a = strips[0]
+    a = strips[h]
     lane = lax.broadcasted_iota(jnp.int32, (1, lp), 1)
-    row_end, col_end, corner = ends[0, 0:1, 0:1], ends[0, 0:1, 1:2], ends[0, 0:1, 2:3]
+    row_end, col_end, corner = ends[h, 0:1, 0:1], ends[h, 0:1, 1:2], ends[h, 0:1, 2:3]
     top = jnp.where(lane == 0, corner, row_end)
-    out[0, 0:1, :] = jnp.where(lane < tokens, top, BIG)
+    out[h, 0:1, :] = jnp.where(lane < tokens, top, BIG)
     for r in range(side):
         shift = (side - 1 - r) * side - 1
         moved = pltpu.roll(a, (wide - shift) % wide, 1)[:side, :lp]
         moved = jnp.where(lane == 0, col_end, moved)
-        out[0, 1 + r * side : 1 + (r + 1) * side, :] = jnp.where(lane < tokens, moved, BIG)
+        out[h, 1 + r * side : 1 + (r + 1) * side, :] = jnp.where(lane < tokens, moved, BIG)
     tail = jnp.where(lane < tokens, 0.0, BIG)
-    out[0, tokens:, :] = jnp.broadcast_to(tail, (lp - tokens, lp))
+    out[h, tokens:, :] = jnp.broadcast_to(tail, (lp - tokens, lp))
 
 
 def expand_bias(position, side, lp):
@@ -454,18 +497,26 @@
     out = pl.pallas_call(
         functools.partial(expand_kernel, side),
         out_shape=jax.ShapeDtypeStruct((layers * heads, lp, lp), F32),
-        grid=(layers * heads,),
+        grid=(layers * heads // 6,),
         in_specs=[
-            pl.BlockSpec((1, 16, wide), lambda i: (i, 0, 0)),
-            pl.BlockSpec((1, 1, 128), lambda i: (i, 0, 0)),
+            pl.BlockSpec((6, 16, wide), lambda i: (i, 0, 0)),
+            pl.BlockSpec((6, 1, 128), lambda i: (i, 0, 0)),
         ],
-        out_specs=pl.BlockSpec((1, lp, lp), lambda i: (i, 0, 0)),
+        out_specs=pl.BlockSpec((6, lp, lp), lambda i: (i, 0, 0)),
         name="expand",
     )(strips, ends)
     return out.reshape(layers, heads, lp, lp)
 
 
 def fold_kernel(side, grads, strips, ends):
+    def head(h, _):
+        fold_head(side, grads, strips, ends, h)
+        return 0
+
+    lax.fori_loop(0, grads.shape[0], head, 0)
+
+
+def fold_head(side, grads, strips, ends, h):
     lp = grads.shape[1]
     wide = strips.shape[2]
     tokens = side * side + 1
@@ -473,16 +524,16 @@
     total = jnp.zeros((16, wide), F32)
     for r in range(side):
         shift = (side - 1 - r) * side - 1
-        part = jnp.where(lane == 0, 0.0, grads[0, 1 + r * side : 1 + (r + 1) * side, :])
+        part = jnp.where(lane == 0, 0.0, grads[h, 1 + r * side : 1 + (r + 1) * side, :])
         part = jnp.concatenate([part, jnp.zeros((16 - side, lp), F32)], axis=0)
         part = jnp.concatenate([part, jnp.zeros((16, wide - lp), F32)], axis=1)
         total = total + pltpu.roll(part, shift % wide, 1)
-    strips[0] = total
-    corner = grads[0, 0:1, 0:1]
-    row_end = jnp.sum(grads[0, 0:1, :], axis=1, keepdims=True) - corner
-    col_end = jnp.sum(grads[0, 1:tokens, 0:1], axis=0, keepdims=True)
+    strips[h] = total
+    corner = grads[h, 0:1, 0:1]
+    row_end = jnp.sum(grads[h, 0:1, :], axis=1, keepdims=True) - corner
+    col_end = jnp.sum(grads[h, 1:tokens, 0:1], axis=0, keepdims=True)
     out_lane = lax.broadcasted_iota(jnp.int32, (1, 128), 1)
-    ends[0] = jnp.where(
+    ends[h] = jnp.where(
         out_lane == 0, row_end, jnp.where(out_lane == 1, col_end, jnp.where(out_lane == 2, corner, 0.0))
     )
 
@@ -497,11 +548,11 @@
             jax.ShapeDtypeStruct((n, 16, wide), F32),
             jax.ShapeDtypeStruct((n, 1, 128), F32),
         ],
-        grid=(n,),
-        in_specs=[pl.BlockSpec((1, lp, lp), lambda i: (i, 0, 0))],
+        grid=(n // 6,),
+        in_specs=[pl.BlockSpec((6, lp, lp), lambda i: (i, 0, 0))],
         out_specs=[
-            pl.BlockSpec((1, 16, wide), lambda i: (i, 0, 0)),
-            pl.BlockSpec((1, 1, 128), lambda i: (i, 0, 0)),
+            pl.BlockSpec((6, 16, wide), lambda i: (i, 0, 0)),
+            pl.BlockSpec((6, 1, 128), lambda i: (i, 0, 0)),
         ],
         name="fold",
     )(grads.reshape(n, lp, lp))
@@ -1004,26 +1055,31 @@
         pack_layer(in_proj[l], out_proj[l], up_proj[l], down_proj[l]).astype(BF16)
         for l in range(layers)
     ]
-    sources = [
-        shards[0],
-        jnp.full((8, 128), count_here),
-        shards[1],
-        embedding.T.astype(BF16),
-        readout.T.astype(BF16),
-    ]
-    wide = (True, False, True, False, False)
+    sources = [shards[0], jnp.full((8, 128), count_here), embedding.T.astype(BF16)]
+    wide = (True, False, False)
     found = gather_all(sources, wide, 1) if custom else gather_plain(sources, wide)
     mask_total = jnp.sum(found[1][:, 0, 0])
-    weights = [found[0].reshape(2, d, -1), found[2].reshape(2, d, -1)]
-    emb_table = found[3].reshape(d, half_vocab)
-    read_table = found[4].reshape(d, half_vocab)
+    weights = [found[0].reshape(2, d, -1)]
+    emb_table = found[2].reshape(d, half_vocab)
+    weights.append(lax.all_gather(shards[1], ("tensor", "dp")).reshape(2, d, -1))
+    read_table = lax.all_gather(readout.T.astype(BF16), "dp").reshape(d, half_vocab)
+
+    peer_at = 1 - tensor_at
+
+    def swap(value):
+        return lax.ppermute(value, "tensor", [(0, 1), (1, 0)])
+
+    def side_of(value, where):
+        return lax.dynamic_slice_in_dim(value, where * mine, mine, 0)
 
     code_rows = jnp.where(masked, -1, token_codes - vocab_start)
-    code_rows = jnp.pad(code_rows, ((0, 0), (1, lp - tokens)), constant_values=-1).reshape(-1)
-    code_hot = (code_rows[:, None] == jnp.arange(half_vocab)[None, :]).astype(BF16)
-    part = dot_nt(code_hot, emb_table).astype(BF16)
-    summed = lax.psum_scatter(part, "tensor", scatter_dimension=0, tiled=True).astype(F32)
-    my_masked = lax.dynamic_slice_in_dim(masked, tensor_at * mine, mine, 0)
+    code_rows = jnp.pad(code_rows, ((0, 0), (1, lp - tokens)), constant_values=-1)
+    codes = jnp.arange(half_vocab)[None, :]
+    peer_hot = (side_of(code_rows, peer_at).reshape(-1, 1) == codes).astype(BF16)
+    own_hot = (side_of(code_rows, tensor_at).reshape(-1, 1) == codes).astype(BF16)
+    came = swap(dot_nt(peer_hot, emb_table).astype(BF16))
+    summed = dot_nt(own_hot, emb_table).astype(BF16).astype(F32) + came.astype(F32)
+    my_masked = side_of(masked, tensor_at)
     mask_flag = jnp.pad(my_masked.astype(F32), ((0, 0), (1, lp - tokens))).reshape(-1, 1)
     lead_flag = jnp.zeros((mine, lp), F32).at[:, 0].set(1.0).reshape(-1, 1)
     x = summed + lead_flag * vectors[tail] + mask_flag * vectors[tail + 1]
@@ -1034,32 +1090,40 @@
         x, saved = forward_layer(x, weights[l], vectors[14 * l : 14 * l + 14], biases[l], mine)
         kept.append(saved)
 
-    my_slots = lax.dynamic_slice_in_dim(mask_slots, tensor_at * mine, mine, 0)
+    my_slots = side_of(mask_slots, tensor_at)
     pick = (jnp.arange(mine)[:, None] * lp + 1 + my_slots).reshape(-1)
     final_in = x[pick]
     unit, _ = norm_parts(final_in)
     u = (unit * vectors[tail + 2] + vectors[tail + 3]).astype(BF16)
-    u_all = lax.all_gather(u, "tensor", axis=0, tiled=True)
-    logits = dot_nn(u_all, read_table)
-    is_target = jnp.arange(half_vocab)[None, :] == (targets.reshape(-1) - vocab_start)[:, None]
-    peak = jnp.max(logits, axis=1)
-    total = jnp.sum(jnp.exp(logits - peak[:, None]), axis=1)
-    chosen = jnp.sum(jnp.where(is_target, logits, 0.0), axis=1)
-    stats = lax.all_gather(jnp.stack([peak, total, chosen]), "tensor")
-    top = jnp.maximum(stats[0, 0], stats[1, 0])
+    u_peer = swap(u)
+    places = [tensor_at, peer_at]
+    logits, stats, target_hot = [], [], []
+    for rows, where in zip((u, u_peer), places):
+        lg = dot_nn(rows, read_table)
+        hot = codes == (side_of(targets, where).reshape(-1) - vocab_start)[:, None]
+        peak = jnp.max(lg, axis=1)
+        total = jnp.sum(jnp.exp(lg - peak[:, None]), axis=1)
+        chosen = jnp.sum(jnp.where(hot, lg, 0.0), axis=1)
+        logits.append(lg)
+        target_hot.append(hot)
+        stats.append(jnp.stack([peak, total, chosen]))
+    both = jnp.stack(stats)
+    other = swap(both)[::-1]
+    top = jnp.maximum(both[:, 0], other[:, 0])
     log_total = top + jnp.log(
-        stats[0, 1] * jnp.exp(stats[0, 0] - top) + stats[1, 1] * jnp.exp(stats[1, 0] - top)
-    )
-    weight_row = live_slot.reshape(-1).astype(F32)
-    loss_here = jnp.sum((log_total - stats[0, 2] - stats[1, 2]) * weight_row)
-    g_logits = (jnp.exp(logits - log_total[:, None]) - is_target.astype(F32)) * (
-        weight_row / mask_total
-    )[:, None]
-    g_logits = g_logits.astype(BF16)
-    grad_final = lax.psum_scatter(
-        dot_nt(g_logits, read_table).astype(BF16), "tensor", scatter_dimension=0, tiled=True
-    ).astype(F32)
-    grad_read = dot_tn(u_all, g_logits)
+        both[:, 1] * jnp.exp(both[:, 0] - top) + other[:, 1] * jnp.exp(other[:, 0] - top)
+    )
+    weight_row = live_slot.astype(F32)
+    weights_of = [side_of(weight_row, where).reshape(-1) for where in places]
+    losses = log_total - both[:, 2] - other[:, 2]
+    loss_here = jnp.sum(losses * jnp.stack(weights_of))
+    g_logits = [
+        ((jnp.exp(logits[i] - log_total[i][:, None]) - target_hot[i].astype(F32)) * (weights_of[i] / mask_total)[:, None]).astype(BF16)
+        for i in range(2)
+    ]
+    came = swap(dot_nt(g_logits[1], read_table).astype(BF16))
+    grad_read = dot_tn(jnp.concatenate([u, u_peer]), jnp.concatenate(g_logits))
+    grad_final = dot_nt(g_logits[0], read_table).astype(BF16).astype(F32) + came.astype(F32)
     back, g_gain, g_shift = norm_back(grad_final, final_in, vectors[tail + 2])
     g = jnp.zeros_like(x).at[pick].add(back)
 
@@ -1076,8 +1140,10 @@
     g0 = g.astype(BF16)
     grad_lead = jnp.sum(g0.astype(F32) * lead_flag, axis=0)
     grad_mask = jnp.sum(g0.astype(F32) * mask_flag, axis=0)
-    g0_all = lax.all_gather(g0, "tensor", axis=0, tiled=True)
-    grad_emb = dot_tn(g0_all, code_hot)
+    g0_peer = swap(g0)
+    grad_emb = dot_tn(
+        jnp.concatenate([g0, g0_peer]), jnp.concatenate([own_hot, peer_hot])
+    )
     vec_local = jnp.concatenate(
         vec_grads + [jnp.stack([grad_lead, grad_mask, g_gain, g_shift])], axis=0
     )

time: 846 us -> 786 us (0.929)
  Pallas kernels: 632 us -> 586 us
  blocking collectives: 23.9 us -> 0 us
  waiting for transfers between devices: 24.4 us -> 7.24 us
  local copies, waits for them, and re-layouts: 37 us -> 54 us
  matrix products: 53.8 us -> 65.1 us
    pallas_call x1, Pallas kernels: 164 us -> 124 us  [gather_all(): pl.pallas_call(functools.partial(gather_kernel, wide), out_shape=outs, in...]
    all_gather x1 -> x2, waiting for transfers between devices: 24.4 us -> 0.02 us  [the longest x1 0.02 us: local(): lax.all_gather(shards[1], ('tensor', 'dp')).reshape(2, d, -1)]
    pallas_call x1, Pallas kernels: 209 us -> 231 us  [reduce_all(): pl.pallas_call(functools.partial(reduce_kernel, nw, nt), out_shape=outs,...]
    all_gather x2 -> x0, blocking collectives: 14.1 us -> none  [the longest x1 10.8 us: local(): u_all = lax.all_gather(u, 'tensor', axis=0, tiled=True)]
    pallas_call x6 -> x8, Pallas kernels: 231 us -> 217 us  [call(): pl.pallas_call(kernel, out_shape=outs, grid=(steps,), in_specs=in_specs,...]
    dot_general x3 -> x5, matrix products: 23.1 us -> 35.2 us  [dot_nt(): lax.dot_general(a, b, (((1,), (1,)), ((), ())), preferred_element_type=F32)]
    unnamed x1 -> x0, blocking collectives: 9.81 us -> none
  transfers between devices with their start and end apart: 3 -> 7, of which waited for: 1 -> 3; matrix products, arithmetic and copies ran while one was open for 4% -> 10% of each run, Pallas kernels for 2% -> 27%
where the time goes in v2:
time: 786 us; the launch traced here: 779 us
  Pallas kernels  586 us (75%)
  matrix products  65.1 us (8%)
  local copies, waits for them, and re-layouts  54 us (7%)
  other arithmetic  47.2 us (6%)
  between operations  16.6 us (2%)
    pallas_call x1, Pallas kernels, reduce_all(): pl.pallas_call(functools.partial(reduce_kernel, nw, nt), out_shape=outs,...  231 us
    pallas_call x8, Pallas kernels, call(): pl.pallas_call(kernel, out_shape=outs, grid=(steps,), in_specs=in_specs,...  217 us
    pallas_call x1, Pallas kernels, gather_all(): pl.pallas_call(functools.partial(gather_kernel, wide), out_shape=outs, in...  124 us
    dot_general x5, matrix products, dot_nt(): lax.dot_general(a, b, (((1,), (1,)), ((), ())), preferred_element_type=F32)  35.2 us
    dot_general x2, matrix products, dot_tn(): lax.dot_general(a, b, (((0,), (0,)), ((), ())), preferred_element_type=F32)  17.9 us
  transfers between devices with their start and end apart: 7, of which 3 were waited for; matrix products, arithmetic and copies ran while one was open for 10% of the time, Pallas kernels for 27%

profile of v2, /device:TPU:9, one launch (start us, length us, event | category | flops | bytes accessed | tf_op | source)
XLA Modules:
  0.0 778.6 jit_solution(8256729543075423829)
XLA Ops:
  16.6 124.2 %gather.7 = (bf16[2,16,48,4608]{3,2,1,0:T(8,128)(2,1)}, f32[16,8,128]{2,1,0:T(8,128)}, bf16[16,48,4096]{2,1,0:T(8,128)(2,1)}) custom-call(bf16[48,4608]{1,0:T(8,128)(2,1)} %copy-done.27, f32[8,128]{1,0:T(8,128)} %broadcast_in_dim.29.refs_1_, bf16[48,4096]{1,0:T(8,128)(2,1)} %convert_bitcast_fusion.1.refs_2_), custom_call_target="tpu_custom_call" | custom-call | tf_op jit(solution)/shard_map/gather/pallas_call | solution.py:767
  140.8 8.3 %convolution_convert_fusion.1 = bf16[624,768]{1,0:T(8,128)(2,1)} fusion(bf16[768,4096]{1,0:T(8,128)(2,1)} %bitcast.201, s32[624]{0:T(1024)S(1)} %eq.76), kind=kOutput, calls=%fused_computation.30 | convolution fusion | flops 3928903680 | bytes 7252416 | tf_op jit(solution)/shard_map/dot_general | solution.py:35
  152.6 5.5 fusion.45
  161.6 6.1 expand.1
  169.8 5.5 fusion.86
  175.3 3.2 iota_compare_fusion
  178.5 3.3 iota_compare_fusion.1
  181.8 8.8 %multiply_add_fusion.x = f32[624,768]{1,0:T(8,128)} fusion(bf16[624,768]{1,0:T(8,128)(2,1)S(1)} %collective-permute-done, bf16[768,4096]{1,0:T(8,128)(2,1)} %bitcast.202, f32[768]{0:T(1024)S(1)} %get-tuple-element.278, f32[624]{0:T(1024)S(1)} %reshape.405, f32[768]{0:T(1024)S(1)} %get-tuple-element.279, f32[624]{0:T(1024)S(1)} %mul.317, s32[624]{0:T(1024)S(1)} %eq.72), kind=kOutput, calls=%fused_computation.29 | convolution fusion | flops 3932258304 | bytes 9180480 | tf_op jit(solution)/shard_map/dot_general | solution.py:35
  190.7 23.9 %attn.2 = (bf16[624,768]{1,0:T(8,128)(2,1)}, bf16[2,624,1152]{2,1,0:T(8,128)(2,1)}, bf16[2,624,384]{2,1,0:T(8,128)(2,1)}, f32[624,768]{1,0:T(8,128)}, f32[624,768]{1,0:T(8,128)}, /*index=5*/bf16[624,768]{1,0:T(8,128)(2,1)}) custom-call(f32[624,768]{1,0:T(8,128)} %multiply_add_fusion.x, bf16[2,768,4608]{2,1,0:T(8,128)(2,1)} %bitcast.160, ...), custom_call_target="tpu_custom_call" | custom-call | flops 4000000000 | bytes 30000000 | tf_op jit(solution)/shard_map/attn/pallas_call | solution.py:197
  214.6 15.9 %feed.2 = (f32[2,624,1536]{2,1,0:T(8,128)}, bf16[2,624,1536]{2,1,0:T(8,128)(2,1)}, f32[624,768]{1,0:T(8,128)}, f32[624,768]{1,0:T(8,128)}) custom-call(f32[624,768]{1,0:T(8,128)} %get-tuple-element.96.middle, bf16[624,768]{1,0:T(8,128)(2,1)} %get-tuple-element.97.y2, bf16[2,768,4608]{2,1,0:T(8,128)(2,1)} %bitcast.161, bf16[2,768,4608]{2,1,0:T(8,128)(2,1)} %bitcast.162, ...), custom_call_target="tpu_custom_call" | custom-call | flops 6000000000 | bytes 30000000 | tf_op jit(solution)/shard_map/feed/pallas_call | solution.py:197
  230.5 23.6 %attn.3 = (bf16[624,768]{1,0:T(8,128)(2,1)}, bf16[2,624,1152]{2,1,0:T(8,128)(2,1)}, bf16[2,624,384]{2,1,0:T(8,128)(2,1)}, f32[624,768]{1,0:T(8,128)}, f32[624,768]{1,0:T(8,128)}, /*index=5*/bf16[624,768]{1,0:T(8,128)(2,1)}) custom-call(f32[624,768]{1,0:T(8,128)} %get-tuple-element.98.x, bf16[2,768,4608]{2,1,0:T(8,128)(2,1)} %bitcast.154, ...), custom_call_target="tpu_custom_call" | custom-call | flops 4000000000 | bytes 30000000 | tf_op jit(solution)/shard_map/attn/pallas_call | solution.py:197
  254.2 15.9 %feed.3 = (f32[2,624,1536]{2,1,0:T(8,128)}, bf16[2,624,1536]{2,1,0:T(8,128)(2,1)}, f32[624,768]{1,0:T(8,128)}, f32[624,768]{1,0:T(8,128)}) custom-call(f32[624,768]{1,0:T(8,128)} %get-tuple-element.99.middle, bf16[624,768]{1,0:T(8,128)(2,1)} %get-tuple-element.100.y2, bf16[2,768,4608]{2,1,0:T(8,128)(2,1)} %bitcast.155, bf16[2,768,4608]{2,1,0:T(8,128)(2,1)} %bitcast.156, ...), custom_call_target="tpu_custom_call" | custom-call | flops 6000000000 | bytes 30000000 | tf_op jit(solution)/shard_map/feed/pallas_call | solution.py:197
  270.1 2.9 gather_fusion
  273.9 4.7 fusion.96
  279.7 3.5 collective-permute-done.1
  291.6 3.5 multiply_convert_fusion
  295.1 5.5 convolution_convert_fusion.3
  302.0 5.9 convolution_convert_fusion
  308.6 6.2 multiply_reduce_fusion
  314.9 4.3 scatter_custom_fusion.g
  319.2 27.2 %feed_back.2 = (f32[624,768]{1,0:T(8,128)}, bf16[2,768,1536]{2,1,0:T(8,128)(2,1)}, bf16[2,768,1536]{2,1,0:T(8,128)(2,1)}, f32[8,768]{1,0:T(8,128)}, f32[6,1,512]{2,1,0:T(1,128)}) custom-call(f32[624,768]{1,0:T(8,128)} %scatter_custom_fusion.g, f32[624,768]{1,0:T(8,128)} %get-tuple-element.103.z, bf16[2,624,1536]{2,1,0:T(8,128)(2,1)} %get-tuple-element.104.hid, ...), custom_call_target="tpu_custom_call" | custom-call | flops 12000000000 | bytes 30000000 | tf_op jit(solution)/shard_map/feed_back/pallas_call | solution.py:197
  346.4 41.7 %attn_back.2 = (f32[624,768]{1,0:T(8,128)}, bf16[2,768,1536]{2,1,0:T(8,128)(2,1)}, f32[8,768]{1,0:T(8,128)}, f32[12,208,208]{2,1,0:T(8,128)}) custom-call(f32[624,768]{1,0:T(8,128)} %get-tuple-element.106.gm, f32[624,768]{1,0:T(8,128)} %get-tuple-element.107.r, f32[624,768]{1,0:T(8,128)} %get-tuple-element.98.x, bf16[624,768]{1,0:T(8,128)(2,1)} %get-tuple-element.108.y1, ...), custom_call_target="tpu_custom_call" | custom-call | flops 6000000000 | bytes 30000000 | tf_op jit(solution)/shard_map/attn_back/pallas_call | solution.py:197
  388.1 27.3 %feed_back.3 = (f32[624,768]{1,0:T(8,128)}, bf16[2,768,1536]{2,1,0:T(8,128)(2,1)}, bf16[2,768,1536]{2,1,0:T(8,128)(2,1)}, f32[8,768]{1,0:T(8,128)}, f32[6,1,512]{2,1,0:T(1,128)}) custom-call(f32[624,768]{1,0:T(8,128)} %get-tuple-element.111.g, f32[624,768]{1,0:T(8,128)} %get-tuple-element.112.z, bf16[2,624,1536]{2,1,0:T(8,128)(2,1)} %get-tuple-element.113.hid, ...), custom_call_target="tpu_custom_call" | custom-call | flops 12000000000 | bytes 30000000 | tf_op jit(solution)/shard_map/feed_back/pallas_call | solution.py:197
  415.4 41.9 %attn_back.3 = (f32[624,768]{1,0:T(8,128)}, bf16[2,768,1536]{2,1,0:T(8,128)(2,1)}, f32[8,768]{1,0:T(8,128)}, f32[12,208,208]{2,1,0:T(8,128)}) custom-call(f32[624,768]{1,0:T(8,128)} %get-tuple-element.115.gm, f32[624,768]{1,0:T(8,128)} %get-tuple-element.116.r, f32[624,768]{1,0:T(8,128)} %multiply_add_fusion.x, bf16[624,768]{1,0:T(8,128)(2,1)} %get-tuple-element.117.y1, ...), custom_call_target="tpu_custom_call" | custom-call | flops 6000000000 | bytes 30000000 | tf_op jit(solution)/shard_map/attn_back/pallas_call | solution.py:197
  457.3 4.4 pad_maximum_fusion
  461.7 7.2 fold.1
  470.3 6.3 fusion.18
  491.0 5.4 concatenate.66
  501.2 2.2 collective-permute-done.4
  503.3 11.9 %fusion.4 = bf16[768,4096]{1,0:T(8,128)(2,1)} fusion(pred[624,4096]{1,0:T(8,128)(4,1)S(1)} %copy-done.9, pred[624,4096]{1,0:T(8,128)(4,1)} %iota_compare_fusion.1, bf16[624,768]{1,0:T(8,128)(2,1)} %collective-permute-done.4, bf16[624,768]{1,0:T(8,128)(2,1)S(1)} %get-tuple-element.310), kind=kOutput, calls=%fused_computation.8 | convolution fusion | flops 7863828480 | bytes 13320192 | tf_op jit(solution)/shard_map/dot_general | solution.py:39
  515.3 230.8 %reduce.21 = (f32[48,1536]{1,0:T(8,128)}, f32[48,1536]{1,0:T(8,128)}, f32[48,1536]{1,0:T(8,128)}, f32[48,1536]{1,0:T(8,128)}, f32[48,1536]{1,0:T(8,128)}, /*inde...) custom-call(bf16[2,4,2,2,48,1536]{5,4,3,2,1,0:T(8,128)(2,1)} %bitcast.174, ...), custom_call_target="tpu_custom_call" | custom-call | tf_op jit(solution)/shard_map/reduce/pallas_call | solution.py:959
  760.1 2.5 fusion.79
  (235 shorter events, 72.3 us)
Async XLA Ops:
  7.2 5.3 copy-start.4
  7.2 6.2 copy-start.45
  7.2 6.3 copy-start.6
  7.2 7.1 copy-start.41
  7.2 7.3 copy-start.40
  7.3 223.3 %all-gather.4.cloned.1.call-start = ((), (), s32[]{:S(2)}) async-start(), calls=%async_computation | async-start | bytes 14598144 | tf_op jit(solution)/shard_map/all_gather | solution.py:1064
  12.5 261.4 %all-gather.6.cloned.1.call-start = ((), (), s32[]{:S(2)}) async-start(), calls=%async_computation.1 | async-start | bytes 6684672 | tf_op jit(solution)/shard_map/all_gather | solution.py:1065
  140.8 11.1 %copy-start.35 = (f32[2,12,732]{2,0,1:T(2,128)S(1)}, f32[2,12,732]{2,0,1:T(2,128)}, u32[]{:S(2)}) copy-start(f32[2,12,732]{2,0,1:T(2,128)} %param.55) | copy-start | bytes 210820
  149.2 32.7 %collective-permute-start = (bf16[624,768]{1,0:T(8,128)(2,1)}, bf16[624,768]{1,0:T(8,128)(2,1)S(1)}, u32[]{:S(2)}, u32[]{:S(2)}) collective-permute-start(bf16[624,768]{1,0:T(8,128)(2,1)} %convolution_convert_fusion.1), channel_id=1, source_target_pairs={{0,1},{1,0},{2,3},{3,2},{4,5},{5,4},{6,7},{7,6},{8,9},{9,8},{10,11... | collective-permute-start | bytes 2875400 | tf_op jit(solution)/shard_map/ppermute | solution.py:1070
  152.6 7.1 copy-start.24
  273.5 9.7 %collective-permute-start.1 = (bf16[234,768]{1,0:T(8,128)(2,1)S(1)}, bf16[234,768]{1,0:T(8,128)(2,1)S(1)}, u32[]{:S(2)}, u32[]{:S(2)}) collective-permute-start(bf16[234,768]{1,0:T(8,128)(2,1)S(1)} %add_convert_fusion), channel_id=1, source_target_pairs={{0,1},{1,0},{2,3},{3,2},{4,5},{5,4},{6,7},{7,6},{8,9},{9,8},{10,11... | collective-permute-start | bytes 1078280 | tf_op jit(solution)/shard_map/ppermute | solution.py:1070
  273.9 9.4 %copy-start = (bf16[768,4096]{1,0:T(8,128)(2,1)S(1)}, bf16[768,4096]{1,0:T(8,128)(2,1)}, u32[]{:S(2)}) copy-start(bf16[768,4096]{1,0:T(8,128)(2,1)} %all-gather.6.cloned.1.call-done) | copy-start | bytes 18874372
  278.6 6.5 copy-start.1
  288.1 2.5 collective-permute-start.2
  295.1 5.5 copy-start.2
  300.6 8.1 %collective-permute-start.3 = (bf16[234,768]{1,0:T(8,128)(2,1)}, bf16[234,768]{1,0:T(8,128)(2,1)}, u32[]{:S(2)}, u32[]{:S(2)}) collective-permute-start(bf16[234,768]{1,0:T(8,128)(2,1)} %convolution_convert_fusion.3), channel_id=1, source_target_pairs={{0,1},{1,0},{2,3},{3,2},{4,5},{5,4},{6,7},{7,6},{8,9},{9,8},{10,11... | collective-permute-start | bytes 1078280 | tf_op jit(solution)/shard_map/ppermute | solution.py:1070
  415.4 41.9 %copy-start.8 = (f32[12,208,208]{2,1,0:T(8,128)S(1)}, f32[12,208,208]{2,1,0:T(8,128)}, u32[]{:S(2)}) copy-start(f32[12,208,208]{2,1,0:T(8,128)} %get-tuple-element.134) | copy-start | bytes 6230020
  470.3 7.0 copy-start.44
  470.3 10.8 %copy-start.43 = (f32[6,1,512]{2,1,0:T(1,128)S(1)}, f32[6,1,512]{2,1,0:T(1,128)}, u32[]{:S(2)}) copy-start(f32[6,1,512]{2,1,0:T(1,128)} %get-tuple-element.129) | copy-start | bytes 36868
  470.3 10.9 %copy-start.42 = (f32[6,1,512]{2,1,0:T(1,128)S(1)}, f32[6,1,512]{2,1,0:T(1,128)}, u32[]{:S(2)}) copy-start(f32[6,1,512]{2,1,0:T(1,128)} %get-tuple-element.132) | copy-start | bytes 36868
  476.6 26.7 %copy-start.9 = (pred[624,4096]{1,0:T(8,128)(4,1)S(1)}, pred[624,4096]{1,0:T(8,128)(4,1)}, u32[]{:S(2)}) copy-start(pred[624,4096]{1,0:T(8,128)(4,1)} %iota_compare_fusion) | copy-start | bytes 7667716
  483.8 19.6 %collective-permute-start.4 = (bf16[624,768]{1,0:T(8,128)(2,1)S(1)}, bf16[624,768]{1,0:T(8,128)(2,1)}, u32[]{:S(2)}, u32[]{:S(2)}) collective-permute-start(bf16[624,768]{1,0:T(8,128)(2,1)S(1)} %get-tuple-element.310), channel_id=1, source_target_pairs={{0,1},{1,0},{2,3},{3,2},{4,5},{5,4},{6,7},{7,6},{8,9},{9,8},{10,11... | collective-permute-start | bytes 2875400 | tf_op jit(solution)/shard_map/ppermute | solution.py:1070
  746.1 14.0 %copy-start.12 = (f32[2,48,3,384]{3,1,2,0:T(8,128)S(1)}, f32[2,48,3,384]{3,1,2,0:T(8,128)}, u32[]{:S(2)}) copy-start(f32[2,48,3,384]{3,1,2,0:T(8,128)} %param.40) | copy-start | bytes 1327108
  746.1 14.0 %copy-start.28 = (f32[2,48,3,384]{3,1,2,0:T(8,128)S(1)}, f32[2,48,3,384]{3,1,2,0:T(8,128)}, u32[]{:S(2)}) copy-start(f32[2,48,3,384]{3,1,2,0:T(8,128)} %param.41) | copy-start | bytes 1327108
  748.6 14.0 %copy-start.5 = (f32[4096,48]{0,1:T(8,128)S(1)}, f32[4096,48]{0,1:T(8,128)}, u32[]{:S(2)}) copy-start(f32[4096,48]{0,1:T(8,128)} %param.37) | copy-start | bytes 2359300
  748.6 14.0 %copy-start.13 = (f32[4096,48]{0,1:T(8,128)S(1)}, f32[4096,48]{0,1:T(8,128)}, u32[]{:S(2)}) copy-start(f32[4096,48]{0,1:T(8,128)} %param.38) | copy-start | bytes 2359300
  760.0 4.5 copy-start.7
  760.1 4.5 copy-start.15
  760.1 4.5 copy-start.16
  760.1 4.5 copy-start.17
  767.2 3.4 copy-start.23
  767.2 3.3 copy-start.33
  (21 other events, 51.1 us)
Sparse Core Ops, SparseCore 0:
  12.6 149.3 all-gather.3
  164.8 61.1 all-gather.5

commit v3 on v2

--- a/solution.py
+++ b/solution.py
@@ -494,18 +494,23 @@
     strips = add_three(dot_nn(split_three(flat[:, :cells][:, ::-1]), jnp.asarray(hot, BF16)))
     strips = strips.reshape(layers * heads, 16, wide)
     ends = jnp.pad(flat[:, cells:], ((0, 0), (0, 125)))[:, None, :]
-    out = pl.pallas_call(
-        functools.partial(expand_kernel, side),
-        out_shape=jax.ShapeDtypeStruct((layers * heads, lp, lp), F32),
-        grid=(layers * heads // 6,),
-        in_specs=[
-            pl.BlockSpec((6, 16, wide), lambda i: (i, 0, 0)),
-            pl.BlockSpec((6, 1, 128), lambda i: (i, 0, 0)),
-        ],
-        out_specs=pl.BlockSpec((6, lp, lp), lambda i: (i, 0, 0)),
-        name="expand",
-    )(strips, ends)
-    return out.reshape(layers, heads, lp, lp)
+    found = []
+    for l in range(layers):
+        own = slice(l * heads, (l + 1) * heads)
+        found.append(
+            pl.pallas_call(
+                functools.partial(expand_kernel, side),
+                out_shape=jax.ShapeDtypeStruct((heads, lp, lp), F32),
+                grid=(heads // 6,),
+                in_specs=[
+                    pl.BlockSpec((6, 16, wide), lambda i: (i, 0, 0)),
+                    pl.BlockSpec((6, 1, 128), lambda i: (i, 0, 0)),
+                ],
+                out_specs=pl.BlockSpec((6, lp, lp), lambda i: (i, 0, 0)),
+                name="expand",
+            )(strips[own], ends[own])
+        )
+    return found
 
 
 def fold_kernel(side, grads, strips, ends):
@@ -538,27 +543,32 @@
     )
 
 
-def fold_bias(grads, side):
-    layers, heads, lp, _ = grads.shape
+def fold_bias(layers, side):
     hot, wide = strip_constant(side)
-    n = layers * heads
-    strips, ends = pl.pallas_call(
-        functools.partial(fold_kernel, side),
-        out_shape=[
-            jax.ShapeDtypeStruct((n, 16, wide), F32),
-            jax.ShapeDtypeStruct((n, 1, 128), F32),
-        ],
-        grid=(n // 6,),
-        in_specs=[pl.BlockSpec((6, lp, lp), lambda i: (i, 0, 0))],
-        out_specs=[
-            pl.BlockSpec((6, 16, wide), lambda i: (i, 0, 0)),
-            pl.BlockSpec((6, 1, 128), lambda i: (i, 0, 0)),
-        ],
-        name="fold",
-    )(grads.reshape(n, lp, lp))
-    cells = add_three(dot_nt(split_three(strips.reshape(n, 16 * wide)), jnp.asarray(hot, BF16)))
-    flat = jnp.concatenate([cells[:, ::-1], ends[:, 0, :3]], axis=1)
-    return flat.reshape(layers, heads, -1)
+    found = []
+    for grads in layers:
+        n, lp, _ = grads.shape
+        found.append(
+            pl.pallas_call(
+                functools.partial(fold_kernel, side),
+                out_shape=[
+                    jax.ShapeDtypeStruct((n, 16, wide), F32),
+                    jax.ShapeDtypeStruct((n, 1, 128), F32),
+                ],
+                grid=(n // 6,),
+                in_specs=[pl.BlockSpec((6, lp, lp), lambda i: (i, 0, 0))],
+                out_specs=[
+                    pl.BlockSpec((6, 16, wide), lambda i: (i, 0, 0)),
+                    pl.BlockSpec((6, 1, 128), lambda i: (i, 0, 0)),
+                ],
+                name="fold",
+            )(grads)
+        )
+    strips = jnp.concatenate([f[0].reshape(-1, 16 * wide) for f in found], axis=0)
+    ends = jnp.concatenate([f[1][:, 0, :3] for f in found], axis=0)
+    cells = add_three(dot_nt(split_three(strips), jnp.asarray(hot, BF16)))
+    flat = jnp.concatenate([cells[:, ::-1], ends], axis=1)
+    return flat.reshape(len(layers), -1, flat.shape[1])
 
 
 def adamw_update(master, gradient, first_mom, second_mom, step_rate, decay_rate):
@@ -570,6 +580,54 @@
         / (jnp.sqrt(second_mom / (1.0 - beta_two**STEP)) + adam_eps)
     )
     return (master - step_rate * (step_dir + decay_rate * master), first_mom, second_mom)
+
+
+def update_kernel(layers, *refs):
+    grads, refs = refs[: 3 * layers + 2], refs[3 * layers + 2 :]
+    olds, news, copies = refs[:18], refs[18:36], refs[36:]
+
+    def put(item, index, gradient, rate):
+        old = [olds[3 * item + k][index] for k in range(3)]
+        found = adamw_update(old[0], gradient, old[1], old[2], rate, decay_matrix)
+        for k in range(3):
+            news[3 * item + k][index] = found[k]
+        if item >= 2:
+            copies[item - 2][index] = found[0].astype(BF16)
+
+    put(0, slice(None), grads[3 * layers + 1][...], rate_table)
+    put(1, slice(None), grads[3 * layers][...], rate_matrix)
+    for l in range(layers):
+        attn, up, down = grads[3 * l : 3 * l + 3]
+        half = attn.shape[1] // 4
+        for k in range(3):
+            put(2, (l, k), attn[:, k * half : (k + 1) * half], rate_matrix)
+        put(3, l, attn[:, 3 * half :], rate_matrix)
+        put(4, l, up[...], rate_matrix)
+        put(5, l, down[...], rate_matrix)
+
+
+def update_all(grads, olds):
+    layers = (len(grads) - 2) // 3
+    rows = grads[0].shape[0]
+    block = 16 if rows % 16 == 0 else rows
+
+    def spec(a):
+        n = len(a.shape)
+        return pl.BlockSpec(
+            tuple(a.shape[:-2]) + (block, a.shape[-1]), lambda i: (0,) * (n - 2) + (i, 0)
+        )
+
+    outs = [jax.ShapeDtypeStruct(a.shape, F32) for a in olds]
+    outs += [jax.ShapeDtypeStruct(olds[3 * k].shape, BF16) for k in range(2, 6)]
+    return pl.pallas_call(
+        functools.partial(update_kernel, layers),
+        out_shape=outs,
+        grid=(rows // block,),
+        in_specs=[spec(a) for a in list(grads) + list(olds)],
+        out_specs=[spec(a) for a in outs],
+        compiler_params=pltpu.CompilerParams(vmem_limit_bytes=56 * 2**20),
+        name="update",
+    )(*grads, *olds)
 
 
 def pack_layer(in_proj, out_proj, up_proj, down_proj):
@@ -1055,7 +1113,24 @@
         pack_layer(in_proj[l], out_proj[l], up_proj[l], down_proj[l]).astype(BF16)
         for l in range(layers)
     ]
-    sources = [shards[0], jnp.full((8, 128), count_here), embedding.T.astype(BF16)]
+    peer_at = 1 - tensor_at
+
+    def swap(value):
+        return lax.ppermute(value, "tensor", [(0, 1), (1, 0)])
+
+    def side_of(value, where):
+        return lax.dynamic_slice_in_dim(value, where * mine, mine, 0)
+
+    code_rows = jnp.where(masked, -1, token_codes - vocab_start)
+    code_rows = jnp.pad(code_rows, ((0, 0), (1, lp - tokens)), constant_values=-1)
+    codes = jnp.arange(half_vocab)[None, :]
+    peer_hot = (side_of(code_rows, peer_at).reshape(-1, 1) == codes).astype(BF16)
+    own_hot = (side_of(code_rows, tensor_at).reshape(-1, 1) == codes).astype(BF16)
+    biases = expand_bias(position, side, lp)
+    first_shard, biases, peer_hot, own_hot = lax.optimization_barrier(
+        (shards[0], biases, peer_hot, own_hot)
+    )
+    sources = [first_shard, jnp.full((8, 128), count_here), embedding.T.astype(BF16)]
     wide = (True, False, False)
     found = gather_all(sources, wide, 1) if custom else gather_plain(sources, wide)
     mask_total = jnp.sum(found[1][:, 0, 0])
@@ -1064,27 +1139,14 @@
     weights.append(lax.all_gather(shards[1], ("tensor", "dp")).reshape(2, d, -1))
     read_table = lax.all_gather(readout.T.astype(BF16), "dp").reshape(d, half_vocab)
 
-    peer_at = 1 - tensor_at
-
-    def swap(value):
-        return lax.ppermute(value, "tensor", [(0, 1), (1, 0)])
-
-    def side_of(value, where):
-        return lax.dynamic_slice_in_dim(value, where * mine, mine, 0)
-
-    code_rows = jnp.where(masked, -1, token_codes - vocab_start)
-    code_rows = jnp.pad(code_rows, ((0, 0), (1, lp - tokens)), constant_values=-1)
-    codes = jnp.arange(half_vocab)[None, :]
-    peer_hot = (side_of(code_rows, peer_at).reshape(-1, 1) == codes).astype(BF16)
-    own_hot = (side_of(code_rows, tensor_at).reshape(-1, 1) == codes).astype(BF16)
     came = swap(dot_nt(peer_hot, emb_table).astype(BF16))
-    summed = dot_nt(own_hot, emb_table).astype(BF16).astype(F32) + came.astype(F32)
+    own_part = lax.optimization_barrier(dot_nt(own_hot, emb_table).astype(BF16))
+    summed = own_part.astype(F32) + came.astype(F32)
     my_masked = side_of(masked, tensor_at)
     mask_flag = jnp.pad(my_masked.astype(F32), ((0, 0), (1, lp - tokens))).reshape(-1, 1)
     lead_flag = jnp.zeros((mine, lp), F32).at[:, 0].set(1.0).reshape(-1, 1)
     x = summed + lead_flag * vectors[tail] + mask_flag * vectors[tail + 1]
 
-    biases = expand_bias(position, side, lp)
     kept = []
     for l in range(layers):
         x, saved = forward_layer(x, weights[l], vectors[14 * l : 14 * l + 14], biases[l], mine)
@@ -1138,6 +1200,7 @@
         rel_grads[l] = rel
 
     g0 = g.astype(BF16)
+    g0, rel_grads[0], rel_grads[1] = lax.optimization_barrier((g0, rel_grads[0], rel_grads[1]))
     grad_lead = jnp.sum(g0.astype(F32) * lead_flag, axis=0)
     grad_mask = jnp.sum(g0.astype(F32) * mask_flag, axis=0)
     g0_peer = swap(g0)
@@ -1147,7 +1210,7 @@
     vec_local = jnp.concatenate(
         vec_grads + [jnp.stack([grad_lead, grad_mask, g_gain, g_shift])], axis=0
     )
-    small_parts = [vec_local, fold_bias(jnp.stack(rel_grads), side), loss_here / tensor_size]
+    small_parts = [vec_local, fold_bias(rel_grads, side), loss_here / tensor_size]
     flat = jnp.concatenate([p.reshape(-1) for p in small_parts])
     flat = jnp.pad(flat, (0, -flat.size % 1024)).reshape(-1, 128)
     if custom:
@@ -1165,47 +1228,33 @@
             [m.astype(BF16).reshape(lead + m.shape[-1:]) for m in (grad_read, grad_emb)],
             flat,
         )
-    grad_read, grad_emb, flat = reduced[3 * layers :]
+    flat = reduced[-1]
     flat = flat.reshape(-1)
     vec_all = flat[: vectors.size].reshape(vectors.shape)
     rel_all = flat[vectors.size : vectors.size + position.size].reshape(position.shape)
     loss_sum = flat[vectors.size + position.size]
 
-    half = d // 2
-    in_g, out_g, up_g, down_g = [], [], [], []
-    for l in range(layers):
-        attn, up, down = reduced[3 * l : 3 * l + 3]
-        in_g.append(attn[:, : 3 * half].reshape(-1, 3, half))
-        out_g.append(attn[:, 3 * half :])
-        up_g.append(up)
-        down_g.append(down)
-    emb_new = adamw_update(
-        embedding, grad_emb.astype(F32).T, emb_first, emb_second, rate_table, decay_matrix
-    )
-    read_new = adamw_update(
-        readout, grad_read.astype(F32).T, read_first, read_second, rate_matrix, decay_matrix
-    )
-    in_new = adamw_update(in_proj, jnp.stack(in_g), in_first, in_second, rate_matrix, decay_matrix)
-    out_new = adamw_update(
-        out_proj, jnp.stack(out_g), out_first, out_second, rate_matrix, decay_matrix
-    )
-    up_new = adamw_update(up_proj, jnp.stack(up_g), up_first, up_second, rate_matrix, decay_matrix)
-    down_new = adamw_update(
-        down_proj, jnp.stack(down_g), down_first, down_second, rate_matrix, decay_matrix
-    )
+    tables = [a.T for a in (embedding, emb_first, emb_second, readout, read_first, read_second)]
+    ins = [a.transpose(0, 2, 1, 3) for a in (in_proj, in_first, in_second)]
+    others = [
+        out_proj,
+        out_first,
+        out_second,
+        up_proj,
+        up_first,
+        up_second,
+        down_proj,
+        down_first,
+        down_second,
+    ]
+    new = update_all(list(reduced[:-1]), tables + ins + others)
+    tables = tuple(a.T for a in new[:6])
+    ins = tuple(a.transpose(0, 2, 1, 3) for a in new[6:9])
+    copies = (new[18].transpose(0, 2, 1, 3),) + tuple(new[19:])
     vec_new = adamw_update(vectors, vec_all, vec_first, vec_second, rate_vector, 0.0)
     pos_new = adamw_update(position, rel_all, pos_first, pos_second, rate_vector, 0.0)
     return (
-        (loss_sum, mask_total)
-        + emb_new
-        + read_new
-        + in_new
-        + out_new
-        + up_new
-        + down_new
-        + vec_new
-        + pos_new
-        + tuple(n[0].astype(BF16) for n in (in_new, out_new, up_new, down_new))
+        (loss_sum, mask_total) + tables + ins + tuple(new[9:18]) + vec_new + pos_new + copies
     )
 
 

time: 786 us -> 753 us (0.958)
  local copies, waits for them, and re-layouts: 54 us -> 26.7 us
  other arithmetic: 47.2 us -> 35.5 us
    pallas_call x1, Pallas kernels: 231 us -> 220 us  [reduce_all(): pl.pallas_call(functools.partial(reduce_kernel, nw, nt), out_shape=outs,...]
    pallas_call x0 -> x1, Pallas kernels: none -> 10.2 us  [update_all(): pl.pallas_call(functools.partial(update_kernel, layers), out_shape=outs,...]
  transfers between devices with their start and end apart: 7 -> 7, of which waited for: 3 -> 3; matrix products, arithmetic and copies ran while one was open for 10% -> 10% of each run, Pallas kernels for 27% -> 29%
where the time goes in v3:
time: 753 us; the launch traced here: 746 us
  Pallas kernels  587 us (78%)
  matrix products  65.8 us (9%)
  other arithmetic  35.5 us (5%)
  local copies, waits for them, and re-layouts  26.7 us (4%)
  between operations  16.4 us (2%)
  waiting for transfers between devices  12 us (2%)
    pallas_call x1, Pallas kernels, reduce_all(): pl.pallas_call(functools.partial(reduce_kernel, nw, nt), out_shape=outs,...  220 us
    pallas_call x8, Pallas kernels, call(): pl.pallas_call(kernel, out_shape=outs, grid=(steps,), in_specs=in_specs,...  217 us
    pallas_call x1, Pallas kernels, gather_all(): pl.pallas_call(functools.partial(gather_kernel, wide), out_shape=outs, in...  123 us
    dot_general x5, matrix products, dot_nt(): lax.dot_general(a, b, (((1,), (1,)), ((), ())), preferred_element_type=F32)  35.6 us
    dot_general x2, matrix products, dot_tn(): lax.dot_general(a, b, (((0,), (0,)), ((), ())), preferred_element_type=F32)  18.4 us
  transfers between devices with their start and end apart: 7, of which 3 were waited for; matrix products, arithmetic and copies ran while one was open for 10% of the time, Pallas kernels for 29%

profile of v3, /device:TPU:9, one launch (start us, length us, event | category | flops | bytes accessed | tf_op | source)
XLA Modules:
  0.0 746.0 jit_solution(17562028572176998069)
XLA Ops:
  15.8 5.3 fusion.41
  22.8 4.0 expand.2.bias
  26.8 4.0 expand.3.bias
  30.9 8.5 %fusion.4 = (bf16[624,4096]{1,0:T(8,128)(2,1)}, bf16[624,4096]{1,0:T(8,128)(2,1)}) fusion(s32[624]{0:T(1024)S(1)} %eq.72, s32[624]{0:T(1024)S(1)} %eq.76), kind=kLoop, calls=%fused_computation.8 | loop fusion | flops 10223616 | bytes 10228608 | tf_op jit(solution)/shard_map/convert_element_type | solution.py:1127
  42.1 122.8 %gather.7 = (bf16[2,16,48,4608]{3,2,1,0:T(8,128)(2,1)}, f32[16,8,128]{2,1,0:T(8,128)}, bf16[16,48,4096]{2,1,0:T(8,128)(2,1)}) custom-call(bf16[48,4608]{1,0:T(8,128)(2,1)} %copy-done.8, f32[8,128]{1,0:T(8,128)} %broadcast_in_dim.26.refs_1_, bf16[48,4096]{1,0:T(8,128)(2,1)} %bitcast_convert_fusion.1.refs_2_), custom_call_target="tpu_custom_call" | custom-call | tf_op jit(solution)/shard_map/gather/pallas_call | solution.py:825
  164.9 9.6 %convolution_convert_fusion.1 = bf16[624,768]{1,0:T(8,128)(2,1)} fusion(bf16[624,4096]{1,0:T(8,128)(2,1)} %get-tuple-element.129, bf16[768,4096]{1,0:T(8,128)(2,1)} %bitcast.218), kind=kOutput, calls=%fused_computation.31 | convolution fusion | flops 3926347776 | bytes 12361728 | tf_op jit(solution)/shard_map/dot_general | solution.py:35
  176.9 8.6 %convolution_convert_fusion.2 = bf16[624,768]{1,0:T(8,128)(2,1)S(1)} fusion(bf16[624,4096]{1,0:T(8,128)(2,1)} %get-tuple-element.126, bf16[768,4096]{1,0:T(8,128)(2,1)} %bitcast.219), kind=kOutput, calls=%fused_computation.32 | convolution fusion | flops 3926347776 | bytes 12361728 | tf_op jit(solution)/shard_map/dot_general | solution.py:35
  189.4 8.2 %collective-permute-done = bf16[624,768]{1,0:T(8,128)(2,1)S(1)} collective-permute-done((bf16[624,768]{1,0:T(8,128)(2,1)}, bf16[624,768]{1,0:T(8,128)(2,1)S(1)}, u32[]{:S(2)}, u32[]{:S(2)}) %collective-permute-start) | collective-permute-done | bytes 958496 | tf_op jit(solution)/shard_map/ppermute | solution.py:1119
  199.3 23.3 %attn.2 = (bf16[624,768]{1,0:T(8,128)(2,1)}, bf16[2,624,1152]{2,1,0:T(8,128)(2,1)}, bf16[2,624,384]{2,1,0:T(8,128)(2,1)}, f32[624,768]{1,0:T(8,128)}, f32[624,768]{1,0:T(8,128)}, /*index=5*/bf16[624,768]{1,0:T(8,128)(2,1)}) custom-call(f32[624,768]{1,0:T(8,128)} %multiply_add_fusion.x, bf16[2,768,4608]{2,1,0:T(8,128)(2,1)} %bitcast.169, ...), custom_call_target="tpu_custom_call" | custom-call | flops 4000000000 | bytes 30000000 | tf_op jit(solution)/shard_map/attn/pallas_call | solution.py:197
  222.7 15.9 %feed.2 = (f32[2,624,1536]{2,1,0:T(8,128)}, bf16[2,624,1536]{2,1,0:T(8,128)(2,1)}, f32[624,768]{1,0:T(8,128)}, f32[624,768]{1,0:T(8,128)}) custom-call(f32[624,768]{1,0:T(8,128)} %get-tuple-element.132.middle, bf16[624,768]{1,0:T(8,128)(2,1)} %get-tuple-element.133.y2, bf16[2,768,4608]{2,1,0:T(8,128)(2,1)} %bitcast.170, bf16[2,768,4608]{2,1,0:T(8,128)(2,1)} %bitcast.171, ...), custom_call_target="tpu_custom_call" | custom-call | flops 6000000000 | bytes 30000000 | tf_op jit(solution)/shard_map/feed/pallas_call | solution.py:197
  238.5 23.4 %attn.3 = (bf16[624,768]{1,0:T(8,128)(2,1)}, bf16[2,624,1152]{2,1,0:T(8,128)(2,1)}, bf16[2,624,384]{2,1,0:T(8,128)(2,1)}, f32[624,768]{1,0:T(8,128)}, f32[624,768]{1,0:T(8,128)}, /*index=5*/bf16[624,768]{1,0:T(8,128)(2,1)}) custom-call(f32[624,768]{1,0:T(8,128)} %get-tuple-element.134.x, bf16[2,768,4608]{2,1,0:T(8,128)(2,1)} %bitcast.163, ...), custom_call_target="tpu_custom_call" | custom-call | flops 4000000000 | bytes 30000000 | tf_op jit(solution)/shard_map/attn/pallas_call | solution.py:197
  261.9 16.2 %feed.3 = (f32[2,624,1536]{2,1,0:T(8,128)}, bf16[2,624,1536]{2,1,0:T(8,128)(2,1)}, f32[624,768]{1,0:T(8,128)}, f32[624,768]{1,0:T(8,128)}) custom-call(f32[624,768]{1,0:T(8,128)} %get-tuple-element.136.middle, bf16[624,768]{1,0:T(8,128)(2,1)} %get-tuple-element.137.y2, bf16[2,768,4608]{2,1,0:T(8,128)(2,1)} %bitcast.164, bf16[2,768,4608]{2,1,0:T(8,128)(2,1)} %bitcast.165, ...), custom_call_target="tpu_custom_call" | custom-call | flops 6000000000 | bytes 30000000 | tf_op jit(solution)/shard_map/feed/pallas_call | solution.py:197
  278.2 2.9 gather_fusion
  281.9 4.7 fusion.82
  287.8 3.3 collective-permute-done.1
  291.0 1.8 fusion.81
  292.9 1.9 copy-done.3
  299.5 3.5 multiply_convert_fusion
  303.0 5.5 convolution_convert_fusion.3
  310.6 5.5 convolution_convert_fusion
  316.7 5.7 multiply_reduce_fusion
  322.4 4.4 scatter_custom_fusion.g
  326.8 27.4 %feed_back.2 = (f32[624,768]{1,0:T(8,128)}, bf16[2,768,1536]{2,1,0:T(8,128)(2,1)}, bf16[2,768,1536]{2,1,0:T(8,128)(2,1)}, f32[8,768]{1,0:T(8,128)}, f32[6,1,512]{2,1,0:T(1,128)}) custom-call(f32[624,768]{1,0:T(8,128)} %scatter_custom_fusion.g, f32[624,768]{1,0:T(8,128)} %get-tuple-element.140.z, bf16[2,624,1536]{2,1,0:T(8,128)(2,1)} %get-tuple-element.141.hid, ...), custom_call_target="tpu_custom_call" | custom-call | flops 12000000000 | bytes 30000000 | tf_op jit(solution)/shard_map/feed_back/pallas_call | solution.py:197
  354.2 41.7 %attn_back.2 = (f32[624,768]{1,0:T(8,128)}, bf16[2,768,1536]{2,1,0:T(8,128)(2,1)}, f32[8,768]{1,0:T(8,128)}, f32[12,208,208]{2,1,0:T(8,128)}) custom-call(f32[624,768]{1,0:T(8,128)} %get-tuple-element.143.gm, f32[624,768]{1,0:T(8,128)} %get-tuple-element.144.r, f32[624,768]{1,0:T(8,128)} %get-tuple-element.134.x, bf16[624,768]{1,0:T(8,128)(2,1)} %get-tuple-element.145.y1, ...), custom_call_target="tpu_custom_call" | custom-call | flops 6000000000 | bytes 30000000 | tf_op jit(solution)/shard_map/attn_back/pallas_call | solution.py:197
  395.9 27.6 %feed_back.3 = (f32[624,768]{1,0:T(8,128)}, bf16[2,768,1536]{2,1,0:T(8,128)(2,1)}, bf16[2,768,1536]{2,1,0:T(8,128)(2,1)}, f32[8,768]{1,0:T(8,128)}, f32[6,1,512]{2,1,0:T(1,128)}) custom-call(f32[624,768]{1,0:T(8,128)} %get-tuple-element.148.g, f32[624,768]{1,0:T(8,128)} %get-tuple-element.149.z, bf16[2,624,1536]{2,1,0:T(8,128)(2,1)} %get-tuple-element.150.hid, ...), custom_call_target="tpu_custom_call" | custom-call | flops 12000000000 | bytes 30000000 | tf_op jit(solution)/shard_map/feed_back/pallas_call | solution.py:197
  423.5 41.7 %attn_back.3 = (f32[624,768]{1,0:T(8,128)}, bf16[2,768,1536]{2,1,0:T(8,128)(2,1)}, f32[8,768]{1,0:T(8,128)}, f32[12,208,208]{2,1,0:T(8,128)}) custom-call(f32[624,768]{1,0:T(8,128)} %get-tuple-element.152.gm, f32[624,768]{1,0:T(8,128)} %get-tuple-element.153.r, f32[624,768]{1,0:T(8,128)} %multiply_add_fusion.x, bf16[624,768]{1,0:T(8,128)(2,1)} %get-tuple-element.154.y1, ...), custom_call_target="tpu_custom_call" | custom-call | flops 6000000000 | bytes 30000000 | tf_op jit(solution)/shard_map/attn_back/pallas_call | solution.py:197
  468.5 4.4 fold.2
  474.9 4.6 fold.3
  481.7 6.3 fusion.20
  489.6 12.9 %fusion.6 = bf16[768,4096]{1,0:T(8,128)(2,1)} fusion(bf16[624,4096]{1,0:T(8,128)(2,1)} %get-tuple-element.129, bf16[624,4096]{1,0:T(8,128)(2,1)} %get-tuple-element.126, bf16[624,768]{1,0:T(8,128)(2,1)S(1)} %collective-permute-done.4, bf16[624,768]{1,0:T(8,128)(2,1)S(1)} %convert_element_type.108), kind=kOutput, calls=%fused_computation.10 | convolution fusion | flops 7879163904 | bytes 18432000 | tf_op jit(solution)/shard_map/dot_general | solution.py:39
  502.6 220.0 %reduce.21 = (f32[48,1536]{1,0:T(8,128)}, f32[48,1536]{1,0:T(8,128)}, f32[48,1536]{1,0:T(8,128)}, f32[48,1536]{1,0:T(8,128)}, f32[48,1536]{1,0:T(8,128)}, /*inde...) custom-call(bf16[2,4,2,2,48,1536]{5,4,3,2,1,0:T(8,128)(2,1)} %bitcast.182, ...), custom_call_target="tpu_custom_call" | custom-call | tf_op jit(solution)/shard_map/reduce/pallas_call | solution.py:1017
  728.7 10.2 %update.1 = (f32[48,4096]{1,0:T(8,128)}, f32[48,4096]{1,0:T(8,128)}, f32[48,4096]{1,0:T(8,128)}, f32[48,4096]{1,0:T(8,128)}, f32[48,4096]{1,0:T(8,128)}, /*index...) custom-call(f32[48,1536]{1,0:T(8,128)} %get-tuple-element.180.refs_0, ...), custom_call_target="tpu_custom_call" | custom-call | tf_op jit(solution)/shard_map/update/pallas_call | solution.py:622
  (204 shorter events, 44.0 us)
Async XLA Ops:
  7.2 5.3 copy-start.5
  7.2 6.1 copy-start.29
  7.2 6.2 copy-start.16
  7.2 6.4 copy-start.15
  7.2 6.7 copy-start.9
  7.3 231.3 %all-gather.4.cloned.1.call-start = ((), (), s32[]{:S(2)}) async-start(), calls=%async_computation | async-start | bytes 14598144 | tf_op jit(solution)/shard_map/all_gather | solution.py:1139
  12.5 269.4 %all-gather.6.cloned.1.call-start = ((), (), s32[]{:S(2)}) async-start(), calls=%async_computation.1 | async-start | bytes 6684672 | tf_op jit(solution)/shard_map/all_gather | solution.py:1140
  30.9 8.5 %copy-start.8 = (bf16[48,4608]{1,0:T(8,128)(2,1)}, bf16[48,4608]{1,0:T(8,128)(2,1)S(1)}, u32[]{:S(2)}) copy-start(bf16[48,4608]{1,0:T(8,128)(2,1)S(1)} %fusion.37.refs_0_) | copy-start | bytes 1327108
  30.9 9.1 %copy-start.4 = (f32[4096,48]{0,1:T(8,128)S(1)}, f32[4096,48]{0,1:T(8,128)}, u32[]{:S(2)}) copy-start(f32[4096,48]{0,1:T(8,128)} %param.34) | copy-start | bytes 2359300
  174.5 23.1 %collective-permute-start = (bf16[624,768]{1,0:T(8,128)(2,1)}, bf16[624,768]{1,0:T(8,128)(2,1)S(1)}, u32[]{:S(2)}, u32[]{:S(2)}) collective-permute-start(bf16[624,768]{1,0:T(8,128)(2,1)} %convolution_convert_fusion.1), channel_id=1, source_target_pairs={{0,1},{1,0},{2,3},{3,2},{4,5},{5,4},{6,7},{7,6},{8,9},{9,8},{10,11... | collective-permute-start | bytes 2875400 | tf_op jit(solution)/shard_map/ppermute | solution.py:1119
  176.5 110.1 %copy-start.21 = (s32[234]{0:T(256)}, s32[234]{0:T(256)S(1)}, u32[]{:S(2)}) copy-start(s32[234]{0:T(256)S(1)} %sub.139) | copy-start | bytes 2812
  176.9 8.6 %copy-start.6 = (f32[32,768]{1,0:T(8,128)S(1)}, f32[32,768]{1,0:T(8,128)}, u32[]{:S(2)}) copy-start(f32[32,768]{1,0:T(8,128)} %param.52) | copy-start | bytes 294916
  281.4 5.2 copy-start.23
  281.6 9.4 %collective-permute-start.1 = (bf16[234,768]{1,0:T(8,128)(2,1)S(1)}, bf16[234,768]{1,0:T(8,128)(2,1)S(1)}, u32[]{:S(2)}, u32[]{:S(2)}) collective-permute-start(bf16[234,768]{1,0:T(8,128)(2,1)S(1)} %add_convert_fusion), channel_id=1, source_target_pairs={{0,1},{1,0},{2,3},{3,2},{4,5},{5,4},{6,7},{7,6},{8,9},{9,8},{10,11... | collective-permute-start | bytes 1078280 | tf_op jit(solution)/shard_map/ppermute | solution.py:1119
  281.9 9.2 %copy-start = (bf16[768,4096]{1,0:T(8,128)(2,1)S(1)}, bf16[768,4096]{1,0:T(8,128)(2,1)}, u32[]{:S(2)}) copy-start(bf16[768,4096]{1,0:T(8,128)(2,1)} %all-gather.6.cloned.1.call-done) | copy-start | bytes 18874372
  286.6 6.2 copy-start.1
  295.9 2.5 collective-permute-start.2
  303.0 6.1 copy-start.2
  303.0 6.1 copy-start.22
  303.0 6.1 copy-start.27
  308.5 8.2 %collective-permute-start.3 = (bf16[234,768]{1,0:T(8,128)(2,1)}, bf16[234,768]{1,0:T(8,128)(2,1)}, u32[]{:S(2)}, u32[]{:S(2)}) collective-permute-start(bf16[234,768]{1,0:T(8,128)(2,1)} %convolution_convert_fusion.3), channel_id=1, source_target_pairs={{0,1},{1,0},{2,3},{3,2},{4,5},{5,4},{6,7},{7,6},{8,9},{9,8},{10,11... | collective-permute-start | bytes 1078280 | tf_op jit(solution)/shard_map/ppermute | solution.py:1119
  316.7 5.7 copy-start.24
  423.5 44.8 %copy-start.26 = (f32[8,768]{1,0:T(8,128)S(1)}, f32[8,768]{1,0:T(8,128)}, u32[]{:S(2)}) copy-start(f32[8,768]{1,0:T(8,128)} %get-tuple-element.168) | copy-start | bytes 73732
  423.5 44.8 %copy-start.25 = (f32[8,768]{1,0:T(8,128)S(1)}, f32[8,768]{1,0:T(8,128)}, u32[]{:S(2)}) copy-start(f32[8,768]{1,0:T(8,128)} %get-tuple-element.171) | copy-start | bytes 73732
  465.2 3.2 copy-start.18
  465.2 3.2 copy-start.17
  467.3 22.3 %collective-permute-start.4 = (bf16[624,768]{1,0:T(8,128)(2,1)S(1)}, bf16[624,768]{1,0:T(8,128)(2,1)S(1)}, u32[]{:S(2)}, u32[]{:S(2)}) collective-permute-start(bf16[624,768]{1,0:T(8,128)(2,1)S(1)} %convert_element_type.108), channel_id=1, source_target_pairs={{0,1},{1,0},{2,3},{3,2},{4,5},{5,4},{6,7},{7,6},{8,9},{9,8},{10,11... | collective-permute-start | bytes 2875400 | tf_op jit(solution)/shard_map/ppermute | solution.py:1119
  502.5 223.3 %copy-start.10 = (f32[2,12,732]{2,0,1:T(2,128)S(1)}, f32[2,12,732]{2,0,1:T(2,128)}, u32[]{:S(2)}) copy-start(f32[2,12,732]{2,0,1:T(2,128)} %param.55) | copy-start | bytes 210820
  502.5 223.3 %copy-start.13 = (f32[2,12,732]{2,0,1:T(2,128)S(1)}, f32[2,12,732]{2,0,1:T(2,128)}, u32[]{:S(2)}) copy-start(f32[2,12,732]{2,0,1:T(2,128)} %param.56) | copy-start | bytes 210820
  502.5 223.3 %copy-start.14 = (f32[2,12,732]{2,0,1:T(2,128)S(1)}, f32[2,12,732]{2,0,1:T(2,128)}, u32[]{:S(2)}) copy-start(f32[2,12,732]{2,0,1:T(2,128)} %param.57) | copy-start | bytes 210820
  502.5 225.4 %copy-start.11 = (f32[32,768]{1,0:T(8,128)S(1)}, f32[32,768]{1,0:T(8,128)}, u32[]{:S(2)}) copy-start(f32[32,768]{1,0:T(8,128)} %param.53) | copy-start | bytes 294916
  502.5 225.4 %copy-start.12 = (f32[32,768]{1,0:T(8,128)S(1)}, f32[32,768]{1,0:T(8,128)}, u32[]{:S(2)}) copy-start(f32[32,768]{1,0:T(8,128)} %param.54) | copy-start | bytes 294916
  (5 other events, 9.5 us)
Sparse Core Ops, SparseCore 0:
  12.6 141.4 all-gather.3
  156.9 66.2 all-gather.5

commit v4 on v3

--- a/solution.py
+++ b/solution.py
@@ -978,25 +978,25 @@
     n, m = len(wide), len(slim)
     fetch("w", 0)
     fetch("t", 0)
-    for k in range(max(n, m) + 4):
+    for k in range(n + 5):
         if k + 1 < n:
             fetch("w", k + 1)
         if k < n:
             core_sum("w", k)
-        if k + 1 < m:
-            fetch("t", k + 1)
-        if k < m:
-            core_sum("t", k)
+        for i in range(2 * k, min(2 * k + 2, m)):
+            if i + 1 < m:
+                fetch("t", i + 1)
+            core_sum("t", i)
         if k <= len(flips):
             small_step(k)
         if 0 <= k - 1 < n:
             after_x(k - 1)
-        if 0 <= k - 1 < m:
-            after_y("t", k - 1)
+        for i in range(max(2 * k - 2, 0), min(2 * k, m)):
+            after_y("t", i)
         if 0 <= k - 2 < n:
             after_y("w", k - 2)
-        if 0 <= k - 2 < m:
-            after_z("t", k - 2)
+        for i in range(max(2 * k - 4, 0), max(min(2 * k - 2, m), 0)):
+            after_z("t", i)
         if 0 <= k - 3 < n:
             after_z("w", k - 3)
     small_out[...] = tot[len(flips)]

time: 753 us -> 746 us (level)
  Pallas kernels: 587 us -> 579 us
    pallas_call x1, Pallas kernels: 220 us -> 212 us  [reduce_all(): pl.pallas_call(functools.partial(reduce_kernel, nw, nt), out_shape=outs,...]
  transfers between devices with their start and end apart: 7 -> 7, of which waited for: 3 -> 3; matrix products, arithmetic and copies ran while one was open for 10% -> 10% of each run, Pallas kernels for 29% -> 30%
where the time goes in v4:
time: 746 us; the launch traced here: 738 us
  Pallas kernels  579 us (78%)
  matrix products  65.8 us (9%)
  other arithmetic  35.5 us (5%)
  local copies, waits for them, and re-layouts  26.7 us (4%)
  between operations  16.4 us (2%)
  waiting for transfers between devices  12 us (2%)
    pallas_call x8, Pallas kernels, call(): pl.pallas_call(kernel, out_shape=outs, grid=(steps,), in_specs=in_specs,...  217 us
    pallas_call x1, Pallas kernels, reduce_all(): pl.pallas_call(functools.partial(reduce_kernel, nw, nt), out_shape=outs,...  212 us
    pallas_call x1, Pallas kernels, gather_all(): pl.pallas_call(functools.partial(gather_kernel, wide), out_shape=outs, in...  123 us
    dot_general x5, matrix products, dot_nt(): lax.dot_general(a, b, (((1,), (1,)), ((), ())), preferred_element_type=F32)  35.6 us
    dot_general x2, matrix products, dot_tn(): lax.dot_general(a, b, (((0,), (0,)), ((), ())), preferred_element_type=F32)  18.4 us
  transfers between devices with their start and end apart: 7, of which 3 were waited for; matrix products, arithmetic and copies ran while one was open for 10% of the time, Pallas kernels for 30%

profile of v4, /device:TPU:9, one launch (start us, length us, event | category | flops | bytes accessed | tf_op | source)
XLA Modules:
  0.0 738.1 jit_solution(9077128764912800454)
XLA Ops:
  15.8 5.3 fusion.41
  22.8 4.0 expand.2.bias
  26.8 4.0 expand.3.bias
  30.9 8.5 %fusion.4 = (bf16[624,4096]{1,0:T(8,128)(2,1)}, bf16[624,4096]{1,0:T(8,128)(2,1)}) fusion(s32[624]{0:T(1024)S(1)} %eq.72, s32[624]{0:T(1024)S(1)} %eq.76), kind=kLoop, calls=%fused_computation.8 | loop fusion | flops 10223616 | bytes 10228608 | tf_op jit(solution)/shard_map/convert_element_type | solution.py:1127
  42.1 122.8 %gather.7 = (bf16[2,16,48,4608]{3,2,1,0:T(8,128)(2,1)}, f32[16,8,128]{2,1,0:T(8,128)}, bf16[16,48,4096]{2,1,0:T(8,128)(2,1)}) custom-call(bf16[48,4608]{1,0:T(8,128)(2,1)} %copy-done.8, f32[8,128]{1,0:T(8,128)} %broadcast_in_dim.26.refs_1_, bf16[48,4096]{1,0:T(8,128)(2,1)} %bitcast_convert_fusion.1.refs_2_), custom_call_target="tpu_custom_call" | custom-call | tf_op jit(solution)/shard_map/gather/pallas_call | solution.py:825
  164.9 9.6 %convolution_convert_fusion.1 = bf16[624,768]{1,0:T(8,128)(2,1)} fusion(bf16[624,4096]{1,0:T(8,128)(2,1)} %get-tuple-element.129, bf16[768,4096]{1,0:T(8,128)(2,1)} %bitcast.218), kind=kOutput, calls=%fused_computation.31 | convolution fusion | flops 3926347776 | bytes 12361728 | tf_op jit(solution)/shard_map/dot_general | solution.py:35
  176.9 8.6 %convolution_convert_fusion.2 = bf16[624,768]{1,0:T(8,128)(2,1)S(1)} fusion(bf16[624,4096]{1,0:T(8,128)(2,1)} %get-tuple-element.126, bf16[768,4096]{1,0:T(8,128)(2,1)} %bitcast.219), kind=kOutput, calls=%fused_computation.32 | convolution fusion | flops 3926347776 | bytes 12361728 | tf_op jit(solution)/shard_map/dot_general | solution.py:35
  189.4 8.2 %collective-permute-done = bf16[624,768]{1,0:T(8,128)(2,1)S(1)} collective-permute-done((bf16[624,768]{1,0:T(8,128)(2,1)}, bf16[624,768]{1,0:T(8,128)(2,1)S(1)}, u32[]{:S(2)}, u32[]{:S(2)}) %collective-permute-start) | collective-permute-done | bytes 958496 | tf_op jit(solution)/shard_map/ppermute | solution.py:1119
  199.3 23.3 %attn.2 = (bf16[624,768]{1,0:T(8,128)(2,1)}, bf16[2,624,1152]{2,1,0:T(8,128)(2,1)}, bf16[2,624,384]{2,1,0:T(8,128)(2,1)}, f32[624,768]{1,0:T(8,128)}, f32[624,768]{1,0:T(8,128)}, /*index=5*/bf16[624,768]{1,0:T(8,128)(2,1)}) custom-call(f32[624,768]{1,0:T(8,128)} %multiply_add_fusion.x, bf16[2,768,4608]{2,1,0:T(8,128)(2,1)} %bitcast.169, ...), custom_call_target="tpu_custom_call" | custom-call | flops 4000000000 | bytes 30000000 | tf_op jit(solution)/shard_map/attn/pallas_call | solution.py:197
  222.7 15.9 %feed.2 = (f32[2,624,1536]{2,1,0:T(8,128)}, bf16[2,624,1536]{2,1,0:T(8,128)(2,1)}, f32[624,768]{1,0:T(8,128)}, f32[624,768]{1,0:T(8,128)}) custom-call(f32[624,768]{1,0:T(8,128)} %get-tuple-element.132.middle, bf16[624,768]{1,0:T(8,128)(2,1)} %get-tuple-element.133.y2, bf16[2,768,4608]{2,1,0:T(8,128)(2,1)} %bitcast.170, bf16[2,768,4608]{2,1,0:T(8,128)(2,1)} %bitcast.171, ...), custom_call_target="tpu_custom_call" | custom-call | flops 6000000000 | bytes 30000000 | tf_op jit(solution)/shard_map/feed/pallas_call | solution.py:197
  238.5 23.4 %attn.3 = (bf16[624,768]{1,0:T(8,128)(2,1)}, bf16[2,624,1152]{2,1,0:T(8,128)(2,1)}, bf16[2,624,384]{2,1,0:T(8,128)(2,1)}, f32[624,768]{1,0:T(8,128)}, f32[624,768]{1,0:T(8,128)}, /*index=5*/bf16[624,768]{1,0:T(8,128)(2,1)}) custom-call(f32[624,768]{1,0:T(8,128)} %get-tuple-element.134.x, bf16[2,768,4608]{2,1,0:T(8,128)(2,1)} %bitcast.163, ...), custom_call_target="tpu_custom_call" | custom-call | flops 4000000000 | bytes 30000000 | tf_op jit(solution)/shard_map/attn/pallas_call | solution.py:197
  261.9 16.2 %feed.3 = (f32[2,624,1536]{2,1,0:T(8,128)}, bf16[2,624,1536]{2,1,0:T(8,128)(2,1)}, f32[624,768]{1,0:T(8,128)}, f32[624,768]{1,0:T(8,128)}) custom-call(f32[624,768]{1,0:T(8,128)} %get-tuple-element.136.middle, bf16[624,768]{1,0:T(8,128)(2,1)} %get-tuple-element.137.y2, bf16[2,768,4608]{2,1,0:T(8,128)(2,1)} %bitcast.164, bf16[2,768,4608]{2,1,0:T(8,128)(2,1)} %bitcast.165, ...), custom_call_target="tpu_custom_call" | custom-call | flops 6000000000 | bytes 30000000 | tf_op jit(solution)/shard_map/feed/pallas_call | solution.py:197
  278.2 2.9 gather_fusion
  281.9 4.7 fusion.82
  287.8 3.3 collective-permute-done.1
  291.0 1.8 fusion.81
  292.9 1.9 copy-done.3
  299.5 3.5 multiply_convert_fusion
  303.0 5.5 convolution_convert_fusion.3
  310.6 5.5 convolution_convert_fusion
  316.7 5.7 multiply_reduce_fusion
  322.4 4.4 scatter_custom_fusion.g
  326.8 27.4 %feed_back.2 = (f32[624,768]{1,0:T(8,128)}, bf16[2,768,1536]{2,1,0:T(8,128)(2,1)}, bf16[2,768,1536]{2,1,0:T(8,128)(2,1)}, f32[8,768]{1,0:T(8,128)}, f32[6,1,512]{2,1,0:T(1,128)}) custom-call(f32[624,768]{1,0:T(8,128)} %scatter_custom_fusion.g, f32[624,768]{1,0:T(8,128)} %get-tuple-element.140.z, bf16[2,624,1536]{2,1,0:T(8,128)(2,1)} %get-tuple-element.141.hid, ...), custom_call_target="tpu_custom_call" | custom-call | flops 12000000000 | bytes 30000000 | tf_op jit(solution)/shard_map/feed_back/pallas_call | solution.py:197
  354.2 41.7 %attn_back.2 = (f32[624,768]{1,0:T(8,128)}, bf16[2,768,1536]{2,1,0:T(8,128)(2,1)}, f32[8,768]{1,0:T(8,128)}, f32[12,208,208]{2,1,0:T(8,128)}) custom-call(f32[624,768]{1,0:T(8,128)} %get-tuple-element.143.gm, f32[624,768]{1,0:T(8,128)} %get-tuple-element.144.r, f32[624,768]{1,0:T(8,128)} %get-tuple-element.134.x, bf16[624,768]{1,0:T(8,128)(2,1)} %get-tuple-element.145.y1, ...), custom_call_target="tpu_custom_call" | custom-call | flops 6000000000 | bytes 30000000 | tf_op jit(solution)/shard_map/attn_back/pallas_call | solution.py:197
  395.9 27.6 %feed_back.3 = (f32[624,768]{1,0:T(8,128)}, bf16[2,768,1536]{2,1,0:T(8,128)(2,1)}, bf16[2,768,1536]{2,1,0:T(8,128)(2,1)}, f32[8,768]{1,0:T(8,128)}, f32[6,1,512]{2,1,0:T(1,128)}) custom-call(f32[624,768]{1,0:T(8,128)} %get-tuple-element.148.g, f32[624,768]{1,0:T(8,128)} %get-tuple-element.149.z, bf16[2,624,1536]{2,1,0:T(8,128)(2,1)} %get-tuple-element.150.hid, ...), custom_call_target="tpu_custom_call" | custom-call | flops 12000000000 | bytes 30000000 | tf_op jit(solution)/shard_map/feed_back/pallas_call | solution.py:197
  423.5 41.7 %attn_back.3 = (f32[624,768]{1,0:T(8,128)}, bf16[2,768,1536]{2,1,0:T(8,128)(2,1)}, f32[8,768]{1,0:T(8,128)}, f32[12,208,208]{2,1,0:T(8,128)}) custom-call(f32[624,768]{1,0:T(8,128)} %get-tuple-element.152.gm, f32[624,768]{1,0:T(8,128)} %get-tuple-element.153.r, f32[624,768]{1,0:T(8,128)} %multiply_add_fusion.x, bf16[624,768]{1,0:T(8,128)(2,1)} %get-tuple-element.154.y1, ...), custom_call_target="tpu_custom_call" | custom-call | flops 6000000000 | bytes 30000000 | tf_op jit(solution)/shard_map/attn_back/pallas_call | solution.py:197
  468.5 4.4 fold.2
  474.9 4.6 fold.3
  481.7 6.3 fusion.20
  489.6 12.9 %fusion.6 = bf16[768,4096]{1,0:T(8,128)(2,1)} fusion(bf16[624,4096]{1,0:T(8,128)(2,1)} %get-tuple-element.129, bf16[624,4096]{1,0:T(8,128)(2,1)} %get-tuple-element.126, bf16[624,768]{1,0:T(8,128)(2,1)S(1)} %collective-permute-done.4, bf16[624,768]{1,0:T(8,128)(2,1)S(1)} %convert_element_type.108), kind=kOutput, calls=%fused_computation.10 | convolution fusion | flops 7879163904 | bytes 18432000 | tf_op jit(solution)/shard_map/dot_general | solution.py:39
  502.6 212.1 %reduce.21 = (f32[48,1536]{1,0:T(8,128)}, f32[48,1536]{1,0:T(8,128)}, f32[48,1536]{1,0:T(8,128)}, f32[48,1536]{1,0:T(8,128)}, f32[48,1536]{1,0:T(8,128)}, /*inde...) custom-call(bf16[2,4,2,2,48,1536]{5,4,3,2,1,0:T(8,128)(2,1)} %bitcast.182, ...), custom_call_target="tpu_custom_call" | custom-call | tf_op jit(solution)/shard_map/reduce/pallas_call | solution.py:1017
  720.8 10.2 %update.1 = (f32[48,4096]{1,0:T(8,128)}, f32[48,4096]{1,0:T(8,128)}, f32[48,4096]{1,0:T(8,128)}, f32[48,4096]{1,0:T(8,128)}, f32[48,4096]{1,0:T(8,128)}, /*index...) custom-call(f32[48,1536]{1,0:T(8,128)} %get-tuple-element.180.refs_0, ...), custom_call_target="tpu_custom_call" | custom-call | tf_op jit(solution)/shard_map/update/pallas_call | solution.py:622
  (204 shorter events, 44.0 us)
Async XLA Ops:
  7.2 5.3 copy-start.5
  7.2 6.1 copy-start.29
  7.2 6.2 copy-start.16
  7.2 6.4 copy-start.15
  7.2 6.7 copy-start.9
  7.3 231.3 %all-gather.4.cloned.1.call-start = ((), (), s32[]{:S(2)}) async-start(), calls=%async_computation | async-start | bytes 14598144 | tf_op jit(solution)/shard_map/all_gather | solution.py:1139
  12.5 269.4 %all-gather.6.cloned.1.call-start = ((), (), s32[]{:S(2)}) async-start(), calls=%async_computation.1 | async-start | bytes 6684672 | tf_op jit(solution)/shard_map/all_gather | solution.py:1140
  30.9 8.5 %copy-start.8 = (bf16[48,4608]{1,0:T(8,128)(2,1)}, bf16[48,4608]{1,0:T(8,128)(2,1)S(1)}, u32[]{:S(2)}) copy-start(bf16[48,4608]{1,0:T(8,128)(2,1)S(1)} %fusion.37.refs_0_) | copy-start | bytes 1327108
  30.9 9.1 %copy-start.4 = (f32[4096,48]{0,1:T(8,128)S(1)}, f32[4096,48]{0,1:T(8,128)}, u32[]{:S(2)}) copy-start(f32[4096,48]{0,1:T(8,128)} %param.34) | copy-start | bytes 2359300
  174.5 23.1 %collective-permute-start = (bf16[624,768]{1,0:T(8,128)(2,1)}, bf16[624,768]{1,0:T(8,128)(2,1)S(1)}, u32[]{:S(2)}, u32[]{:S(2)}) collective-permute-start(bf16[624,768]{1,0:T(8,128)(2,1)} %convolution_convert_fusion.1), channel_id=1, source_target_pairs={{0,1},{1,0},{2,3},{3,2},{4,5},{5,4},{6,7},{7,6},{8,9},{9,8},{10,11... | collective-permute-start | bytes 2875400 | tf_op jit(solution)/shard_map/ppermute | solution.py:1119
  176.5 110.1 %copy-start.21 = (s32[234]{0:T(256)}, s32[234]{0:T(256)S(1)}, u32[]{:S(2)}) copy-start(s32[234]{0:T(256)S(1)} %sub.139) | copy-start | bytes 2812
  176.9 8.6 %copy-start.6 = (f32[32,768]{1,0:T(8,128)S(1)}, f32[32,768]{1,0:T(8,128)}, u32[]{:S(2)}) copy-start(f32[32,768]{1,0:T(8,128)} %param.52) | copy-start | bytes 294916
  281.4 5.2 copy-start.23
  281.6 9.4 %collective-permute-start.1 = (bf16[234,768]{1,0:T(8,128)(2,1)S(1)}, bf16[234,768]{1,0:T(8,128)(2,1)S(1)}, u32[]{:S(2)}, u32[]{:S(2)}) collective-permute-start(bf16[234,768]{1,0:T(8,128)(2,1)S(1)} %add_convert_fusion), channel_id=1, source_target_pairs={{0,1},{1,0},{2,3},{3,2},{4,5},{5,4},{6,7},{7,6},{8,9},{9,8},{10,11... | collective-permute-start | bytes 1078280 | tf_op jit(solution)/shard_map/ppermute | solution.py:1119
  281.9 9.2 %copy-start = (bf16[768,4096]{1,0:T(8,128)(2,1)S(1)}, bf16[768,4096]{1,0:T(8,128)(2,1)}, u32[]{:S(2)}) copy-start(bf16[768,4096]{1,0:T(8,128)(2,1)} %all-gather.6.cloned.1.call-done) | copy-start | bytes 18874372
  286.6 6.2 copy-start.1
  295.9 2.5 collective-permute-start.2
  303.0 6.1 copy-start.2
  303.0 6.1 copy-start.22
  303.0 6.1 copy-start.27
  308.5 8.2 %collective-permute-start.3 = (bf16[234,768]{1,0:T(8,128)(2,1)}, bf16[234,768]{1,0:T(8,128)(2,1)}, u32[]{:S(2)}, u32[]{:S(2)}) collective-permute-start(bf16[234,768]{1,0:T(8,128)(2,1)} %convolution_convert_fusion.3), channel_id=1, source_target_pairs={{0,1},{1,0},{2,3},{3,2},{4,5},{5,4},{6,7},{7,6},{8,9},{9,8},{10,11... | collective-permute-start | bytes 1078280 | tf_op jit(solution)/shard_map/ppermute | solution.py:1119
  316.7 5.7 copy-start.24
  423.5 44.8 %copy-start.26 = (f32[8,768]{1,0:T(8,128)S(1)}, f32[8,768]{1,0:T(8,128)}, u32[]{:S(2)}) copy-start(f32[8,768]{1,0:T(8,128)} %get-tuple-element.168) | copy-start | bytes 73732
  423.5 44.8 %copy-start.25 = (f32[8,768]{1,0:T(8,128)S(1)}, f32[8,768]{1,0:T(8,128)}, u32[]{:S(2)}) copy-start(f32[8,768]{1,0:T(8,128)} %get-tuple-element.171) | copy-start | bytes 73732
  465.2 3.2 copy-start.18
  465.2 3.2 copy-start.17
  467.3 22.3 %collective-permute-start.4 = (bf16[624,768]{1,0:T(8,128)(2,1)S(1)}, bf16[624,768]{1,0:T(8,128)(2,1)S(1)}, u32[]{:S(2)}, u32[]{:S(2)}) collective-permute-start(bf16[624,768]{1,0:T(8,128)(2,1)S(1)} %convert_element_type.108), channel_id=1, source_target_pairs={{0,1},{1,0},{2,3},{3,2},{4,5},{5,4},{6,7},{7,6},{8,9},{9,8},{10,11... | collective-permute-start | bytes 2875400 | tf_op jit(solution)/shard_map/ppermute | solution.py:1119
  502.5 215.3 %copy-start.10 = (f32[2,12,732]{2,0,1:T(2,128)S(1)}, f32[2,12,732]{2,0,1:T(2,128)}, u32[]{:S(2)}) copy-start(f32[2,12,732]{2,0,1:T(2,128)} %param.55) | copy-start | bytes 210820
  502.5 215.4 %copy-start.13 = (f32[2,12,732]{2,0,1:T(2,128)S(1)}, f32[2,12,732]{2,0,1:T(2,128)}, u32[]{:S(2)}) copy-start(f32[2,12,732]{2,0,1:T(2,128)} %param.56) | copy-start | bytes 210820
  502.5 215.4 %copy-start.14 = (f32[2,12,732]{2,0,1:T(2,128)S(1)}, f32[2,12,732]{2,0,1:T(2,128)}, u32[]{:S(2)}) copy-start(f32[2,12,732]{2,0,1:T(2,128)} %param.57) | copy-start | bytes 210820
  502.5 217.5 %copy-start.11 = (f32[32,768]{1,0:T(8,128)S(1)}, f32[32,768]{1,0:T(8,128)}, u32[]{:S(2)}) copy-start(f32[32,768]{1,0:T(8,128)} %param.53) | copy-start | bytes 294916
  502.5 217.5 %copy-start.12 = (f32[32,768]{1,0:T(8,128)S(1)}, f32[32,768]{1,0:T(8,128)}, u32[]{:S(2)}) copy-start(f32[32,768]{1,0:T(8,128)} %param.54) | copy-start | bytes 294916
  (5 other events, 9.5 us)
Sparse Core Ops, SparseCore 0:
  12.6 141.4 all-gather.3
  156.9 66.2 all-gather.5
